TPU v7x, 32 devices: a whole 2x2x4 slice. The times are simulated.
32 devices in a mesh: seq: 8 (over y, x, core), tp: 4 (over z).
Axes of the slice: x: 2, y: 2, z: 4, core: 2. Of those that a mesh axis runs over, the one named last changes fastest.
Arguments:
- hidden_in: bfloat16 [2, 2048, 2048], P(None, ('seq', 'tp')), may hold values from -6 to 6
- output_grad: bfloat16 [2, 2048, 2048], P(None, ('seq', 'tp')), may hold values from -6 to 6
- document_lengths: int32 [2, 4], replicated, may hold values from 1 to 2047, as said below
- attention_gain: float32 [2048], replicated, may hold values from 0.5 to 1.5
- query_weight: bfloat16 [2048, 2048], P(None, 'tp'), may hold values from -0.125 to 0.125
- key_weight: bfloat16 [2048, 1024], P(None, 'tp'), may hold values from -0.125 to 0.125
- value_weight: bfloat16 [2048, 1024], P(None, 'tp'), may hold values from -0.125 to 0.125
- query_gain: float32 [128], replicated, may hold values from 0.5 to 1.5
- key_gain: float32 [128], replicated, may hold values from 0.5 to 1.5
- output_weight: bfloat16 [2048, 2048], P('tp'), may hold values from -0.5 to 0.5
- feedforward_gain: float32 [2048], replicated, may hold values from 0.5 to 1.5
- gate_weight: bfloat16 [2048, 6144], P(None, 'tp'), may hold values from -0.125 to 0.125
- up_weight: bfloat16 [2048, 6144], P(None, 'tp'), may hold values from -0.125 to 0.125
- down_weight: bfloat16 [6144, 2048], P('tp'), may hold values from -0.078125 to 0.078125
Outputs:
- block_out: bfloat16 [2, 2048, 2048], P(None, ('seq', 'tp'))
- input_grad: float32 [2, 2048, 2048], P(None, ('seq', 'tp'))
- attention_gain_grad: float32 [2048], replicated
- query_weight_grad: float32 [2048, 2048], P(None, 'tp')
- key_weight_grad: float32 [2048, 1024], P(None, 'tp')
- value_weight_grad: float32 [2048, 1024], P(None, 'tp')
- query_gain_grad: float32 [128], replicated
- key_gain_grad: float32 [128], replicated
- output_weight_grad: float32 [2048, 2048], P('tp')
- feedforward_gain_grad: float32 [2048], replicated
- gate_weight_grad: float32 [2048, 6144], P(None, 'tp')
- up_weight_grad: float32 [2048, 6144], P(None, 'tp')
- down_weight_grad: float32 [6144, 2048], P('tp')
Inputs may be any that keep to these rules, and one draw needn't show every extreme that they name: `document_lengths`: each row holds four documents, lengths summing to 2048; in one row, drawn from the seed, a document starts within the first 256 positions and ends within the last 256.
All inputs are finite; a program needn't handle non-finite values.
Results may differ from a plain program's by a relative error of at most 0.02.
Values may be sent and summed in bfloat16 or wider, within the bound.
No kernel may reach another device: no remote copies, remote signals or barrier semaphores. Data moves between devices by JAX's collectives and lax.ppermute only.
A program may use at most 192 MiB of HBM per device.

v0:
```python
import jax
import jax.numpy as jnp
from jax import lax
from jax.sharding import PartitionSpec as P

HEAD = 128


epsilon = 1e-06
rope_base = 1000000.0
masked_score = -1e30


def doc_tables(document_lengths, length):
    doc_ends = jnp.cumsum(document_lengths, axis=1)
    doc_starts = doc_ends - document_lengths
    places = jnp.arange(length, dtype=jnp.int32)
    segment = jnp.sum((places[None, :, None] >= doc_ends[:, None, :]).astype(jnp.int32), axis=2)
    numbers = jnp.arange(document_lengths.shape[1], dtype=jnp.int32)
    owned_by = segment[:, :, None] == numbers[None, None, :]
    doc_begin = jnp.sum(jnp.where(owned_by, doc_starts[:, None, :], 0), axis=2)
    return (segment, places[None, :] - doc_begin)


def rope_tables(within, head_size):
    half_size = head_size // 2
    frequency = rope_base ** (-2.0 * jnp.arange(half_size, dtype=jnp.float32) / head_size)
    angles = within.astype(jnp.float32)[..., None] * frequency
    return (jnp.cos(angles)[:, :, None, :], jnp.sin(angles)[:, :, None, :])


def rotate(values, cos_table, sin_table):
    half_size = values.shape[-1] // 2
    front_half = values[..., :half_size]
    back_half = values[..., half_size:]
    return jnp.concatenate(
        [
            front_half * cos_table - back_half * sin_table,
            back_half * cos_table + front_half * sin_table,
        ],
        axis=-1,
    )


def unrotate(upstream, cos_table, sin_table):
    half_size = upstream.shape[-1] // 2
    front_half = upstream[..., :half_size]
    back_half = upstream[..., half_size:]
    return jnp.concatenate(
        [
            front_half * cos_table + back_half * sin_table,
            back_half * cos_table - front_half * sin_table,
        ],
        axis=-1,
    )


def rms_forward(values, gain_vec):
    inverse = lax.rsqrt(jnp.mean(values * values, axis=-1, keepdims=True) + epsilon)
    return (values * inverse * gain_vec, inverse)


def rms_backward(values, inverse, gain_vec, upstream):
    scaled = upstream * gain_vec
    through = inverse * scaled - values * (inverse * inverse * inverse) * jnp.mean(
        values * scaled, axis=-1, keepdims=True
    )
    gain_grad = jnp.sum((upstream * values * inverse).reshape(-1, values.shape[-1]), axis=0)
    return (through, gain_grad)


def project(activations, weight_mat):
    return jnp.einsum("rcd,de->rce", activations, weight_mat, preferred_element_type=jnp.float32)


def project_back(grads_in, weight_mat):
    return jnp.einsum("rce,de->rcd", grads_in, weight_mat, preferred_element_type=jnp.float32)


def weight_grad(activations, grads_in):
    return jnp.einsum("rcd,rce->de", activations, grads_in, preferred_element_type=jnp.float32)


def attend_forward(queries, all_keys, all_values, allowed, scale_by):

    def one_row(row_items):
        query_row, key_row, value_row, mask_row = row_items
        scores = (
            jnp.einsum("qkgd,lkd->kgql", query_row, key_row, preferred_element_type=jnp.float32)
            * scale_by
        )
        scores = jnp.where(mask_row[None, None], scores, masked_score)
        row_top = jnp.max(scores, axis=-1, keepdims=True)
        powers = jnp.exp(scores - row_top)
        totals = jnp.sum(powers, axis=-1, keepdims=True)
        probability = (powers / totals).astype(jnp.bfloat16)
        attended = jnp.einsum(
            "kgql,lkd->qkgd", probability, value_row, preferred_element_type=jnp.float32
        )
        return (attended, (row_top + jnp.log(totals))[..., 0])

    return lax.map(one_row, (queries, all_keys, all_values, allowed))


def attend_backward(queries, all_keys, all_values, attn_grad, log_sums, allowed, scale_by):

    def one_row(row_items):
        query_row, key_row, value_row, grad_row, lse_row, mask_row = row_items
        scores = (
            jnp.einsum("qkgd,lkd->kgql", query_row, key_row, preferred_element_type=jnp.float32)
            * scale_by
        )
        probability = jnp.where(mask_row[None, None], jnp.exp(scores - lse_row[..., None]), 0.0)
        prob_grad = jnp.einsum(
            "qkgd,lkd->kgql", grad_row, value_row, preferred_element_type=jnp.float32
        )
        centre = jnp.sum(probability * prob_grad, axis=-1, keepdims=True)
        score_grad = (probability * (prob_grad - centre)).astype(jnp.bfloat16)
        query_grad = (
            jnp.einsum("kgql,lkd->qkgd", score_grad, key_row, preferred_element_type=jnp.float32)
            * scale_by
        )
        key_grad = (
            jnp.einsum("kgql,qkgd->lkd", score_grad, query_row, preferred_element_type=jnp.float32)
            * scale_by
        )
        value_grad = jnp.einsum(
            "kgql,qkgd->lkd",
            probability.astype(jnp.bfloat16),
            grad_row,
            preferred_element_type=jnp.float32,
        )
        return (query_grad, key_grad, value_grad)

    return lax.map(one_row, (queries, all_keys, all_values, attn_grad, log_sums, allowed))


def body(
    hidden_in,
    output_grad,
    document_lengths,
    attention_gain,
    query_weight,
    key_weight,
    value_weight,
    query_gain,
    key_gain,
    output_weight,
    feedforward_gain,
    gate_weight,
    up_weight,
    down_weight,
):
    tp_count = lax.axis_size("tp")
    seq_count = lax.axis_size("seq")
    row_count, share_rows, model_width = hidden_in.shape
    span_rows = share_rows * tp_count
    row_length = span_rows * seq_count
    key_heads = key_weight.shape[1] // HEAD
    group_size = query_weight.shape[1] // key_weight.shape[1]
    scale_by = HEAD ** (-0.5)
    segment, within = doc_tables(document_lengths, row_length)
    first_place = lax.axis_index("seq") * span_rows
    query_segment = lax.dynamic_slice_in_dim(segment, first_place, span_rows, 1)
    query_within = lax.dynamic_slice_in_dim(within, first_place, span_rows, 1)
    query_places = first_place + jnp.arange(span_rows, dtype=jnp.int32)
    key_places = jnp.arange(row_length, dtype=jnp.int32)
    allowed = (key_places[None, None, :] <= query_places[None, :, None]) & (
        segment[:, None, :] == query_segment[:, :, None]
    )
    cos_table, sin_table = rope_tables(query_within, HEAD)
    hidden_float = hidden_in.astype(jnp.float32)

    def front(hidden_base):
        norm1_share, norm1_inverse = rms_forward(hidden_base, attention_gain)
        normed1 = lax.all_gather(norm1_share.astype(jnp.bfloat16), "tp", axis=1, tiled=True)
        query_raw = project(normed1, query_weight).reshape(
            row_count, span_rows, key_heads * group_size, HEAD
        )
        key_raw = project(normed1, key_weight).reshape(row_count, span_rows, key_heads, HEAD)
        value_local = project(normed1, value_weight).astype(jnp.bfloat16)
        query_normed, query_inverse = rms_forward(query_raw, query_gain)
        key_normed, key_inverse = rms_forward(key_raw, key_gain)
        queries = rotate(query_normed, cos_table, sin_table).astype(jnp.bfloat16)
        queries = queries.reshape(row_count, span_rows, key_heads, group_size, HEAD)
        key_local = (
            rotate(key_normed, cos_table, sin_table)
            .astype(jnp.bfloat16)
            .reshape(row_count, span_rows, key_heads * HEAD)
        )
        all_keys, all_values = (
            lax.all_gather(key_local, "seq", axis=1, tiled=True),
            lax.all_gather(value_local, "seq", axis=1, tiled=True),
        )
        all_keys = all_keys.reshape(row_count, row_length, key_heads, HEAD)
        all_values = all_values.reshape(row_count, row_length, key_heads, HEAD)
        attended, log_sums = attend_forward(queries, all_keys, all_values, allowed, scale_by)
        attn_out = attended.reshape(row_count, span_rows, key_heads * group_size * HEAD).astype(
            jnp.bfloat16
        )
        attn_share = lax.psum_scatter(
            project(attn_out, output_weight), "tp", scatter_dimension=1, tiled=True
        )
        middle = hidden_base + attn_share
        norm2_share, norm2_inverse = rms_forward(middle, feedforward_gain)
        normed2 = lax.all_gather(norm2_share.astype(jnp.bfloat16), "tp", axis=1, tiled=True)
        gate_act = project(normed2, gate_weight)
        up_act = project(normed2, up_weight)
        hidden_mid = (jax.nn.silu(gate_act) * up_act).astype(jnp.bfloat16)
        return (
            norm1_inverse,
            normed1,
            query_raw,
            query_inverse,
            key_raw,
            key_inverse,
            queries,
            all_keys,
            all_values,
            log_sums,
            attn_out,
            middle,
            norm2_inverse,
            normed2,
            gate_act,
            up_act,
            hidden_mid,
        )

    state = front(hidden_float)
    feedforward_share = lax.psum_scatter(
        project(state[16], down_weight).astype(jnp.bfloat16), "tp", scatter_dimension=1, tiled=True
    ).astype(jnp.float32)
    block_out = (state[11] + feedforward_share).astype(jnp.bfloat16)
    hidden_again, block_out = lax.optimization_barrier((hidden_float, block_out))
    state = front(hidden_again)
    (
        norm1_inverse,
        normed1,
        query_raw,
        query_inverse,
        key_raw,
        key_inverse,
        queries,
        all_keys,
        all_values,
        log_sums,
        attn_out,
        middle,
        norm2_inverse,
        normed2,
        gate_act,
        up_act,
        hidden_mid,
    ) = state
    out_rows = lax.all_gather(output_grad, "tp", axis=1, tiled=True)
    mid_grad = jnp.einsum("rcd,fd->rcf", out_rows, down_weight, preferred_element_type=jnp.float32)
    down_grad = weight_grad(hidden_mid, out_rows)
    sigmoid_gate = jax.nn.sigmoid(gate_act)
    gate_grad = (mid_grad * up_act * sigmoid_gate * (1.0 + gate_act * (1.0 - sigmoid_gate))).astype(
        jnp.bfloat16
    )
    up_grad = (mid_grad * gate_act * sigmoid_gate).astype(jnp.bfloat16)
    gate_total = weight_grad(normed2, gate_grad)
    up_total = weight_grad(normed2, up_grad)
    normed2_part = project_back(gate_grad, gate_weight) + project_back(up_grad, up_weight)
    normed2_grad = lax.psum_scatter(normed2_part, "tp", scatter_dimension=1, tiled=True)
    middle_through, feedforward_gain_part = rms_backward(
        middle, norm2_inverse, feedforward_gain, normed2_grad
    )
    middle_grad = output_grad.astype(jnp.float32) + middle_through
    branch_grad = lax.all_gather(middle_grad.astype(jnp.bfloat16), "tp", axis=1, tiled=True)
    output_total = weight_grad(attn_out, branch_grad)
    attn_grad = project_back(branch_grad, output_weight).astype(jnp.bfloat16)
    attn_grad = attn_grad.reshape(row_count, span_rows, key_heads, group_size, HEAD)
    query_rot_grad, key_rot_all, value_grad_all = attend_backward(
        queries, all_keys, all_values, attn_grad, log_sums, allowed, scale_by
    )
    key_rot_grad, value_grad = (
        lax.psum_scatter(
            key_rot_all.reshape(row_count, row_length, key_heads * HEAD).astype(jnp.bfloat16),
            "seq",
            scatter_dimension=1,
            tiled=True,
        ).astype(jnp.float32),
        lax.psum_scatter(
            value_grad_all.reshape(row_count, row_length, key_heads * HEAD).astype(jnp.bfloat16),
            "seq",
            scatter_dimension=1,
            tiled=True,
        ).astype(jnp.float32),
    )
    query_unrot = unrotate(
        query_rot_grad.reshape(row_count, span_rows, key_heads * group_size, HEAD),
        cos_table,
        sin_table,
    )
    query_raw_grad, query_gain_part = rms_backward(
        query_raw, query_inverse, query_gain, query_unrot
    )
    key_unrot = unrotate(
        key_rot_grad.reshape(row_count, span_rows, key_heads, HEAD), cos_table, sin_table
    )
    key_raw_grad, key_gain_part = rms_backward(key_raw, key_inverse, key_gain, key_unrot)
    query_low = query_raw_grad.reshape(row_count, span_rows, key_heads * group_size * HEAD).astype(
        jnp.bfloat16
    )
    key_low = key_raw_grad.reshape(row_count, span_rows, key_heads * HEAD).astype(jnp.bfloat16)
    value_low = value_grad.astype(jnp.bfloat16)
    query_total = weight_grad(normed1, query_low)
    key_total = weight_grad(normed1, key_low)
    value_total = weight_grad(normed1, value_low)
    normed1_part = (
        project_back(query_low, query_weight)
        + project_back(key_low, key_weight)
        + project_back(value_low, value_weight)
    )
    normed1_grad = lax.psum_scatter(
        normed1_part.astype(jnp.bfloat16), "tp", scatter_dimension=1, tiled=True
    ).astype(jnp.float32)
    input_through, attention_gain_part = rms_backward(
        hidden_float, norm1_inverse, attention_gain, normed1_grad
    )
    input_grad = middle_grad + input_through
    attention_gain_grad, query_gain_grad, key_gain_grad, feedforward_gain_grad = lax.psum(
        (attention_gain_part, query_gain_part, key_gain_part, feedforward_gain_part), ("seq", "tp")
    )
    query_total, key_total, value_total, output_total, gate_total, up_total, down_grad = (
        lax.psum(query_total.astype(jnp.bfloat16), "seq").astype(jnp.float32),
        lax.psum(key_total.astype(jnp.bfloat16), "seq").astype(jnp.float32),
        lax.psum(value_total.astype(jnp.bfloat16), "seq").astype(jnp.float32),
        lax.psum(output_total.astype(jnp.bfloat16), "seq").astype(jnp.float32),
        lax.psum(gate_total.astype(jnp.bfloat16), "seq").astype(jnp.float32),
        lax.psum(up_total.astype(jnp.bfloat16), "seq").astype(jnp.float32),
        lax.psum(down_grad.astype(jnp.bfloat16), "seq").astype(jnp.float32),
    )
    return (
        block_out,
        input_grad,
        attention_gain_grad,
        query_total,
        key_total,
        value_total,
        query_gain_grad,
        key_gain_grad,
        output_total,
        feedforward_gain_grad,
        gate_total,
        up_total,
        down_grad,
    )


def solution(mesh):
    in_specs = (
        P(None, ("seq", "tp"), None),
        P(None, ("seq", "tp"), None),
        P(),
        P(),
        P(None, "tp"),
        P(None, "tp"),
        P(None, "tp"),
        P(),
        P(),
        P("tp", None),
        P(),
        P(None, "tp"),
        P(None, "tp"),
        P("tp", None),
    )
    out_specs = (
        P(None, ("seq", "tp"), None),
        P(None, ("seq", "tp"), None),
        P(),
        P(None, "tp"),
        P(None, "tp"),
        P(None, "tp"),
        P(),
        P(),
        P("tp", None),
        P(),
        P(None, "tp"),
        P(None, "tp"),
        P("tp", None),
    )
    return jax.shard_map(body, mesh=mesh, in_specs=in_specs, out_specs=out_specs, check_vma=False)
```

profile of v0, /device:TPU:0, one launch (start us, length us, event | category | flops | bytes accessed | tf_op | source)
XLA Modules:
  0.0 1361.8 jit_solution(9586340191429862947)
XLA Ops:
  10.7 48.7 %all-gather.11.cloned.1.call-done = bf16[2,256,2048]{2,1,0:T(8,128)(2,1)} async-done(((bf16[2,64,2048]{2,1,0:T(8,128)(2,1)}), bf16[2,256,2048]{2,1,0:T(8,128)(2,1)}) %all-gather.11.cloned.1.call-update) | async-done | bytes 2097168 | tf_op jit(solution)/shard_map/all_gather | solution.py:176
  93.5 26.7 %all-gather.15.cloned.1.call-done = bf16[2,2048,256]{1,2,0:T(8,128)(2,1)} async-done(((bf16[2,256,256]{1,2,0:T(8,128)(2,1)}), bf16[2,2048,256]{1,2,0:T(8,128)(2,1)}) %all-gather.15.cloned.1.call-update) | async-done | bytes 2097168 | tf_op jit(solution)/shard_map/all_gather | solution.py:192
  120.2 28.2 %while.39 = (s32[]{:T(128)}, bf16[2,256,2,2,128]{1,4,3,2,0:T(8,128)(2,1)}, bf16[2,2048,2,128]{1,3,2,0:T(8,128)(2,1)}, pred[2,256,2048]{1,2,0:T(8,128)(4,1)S(1)},...) while((s32[]{:T(128)}, bf16[2,256,2,2,128]{1,4,3,2,0:T(8,128)(2,1)}, ...), condition=%wide.region_9.10_spmd.clone, body=%wide.region_6.9_spmd.sunk.clone | while | flops 1090521088 | bytes 50604196 | solution.py:102
  123.0 6.3 fusion.234
  137.1 6.3 fusion.234
  152.9 76.9 %reduce-scatter.8.cloned.1.call-done = f32[2,64,2048]{2,1,0:T(8,128)} async-done(((f32[2,256,2048]{2,1,0:T(8,128)}), f32[2,64,2048]{2,1,0:T(8,128)}) %reduce-scatter.8.cloned.1.call-update) | async-done | bytes 1048592 | tf_op jit(solution)/shard_map/reduce_scatter | solution.py:201
  234.0 46.4 %all-gather.17.cloned.1.call-done = bf16[2,256,2048]{2,1,0:T(8,128)(2,1)} async-done(((bf16[2,64,2048]{2,1,0:T(8,128)(2,1)}), bf16[2,256,2048]{2,1,0:T(8,128)(2,1)}) %all-gather.17.cloned.1.call-update) | async-done | bytes 2097168 | tf_op jit(solution)/shard_map/all_gather | solution.py:206
  280.3 8.5 fusion.82
  288.8 14.1 %fusion.93 = bf16[2,256,2048]{2,1,0:T(8,128)(2,1)} fusion(bf16[1536,2048]{1,0:T(8,128)(2,1)} %param.33, bf16[2,256,2048]{2,1,0:T(8,128)(2,1)} %all-gather.17.cloned.1.call-done, bf16[2048,1536]{1,0:T(8,128)(2,1)} %param.32, f32[2,256,1536]{2,1,0:T(8,128)} %fusion.82), kind=kOutput, calls=%fused_computation.114 | convolution fusion | flops 6448218112 | bytes 19922944 | tf_op jit(solution)/shard_map/rcd,de->rce/dot_general | solution.py:73
  305.2 40.6 %reduce-scatter.10.cloned.1.call-done = bf16[2,64,2048]{2,1,0:T(8,128)(2,1)} async-done(((bf16[2,256,2048]{2,1,0:T(8,128)(2,1)}), bf16[2,64,2048]{2,1,0:T(8,128)(2,1)}) %reduce-scatter.10.cloned.1.call-update) | async-done | bytes 524304 | tf_op jit(solution)/shard_map/reduce_scatter | solution.py:231
  350.6 45.4 %all-gather.19.cloned.1.call-done = bf16[2,256,2048]{2,1,0:T(8,128)(2,1)} async-done(((bf16[2,64,2048]{2,1,0:T(8,128)(2,1)}), bf16[2,256,2048]{2,1,0:T(8,128)(2,1)}) %all-gather.19.cloned.1.call-update) | async-done | bytes 2097168 | tf_op jit(solution)/shard_map/all_gather | solution.py:176
  425.9 8.8 all-gather.23.cloned.1.call-done
  438.7 26.4 %all-gather.21.cloned.1.call-done = bf16[2,2048,256]{2,1,0:T(8,128)(2,1)} async-done(((bf16[2,256,256]{2,1,0:T(8,128)(2,1)}), bf16[2,2048,256]{2,1,0:T(8,128)(2,1)}) %all-gather.21.cloned.1.call-update) | async-done | bytes 2097168 | tf_op jit(solution)/shard_map/all_gather | solution.py:193
  469.1 33.3 %while.40 = (s32[]{:T(128)}, bf16[2,256,2,2,128]{1,4,3,2,0:T(8,128)(2,1)}, f32[2,2,2,256]{3,2,1,0:T(2,128)S(1)}, bf16[2,2048,2,128]{3,2,1,0:T(2,128)(2,1)}, pred...) while((s32[]{:T(128)}, ...), condition=%wide.region_19.20_spmd.clone, body=%wide.region_16.19_spmd.sunk.clone | while | flops 1098906624 | bytes 87327976 | solution.py:102
  478.7 7.0 fusion.239
  495.4 7.0 fusion.239
  507.5 76.1 %reduce-scatter.12.cloned.1.call-done = f32[2,64,2048]{2,1,0:T(8,128)} async-done(((f32[2,256,2048]{2,1,0:T(8,128)}), f32[2,64,2048]{2,1,0:T(8,128)}) %reduce-scatter.12.cloned.1.call-update) | async-done | bytes 1048592 | tf_op jit(solution)/shard_map/reduce_scatter | solution.py:201
  587.7 44.1 %all-gather.25.cloned.1.call-done = bf16[2,256,2048]{2,1,0:T(8,128)(2,1)} async-done(((bf16[2,64,2048]{2,1,0:T(8,128)(2,1)}), bf16[2,256,2048]{2,1,0:T(8,128)(2,1)}) %all-gather.25.cloned.1.call-update) | async-done | bytes 2097168 | tf_op jit(solution)/shard_map/all_gather | solution.py:256
  631.8 8.5 fusion.68
  640.3 38.2 %all-gather.27.cloned.1.call-done = bf16[2,256,2048]{2,1,0:T(8,128)(2,1)} async-done(((bf16[2,64,2048]{2,1,0:T(8,128)(2,1)}), bf16[2,256,2048]{2,1,0:T(8,128)(2,1)}) %all-gather.27.cloned.1.call-update) | async-done | bytes 2097168 | tf_op jit(solution)/shard_map/all_gather | solution.py:206
  684.9 10.0 multiply_convert_fusion.2
  703.5 75.6 %reduce-scatter.14.cloned.1.call-done = f32[2,64,2048]{2,1,0:T(8,128)} async-done(((f32[2,256,2048]{2,1,0:T(8,128)}), f32[2,64,2048]{2,1,0:T(8,128)}) %reduce-scatter.14.cloned.1.call-update) | async-done | bytes 1048592 | tf_op jit(solution)/shard_map/reduce_scatter | solution.py:267
  784.9 46.1 %all-gather.29.cloned.1.call-done = bf16[2,256,2048]{2,1,0:T(8,128)(2,1)} async-done(((bf16[2,64,2048]{2,1,0:T(8,128)(2,1)}), bf16[2,256,2048]{2,1,0:T(8,128)(2,1)}) %all-gather.29.cloned.1.call-update) | async-done | bytes 2097168 | tf_op jit(solution)/shard_map/all_gather | solution.py:272
  835.8 31.7 %while.41 = (s32[]{:T(128)}, f32[2,256,2,2,128]{1,4,3,2,0:T(8,128)}, bf16[2,2048,2,128]{1,3,2,0:T(8,128)(2,1)}, bf16[2,2048,2,128]{1,3,2,0:T(8,128)(2,1)}, bf16[...) while((s32[]{:T(128)}, ...), condition=%wide.region_26.27_spmd.clone, body=%wide.region_24.26_spmd.sunk.clone | while | flops 2716466176 | bytes 142114272 | solution.py:135
  895.8 11.8 reduce-scatter.16.cloned.1.call-done
  917.8 35.1 %reduce-scatter.18.cloned.1.call-done = bf16[2,256,256]{2,1,0:T(8,128)(2,1)} async-done(((bf16[2,2048,256]{2,1,0:T(8,128)(2,1)}), bf16[2,256,256]{2,1,0:T(8,128)(2,1)}) %reduce-scatter.18.cloned.1.call-update) | async-done | bytes 262160 | tf_op jit(solution)/shard_map/reduce_scatter | solution.py:286
  959.9 8.4 bitcast_convert_fusion.2
  997.5 6.3 reduce-scatter.20.cloned.1.call-done
  1005.3 40.8 %all-reduce = (f32[2048]{0:T(1024)}, f32[128]{0:T(128)}, f32[128]{0:T(128)}, f32[2048]{0:T(1024)}) all-reduce(f32[2048]{0:T(1024)S(1)} %get-tuple-element.310, f32[128]{0:T(128)S(1)} %fusion.124, f32[128]{0:T(128)S(1)} %fusion.138, f32[2048]{0:T(1024)S(1)} %copy-done.60), channel_id=1, replica_groups=mesh['seq'=8,'tp'=4] {'seq','tp'}, use_global_device_ids=true, to_apply=%region_34.35 | all-reduce | flops 4352 | bytes 34816 | tf_op jit(solution)/shard_map/psum | solution.py:325
  1048.8 273.6 %all-reduce.4.cloned.1.call-done = (bf16[2048,512]{1,0:T(8,128)(2,1)}, bf16[2048,256]{1,0:T(8,128)(2,1)}, bf16[2048,256]{1,0:T(8,128)(2,1)}, bf16[512,2048]{1,0:...) async-done(((bf16[2048,512]{1,0:T(8,128)(2,1)}, bf16[2048,256]{1,0:T(8,128)(2,1)}, bf16[2048,256]{1,0:T(8,128)(2,1)}, ...) | async-done | bytes 25165840 | tf_op jit(solution)/shard_map/psum | solution.py:329
  1332.3 9.5 convert_element_type.205
  1341.9 6.6 convert_element_type.207
  (439 shorter events, 285.7 us)
Async XLA Ops:
  7.2 141.3 %copy-start = (bf16[512,2048]{1,0:T(8,128)(2,1)S(1)}, bf16[512,2048]{1,0:T(8,128)(2,1)}, u32[]{:S(2)}) copy-start(bf16[512,2048]{1,0:T(8,128)(2,1)} %param.29) | copy-start | bytes 6291460
  7.2 52.3 %all-gather.11.cloned.1.call-start = ((), (), s32[]{:S(2)}) async-start(), calls=%async_computation.7 | async-start | bytes 2621440 | tf_op jit(solution)/shard_map/all_gather | solution.py:176
  7.2 55.6 %copy-start.75 = (s32[2,4]{1,0:T(2,128)S(1)}, s32[2,4]{1,0:T(2,128)}, u32[]{:S(2)}) copy-start(s32[2,4]{1,0:T(2,128)} %param.22) | copy-start | bytes 100
  10.7 78.9 %all-gather.13.cloned.1.call-start = ((), (), s32[]{:S(2)}) async-start(), calls=%async_computation.8 | async-start | bytes 2359296 | tf_op jit(solution)/shard_map/all_gather | solution.py:193
  62.8 57.5 %all-gather.15.cloned.1.call-start = ((), (), s32[]{:S(2)}) async-start(), calls=%async_computation.9 | async-start | bytes 2359296 | tf_op jit(solution)/shard_map/all_gather | solution.py:192
  64.3 359.5 %copy-start.16 = (f32[2,256,64]{2,1,0:T(8,128)}, f32[2,256,64]{2,1,0:T(8,128)S(1)}, u32[]{:S(2)}) copy-start(f32[2,256,64]{2,1,0:T(8,128)S(1)} %get-tuple-element.405) | copy-start | bytes 393220
  70.7 159.0 %reduce-scatter.8.cloned.1.call-start = ((), (), s32[]{:S(2)}) async-start(), calls=%async_computation.10 | async-start | bytes 5242880 | tf_op jit(solution)/shard_map/reduce_scatter | solution.py:201
  152.8 78.5 %copy-start.54 = (f32[2048]{0:T(1024)S(1)}, f32[2048]{0:T(1024)}, u32[]{:S(2)}) copy-start(f32[2048]{0:T(1024)} %param.30) | copy-start | bytes 24580
  152.8 127.5 %all-gather.17.cloned.1.call-start = ((), (), s32[]{:S(2)}) async-start(), calls=%async_computation.11 | async-start | bytes 2621440 | tf_op jit(solution)/shard_map/all_gather | solution.py:206
  233.7 112.0 %reduce-scatter.10.cloned.1.call-start = ((), (), s32[]{:S(2)}) async-start(), calls=%async_computation.12 | async-start | bytes 2621440 | tf_op jit(solution)/shard_map/reduce_scatter | solution.py:231
  303.0 92.9 %all-gather.19.cloned.1.call-start = ((), (), s32[]{:S(2)}) async-start(), calls=%async_computation.13 | async-start | bytes 2621440 | tf_op jit(solution)/shard_map/all_gather | solution.py:176
  350.5 84.2 %all-gather.23.cloned.1.call-start = ((), (), s32[]{:S(2)}) async-start(), calls=%async_computation.15 | async-start | bytes 2359296 | tf_op jit(solution)/shard_map/all_gather | solution.py:192
  407.7 57.5 %all-gather.21.cloned.1.call-start = ((), (), s32[]{:S(2)}) async-start(), calls=%async_computation.14 | async-start | bytes 2359296 | tf_op jit(solution)/shard_map/all_gather | solution.py:193
  411.0 172.7 %reduce-scatter.12.cloned.1.call-start = ((), (), s32[]{:S(2)}) async-start(), calls=%async_computation.16 | async-start | bytes 5242880 | tf_op jit(solution)/shard_map/reduce_scatter | solution.py:201
  506.7 125.0 %all-gather.25.cloned.1.call-start = ((), (), s32[]{:S(2)}) async-start(), calls=%async_computation.17 | async-start | bytes 2621440 | tf_op jit(solution)/shard_map/all_gather | solution.py:256
  507.5 171.1 %all-gather.27.cloned.1.call-start = ((), (), s32[]{:S(2)}) async-start(), calls=%async_computation.18 | async-start | bytes 2621440 | tf_op jit(solution)/shard_map/all_gather | solution.py:206
  585.4 196.1 %copy-start.61 = (f32[2,64]{1,0:T(2,128)}, f32[2,64]{1,0:T(2,128)S(1)}, u32[]{:S(2)}) copy-start(f32[2,64]{1,0:T(2,128)S(1)} %get-tuple-element.410) | copy-start | bytes 1540
  585.4 196.1 %copy-start.66 = (f32[2,64]{1,0:T(2,128)}, f32[2,64]{1,0:T(2,128)S(1)}, u32[]{:S(2)}) copy-start(f32[2,64]{1,0:T(2,128)S(1)} %get-tuple-element.409) | copy-start | bytes 1540
  587.5 191.6 %reduce-scatter.14.cloned.1.call-start = ((), (), s32[]{:S(2)}) async-start(), calls=%async_computation.19 | async-start | bytes 5242880 | tf_op jit(solution)/shard_map/reduce_scatter | solution.py:267
  703.5 127.5 %all-gather.29.cloned.1.call-start = ((), (), s32[]{:S(2)}) async-start(), calls=%async_computation.20 | async-start | bytes 2621440 | tf_op jit(solution)/shard_map/all_gather | solution.py:272
  781.5 53.2 %copy-start.68 = (f32[2,64]{1,0:T(2,128)}, f32[2,64]{1,0:T(2,128)S(1)}, u32[]{:S(2)}) copy-start(f32[2,64]{1,0:T(2,128)S(1)} %broadcast_multiply_fusion.3) | copy-start | bytes 1540
  784.4 123.3 %reduce-scatter.16.cloned.1.call-start = ((), (), s32[]{:S(2)}) async-start(), calls=%async_computation.21 | async-start | bytes 2359296 | tf_op jit(solution)/shard_map/reduce_scatter | solution.py:280
  867.6 85.4 %reduce-scatter.18.cloned.1.call-start = ((), (), s32[]{:S(2)}) async-start(), calls=%async_computation.22 | async-start | bytes 2359296 | tf_op jit(solution)/shard_map/reduce_scatter | solution.py:286
  871.6 132.2 %reduce-scatter.20.cloned.1.call-start = ((), (), s32[]{:S(2)}) async-start(), calls=%async_computation.23 | async-start | bytes 2621440 | tf_op jit(solution)/shard_map/reduce_scatter | solution.py:318
  959.8 362.5 %all-reduce.4.cloned.1.call-start = ((), (), s32[]{:S(2)}) async-start(), calls=%async_computation.24 | async-start | bytes 50331648 | tf_op jit(solution)/shard_map/psum | solution.py:329
  994.0 52.0 %copy-start.11 = (f32[2,64,2048]{2,1,0:T(8,128)S(1)}, f32[2,64,2048]{2,1,0:T(8,128)}, u32[]{:S(2)}) copy-start(f32[2,64,2048]{2,1,0:T(8,128)} %copy-done.10) | copy-start | bytes 3145732
  994.1 52.0 %copy-start.22 = (f32[2,64,2048]{2,1,0:T(8,128)S(1)}, f32[2,64,2048]{2,1,0:T(8,128)}, u32[]{:S(2)}) copy-start(f32[2,64,2048]{2,1,0:T(8,128)} %reduce-scatter.14.cloned.1.call-done) | copy-start | bytes 3145732
  994.1 52.0 %copy-start.28 = (bf16[2,64,2048]{2,1,0:T(8,128)(2,1)S(1)}, bf16[2,64,2048]{2,1,0:T(8,128)(2,1)}, u32[]{:S(2)}) copy-start(bf16[2,64,2048]{2,1,0:T(8,128)(2,1)} %param.21) | copy-start | bytes 1572868
  994.1 52.0 %copy-start.55 = (f32[2048]{0:T(1024)S(1)}, f32[2048]{0:T(1024)}, u32[]{:S(2)}) copy-start(f32[2048]{0:T(1024)} %param.30) | copy-start | bytes 24580
  994.1 52.0 %copy-start.62 = (f32[2,64]{1,0:T(2,128)S(1)}, f32[2,64]{1,0:T(2,128)}, u32[]{:S(2)}) copy-start(f32[2,64]{1,0:T(2,128)} %copy-done.61) | copy-start | bytes 1540
  994.1 52.0 %copy-start.67 = (f32[2,64]{1,0:T(2,128)S(1)}, f32[2,64]{1,0:T(2,128)}, u32[]{:S(2)}) copy-start(f32[2,64]{1,0:T(2,128)} %copy-done.66) | copy-start | bytes 1540
  994.1 52.0 %copy-start.69 = (f32[2,64]{1,0:T(2,128)S(1)}, f32[2,64]{1,0:T(2,128)}, u32[]{:S(2)}) copy-start(f32[2,64]{1,0:T(2,128)} %copy-done.68) | copy-start | bytes 1540
  (101 other events, 607.2 us)
Sparse Core Ops, SparseCore 0:
  10.8 48.6 all-gather.10
  62.9 26.6 all-gather.12
  92.0 28.1 all-gather.14
  153.0 76.7 reduce-scatter.7
  233.8 46.4 all-gather.16
  303.1 42.5 reduce-scatter.9
  350.7 45.2 all-gather.18
  407.8 26.8 all-gather.22
  437.2 27.8 all-gather.20
  506.9 76.7 reduce-scatter.11
  585.3 46.4 all-gather.24
  633.9 44.6 all-gather.26
  703.6 75.4 reduce-scatter.13
  784.5 46.4 all-gather.28
  867.7 39.9 reduce-scatter.15
  911.7 41.2 reduce-scatter.17
  959.9 43.8 reduce-scatter.19
  1010.7 311.6 all-reduce.3
where the time goes:
time: 1370 us; the launch traced here: 1360 us
  waiting for transfers between devices  932 us (68%)
  matrix products  181 us (13%)
  other arithmetic  113 us (8%)
  local copies, waits for them, and re-layouts  77.1 us (6%)
  blocking collectives  40.8 us (3%)
  between operations  15.5 us (1%)
    psum x1, waiting for transfers between devices, body(): lax.psum(query_total.astype(jnp.bfloat16), 'seq').astype(jnp.float32)  274 us
    reduce_scatter x2, waiting for transfers between devices, front(): lax.psum_scatter(project(attn_out, output_weight), 'tp', scatter_dimensio...  153 us
    all_gather x2, waiting for transfers between devices, front(): lax.all_gather(norm1_share.astype(jnp.bfloat16), 'tp', axis=1, tiled=True)  94.1 us
    all_gather x2, waiting for transfers between devices, front(): lax.all_gather(norm2_share.astype(jnp.bfloat16), 'tp', axis=1, tiled=True)  84.6 us
    reduce_scatter x1, waiting for transfers between devices, body(): lax.psum_scatter(normed2_part, 'tp', scatter_dimension=1, tiled=True)  75.6 us
    dot_general x12, matrix products, project(): jnp.einsum('rcd,de->rce', activations, weight_mat, preferred_element_type...  68.8 us
    all_gather x1, waiting for transfers between devices, body(): lax.all_gather(middle_grad.astype(jnp.bfloat16), 'tp', axis=1, tiled=True)  46.1 us
    all_gather x1, waiting for transfers between devices, body(): out_rows = lax.all_gather(output_grad, 'tp', axis=1, tiled=True)  44.1 us
  transfers between devices with their start and end apart: 18, of which 18 were waited for; matrix products, arithmetic and copies ran while one was open for 10% of the time, Pallas kernels for 0%

commit v1 on v0

--- a/solution.py
+++ b/solution.py
@@ -12,7 +12,9 @@
 
 
 def doc_tables(document_lengths, length):
-    doc_ends = jnp.cumsum(document_lengths, axis=1)
+    doc_ends = jnp.stack(
+        [jnp.sum(document_lengths[:, : n + 1], axis=1) for n in range(document_lengths.shape[1])], axis=1
+    )
     doc_starts = doc_ends - document_lengths
     places = jnp.arange(length, dtype=jnp.int32)
     segment = jnp.sum((places[None, :, None] >= doc_ends[:, None, :]).astype(jnp.int32), axis=2)
@@ -199,8 +201,8 @@
             jnp.bfloat16
         )
         attn_share = lax.psum_scatter(
-            project(attn_out, output_weight), "tp", scatter_dimension=1, tiled=True
-        )
+            project(attn_out, output_weight).astype(jnp.bfloat16), "tp", scatter_dimension=1, tiled=True
+        ).astype(jnp.float32)
         middle = hidden_base + attn_share
         norm2_share, norm2_inverse = rms_forward(middle, feedforward_gain)
         normed2 = lax.all_gather(norm2_share.astype(jnp.bfloat16), "tp", axis=1, tiled=True)
@@ -232,8 +234,6 @@
         project(state[16], down_weight).astype(jnp.bfloat16), "tp", scatter_dimension=1, tiled=True
     ).astype(jnp.float32)
     block_out = (state[11] + feedforward_share).astype(jnp.bfloat16)
-    hidden_again, block_out = lax.optimization_barrier((hidden_float, block_out))
-    state = front(hidden_again)
     (
         norm1_inverse,
         normed1,
@@ -264,7 +264,9 @@
     gate_total = weight_grad(normed2, gate_grad)
     up_total = weight_grad(normed2, up_grad)
     normed2_part = project_back(gate_grad, gate_weight) + project_back(up_grad, up_weight)
-    normed2_grad = lax.psum_scatter(normed2_part, "tp", scatter_dimension=1, tiled=True)
+    normed2_grad = lax.psum_scatter(
+        normed2_part.astype(jnp.bfloat16), "tp", scatter_dimension=1, tiled=True
+    ).astype(jnp.float32)
     middle_through, feedforward_gain_part = rms_backward(
         middle, norm2_inverse, feedforward_gain, normed2_grad
     )

time: 1370 us -> 998 us (0.73)
  waiting for transfers between devices: 932 us -> 645 us
  matrix products: 181 us -> 124 us
  other arithmetic: 113 us -> 86.6 us
    reduce_scatter x3 -> x2, waiting for transfers between devices: 229 us -> 86.1 us  [the longest x1 43.4 us: front(): lax.psum_scatter(project(attn_out, output_weight).astype(jnp.bfloat16), '...]
    all_gather x2 -> x1, waiting for transfers between devices: 94.1 us -> 44.1 us  [front(): lax.all_gather(norm1_share.astype(jnp.bfloat16), 'tp', axis=1, tiled=True)]
    all_gather x2 -> x1, waiting for transfers between devices: 84.6 us -> 38.2 us  [front(): lax.all_gather(norm2_share.astype(jnp.bfloat16), 'tp', axis=1, tiled=True)]
    reduce_scatter x1, waiting for transfers between devices: 40.6 us -> 0.01 us  [body(): lax.psum_scatter(project(state[16], down_weight).astype(jnp.bfloat16), 't...]
    psum x1, waiting for transfers between devices: 274 us -> 313 us  [body(): lax.psum(query_total.astype(jnp.bfloat16), 'seq').astype(jnp.float32)]
    dot_general x12 -> x7, matrix products: 68.8 us -> 37.7 us  [project(): jnp.einsum('rcd,de->rce', activations, weight_mat, preferred_element_type...]
    all_gather x2 -> x1, waiting for transfers between devices: 35.5 us -> 6.36 us  [front(): lax.all_gather(key_local, 'seq', axis=1, tiled=True)]
    dot_general x4 -> x2, matrix products: 22.4 us -> 4.96 us  [one_row(): jnp.einsum('kgql,lkd->qkgd', probability, value_row, preferred_element_ty...]
  transfers between devices with their start and end apart: 18 -> 13, of which waited for: 18 -> 11; matrix products, arithmetic and copies ran while one was open for 10% -> 13% of each run, Pallas kernels for 0% -> 0%
where the time goes in v1:
time: 998 us; the launch traced here: 992 us
  waiting for transfers between devices  645 us (65%)
  matrix products  124 us (12%)
  other arithmetic  86.6 us (9%)
  local copies, waits for them, and re-layouts  76.1 us (8%)
  blocking collectives  43.6 us (4%)
  between operations  14.9 us (1%)
    psum x1, waiting for transfers between devices, body(): lax.psum(query_total.astype(jnp.bfloat16), 'seq').astype(jnp.float32)  313 us
    all_gather x1, waiting for transfers between devices, body(): lax.all_gather(middle_grad.astype(jnp.bfloat16), 'tp', axis=1, tiled=True)  45.1 us
    all_gather x1, waiting for transfers between devices, front(): lax.all_gather(norm1_share.astype(jnp.bfloat16), 'tp', axis=1, tiled=True)  44.1 us
    psum x1, blocking collectives, body(): lax.psum((attention_gain_part, query_gain_part, key_gain_part, feedforwar...  43.6 us
    reduce_scatter x1, waiting for transfers between devices, front(): lax.psum_scatter(project(attn_out, output_weight).astype(jnp.bfloat16), '...  43.4 us
    all_gather x1, waiting for transfers between devices, body(): out_rows = lax.all_gather(output_grad, 'tp', axis=1, tiled=True)  42.9 us
    reduce_scatter x1, waiting for transfers between devices, body(): lax.psum_scatter(normed2_part.astype(jnp.bfloat16), 'tp', scatter_dimensi...  42.7 us
    all_gather x1, waiting for transfers between devices, front(): lax.all_gather(norm2_share.astype(jnp.bfloat16), 'tp', axis=1, tiled=True)  38.2 us
  transfers between devices with their start and end apart: 13, of which 11 were waited for; matrix products, arithmetic and copies ran while one was open for 13% of the time, Pallas kernels for 0%

profile of v1, /device:TPU:0, one launch (start us, length us, event | category | flops | bytes accessed | tf_op | source)
XLA Modules:
  0.0 992.4 jit_solution(3358059744379380965)
XLA Ops:
  16.5 44.1 %all-gather.7.cloned.1.call-done = bf16[2,256,2048]{2,1,0:T(8,128)(2,1)} async-done(((bf16[2,64,2048]{2,1,0:T(8,128)(2,1)}), bf16[2,256,2048]{2,1,0:T(8,128)(2,1)}) %all-gather.7.cloned.1.call-update) | async-done | bytes 2097168 | tf_op jit(solution)/shard_map/all_gather | solution.py:178
  73.7 4.5 fusion.72
  88.1 6.4 all-gather.11.cloned.1.call-done
  94.4 3.9 copy.245
  98.4 26.5 %all-gather.9.cloned.1.call-done = bf16[2,2048,256]{2,1,0:T(8,128)(2,1)} async-done(((bf16[2,256,256]{2,1,0:T(8,128)(2,1)}), bf16[2,2048,256]{2,1,0:T(8,128)(2,1)}) %all-gather.9.cloned.1.call-update) | async-done | bytes 2097168 | tf_op jit(solution)/shard_map/all_gather | solution.py:195
  124.9 4.0 reshape.255
  128.8 27.7 %while.28 = (s32[]{:T(128)}, bf16[2,256,2,2,128]{1,4,3,2,0:T(8,128)(2,1)}, f32[2,2,2,256]{3,2,1,0:T(2,128)S(1)}, bf16[2,2048,2,128]{3,2,1,0:T(2,128)(2,1)}, pred...) while((s32[]{:T(128)}, ...), condition=%wide.region_11.12_spmd.clone, body=%wide.region_8.11_spmd.sunk.clone | while | flops 1098906624 | bytes 53773580 | solution.py:104
  160.8 43.4 %reduce-scatter.7.cloned.1.call-done = bf16[2,64,2048]{2,1,0:T(8,128)(2,1)} async-done(((bf16[2,256,2048]{2,1,0:T(8,128)(2,1)}), bf16[2,64,2048]{2,1,0:T(8,128)(2,1)}) %reduce-scatter.7.cloned.1.call-update) | async-done | bytes 524304 | tf_op jit(solution)/shard_map/reduce_scatter | solution.py:203
  208.2 42.9 %all-gather.15.cloned.1.call-done = bf16[2,256,2048]{2,1,0:T(8,128)(2,1)} async-done(((bf16[2,64,2048]{2,1,0:T(8,128)(2,1)}), bf16[2,256,2048]{2,1,0:T(8,128)(2,1)}) %all-gather.15.cloned.1.call-update) | async-done | bytes 2097168 | tf_op jit(solution)/shard_map/all_gather | solution.py:256
  251.0 8.5 fusion.49
  259.6 38.2 %all-gather.13.cloned.1.call-done = bf16[2,256,2048]{2,1,0:T(8,128)(2,1)} async-done(((bf16[2,64,2048]{2,1,0:T(8,128)(2,1)}), bf16[2,256,2048]{2,1,0:T(8,128)(2,1)}) %all-gather.13.cloned.1.call-update) | async-done | bytes 2097168 | tf_op jit(solution)/shard_map/all_gather | solution.py:208
  297.8 6.3 fusion.55
  304.2 8.5 multiply_convert_fusion.1
  316.2 4.6 add_convert_fusion.1
  320.9 42.7 %reduce-scatter.11.cloned.1.call-done = bf16[2,64,2048]{2,1,0:T(8,128)(2,1)} async-done(((bf16[2,256,2048]{2,1,0:T(8,128)(2,1)}), bf16[2,64,2048]{2,1,0:T(8,128)(2,1)}) %reduce-scatter.11.cloned.1.call-update) | async-done | bytes 524304 | tf_op jit(solution)/shard_map/reduce_scatter | solution.py:267
  369.0 45.1 %all-gather.17.cloned.1.call-done = bf16[2,256,2048]{2,1,0:T(8,128)(2,1)} async-done(((bf16[2,64,2048]{2,1,0:T(8,128)(2,1)}), bf16[2,256,2048]{2,1,0:T(8,128)(2,1)}) %all-gather.17.cloned.1.call-update) | async-done | bytes 2097168 | tf_op jit(solution)/shard_map/all_gather | solution.py:274
  414.2 3.7 fusion.74
  419.8 33.0 %while.29 = (s32[]{:T(128)}, f32[2,256,2,2,128]{1,4,3,2,0:T(8,128)}, bf16[2,2048,2,128]{1,3,2,0:T(8,128)(2,1)}, bf16[2,2048,2,128]{1,3,2,0:T(8,128)(2,1)}, bf16[...) while((s32[]{:T(128)}, ...), condition=%wide.region_19.20_spmd.clone, body=%wide.region_17.19_spmd.sunk.clone | while | flops 2716466176 | bytes 129531248 | solution.py:137
  478.9 14.0 %reduce-scatter.13.cloned.1.call-done = bf16[2,256,256]{1,2,0:T(8,128)(2,1)} async-done(((bf16[2,2048,256]{1,2,0:T(8,128)(2,1)}), bf16[2,256,256]{1,2,0:T(8,128)(2,1)}) %reduce-scatter.13.cloned.1.call-update) | async-done | bytes 262160 | tf_op jit(solution)/shard_map/reduce_scatter | solution.py:282
  506.3 4.1 fusion.96
  510.3 27.9 %reduce-scatter.15.cloned.1.call-done = bf16[2,256,256]{2,1,0:T(8,128)(2,1)} async-done(((bf16[2,2048,256]{2,1,0:T(8,128)(2,1)}), bf16[2,256,256]{2,1,0:T(8,128)(2,1)}) %reduce-scatter.15.cloned.1.call-update) | async-done | bytes 262160 | tf_op jit(solution)/shard_map/reduce_scatter | solution.py:288
  540.9 4.3 add_convert_fusion
  545.4 8.0 fusion.63
  553.5 8.4 bitcast_convert_fusion
  561.9 5.4 bitcast_convert_fusion.2
  567.3 5.4 bitcast_convert_fusion.1
  593.4 43.6 %all-reduce = (f32[2048]{0:T(1024)}, f32[128]{0:T(128)}, f32[128]{0:T(128)}, f32[2048]{0:T(1024)}) all-reduce(f32[2048]{0:T(1024)S(1)} %get-tuple-element.231, f32[128]{0:T(128)S(1)} %fusion.95, f32[128]{0:T(128)S(1)} %fusion.104, f32[2048]{0:T(1024)S(1)} %copy-done.51), channel_id=1, replica_groups=mesh['seq'=8,'tp'=4] {'seq','tp'}, use_global_device_ids=true, to_apply=%region_27.28 | all-reduce | flops 4352 | bytes 34816 | tf_op jit(solution)/shard_map/psum | solution.py:327
  640.2 313.1 %all-reduce.4.cloned.1.call-done = (bf16[2048,512]{1,0:T(8,128)(2,1)}, bf16[2048,256]{1,0:T(8,128)(2,1)}, bf16[2048,256]{1,0:T(8,128)(2,1)}, bf16[512,2048]{1,0:...) async-done(((bf16[2048,512]{1,0:T(8,128)(2,1)}, bf16[2048,256]{1,0:T(8,128)(2,1)}, bf16[2048,256]{1,0:T(8,128)(2,1)}, ...) | async-done | bytes 25165840 | tf_op jit(solution)/shard_map/psum | solution.py:331
  953.3 4.3 convert_element_type.179
  963.3 9.5 convert_element_type.187
  972.8 6.6 convert_element_type.189
  979.4 6.3 convert_element_type.191
  (356 shorter events, 183.1 us)
Async XLA Ops:
  7.2 149.4 %copy-start = (bf16[512,2048]{1,0:T(8,128)(2,1)S(1)}, bf16[512,2048]{1,0:T(8,128)(2,1)}, u32[]{:S(2)}) copy-start(bf16[512,2048]{1,0:T(8,128)(2,1)} %param.27) | copy-start | bytes 6291460
  7.2 53.4 %all-gather.7.cloned.1.call-start = ((), (), s32[]{:S(2)}) async-start(), calls=%async_computation.6 | async-start | bytes 2621440 | tf_op jit(solution)/shard_map/all_gather | solution.py:178
  11.8 54.1 %copy-start.64 = (f32[128]{0:T(128)S(1)}, f32[128]{0:T(128)}, u32[]{:S(2)}) copy-start(f32[128]{0:T(128)} %param.26) | copy-start | bytes 1540
  11.8 82.7 %all-gather.11.cloned.1.call-start = ((), (), s32[]{:S(2)}) async-start(), calls=%async_computation.8 | async-start | bytes 2359296 | tf_op jit(solution)/shard_map/all_gather | solution.py:194
  16.5 49.9 %copy-start.15 = (f32[2,256,64]{2,1,0:T(8,128)}, f32[2,256,64]{2,1,0:T(8,128)S(1)}, u32[]{:S(2)}) copy-start(f32[2,256,64]{2,1,0:T(8,128)S(1)} %get-tuple-element.308) | copy-start | bytes 393220
  16.5 69.5 %copy-start.13 = (f32[2,256,64]{2,1,0:T(8,128)}, f32[2,256,64]{2,1,0:T(8,128)S(1)}, u32[]{:S(2)}) copy-start(f32[2,256,64]{2,1,0:T(8,128)S(1)} %get-tuple-element.307) | copy-start | bytes 393220
  67.4 57.5 %all-gather.9.cloned.1.call-start = ((), (), s32[]{:S(2)}) async-start(), calls=%async_computation.7 | async-start | bytes 2359296 | tf_op jit(solution)/shard_map/all_gather | solution.py:195
  70.7 133.5 %reduce-scatter.7.cloned.1.call-start = ((), (), s32[]{:S(2)}) async-start(), calls=%async_computation.9 | async-start | bytes 2621440 | tf_op jit(solution)/shard_map/reduce_scatter | solution.py:203
  160.2 45.5 %copy-start.46 = (f32[2048]{0:T(1024)S(1)}, f32[2048]{0:T(1024)}, u32[]{:S(2)}) copy-start(f32[2048]{0:T(1024)} %param.28) | copy-start | bytes 24580
  160.2 90.8 %all-gather.15.cloned.1.call-start = ((), (), s32[]{:S(2)}) async-start(), calls=%async_computation.12 | async-start | bytes 2621440 | tf_op jit(solution)/shard_map/all_gather | solution.py:256
  160.8 137.0 %all-gather.13.cloned.1.call-start = ((), (), s32[]{:S(2)}) async-start(), calls=%async_computation.10 | async-start | bytes 2621440 | tf_op jit(solution)/shard_map/all_gather | solution.py:208
  205.7 160.2 %copy-start.52 = (f32[2,64]{1,0:T(2,128)}, f32[2,64]{1,0:T(2,128)S(1)}, u32[]{:S(2)}) copy-start(f32[2,64]{1,0:T(2,128)S(1)} %get-tuple-element.314) | copy-start | bytes 1540
  205.7 160.2 %copy-start.57 = (f32[2,64]{1,0:T(2,128)}, f32[2,64]{1,0:T(2,128)S(1)}, u32[]{:S(2)}) copy-start(f32[2,64]{1,0:T(2,128)S(1)} %get-tuple-element.313) | copy-start | bytes 1540
  207.9 155.7 %reduce-scatter.11.cloned.1.call-start = ((), (), s32[]{:S(2)}) async-start(), calls=%async_computation.13 | async-start | bytes 2621440 | tf_op jit(solution)/shard_map/reduce_scatter | solution.py:267
  297.8 14.9 %slice-start.4 = ((s8[6291456]{0:T(1024)(128)(4,1)}), s8[4194304]{0:T(1024)(128)(4,1)S(1)}, s32[]{:S(2)}) async-start(s8[6291456]{0:T(1024)(128)(4,1)} %bitcast.377), calls=%async_computation.23 | async-start | bytes 8388608
  297.8 18.4 %slice-start.6 = ((s8[6291456]{0:T(1024)(128)(4,1)}), s8[4194304]{0:T(1024)(128)(4,1)S(1)}, s32[]{:S(2)}) async-start(s8[6291456]{0:T(1024)(128)(4,1)} %bitcast.379), calls=%async_computation.25 | async-start | bytes 8388608
  320.9 93.3 %all-gather.17.cloned.1.call-start = ((), (), s32[]{:S(2)}) async-start(), calls=%async_computation.14 | async-start | bytes 2621440 | tf_op jit(solution)/shard_map/all_gather | solution.py:274
  365.9 51.9 %copy-start.59 = (f32[2,64]{1,0:T(2,128)}, f32[2,64]{1,0:T(2,128)S(1)}, u32[]{:S(2)}) copy-start(f32[2,64]{1,0:T(2,128)S(1)} %broadcast_multiply_fusion.3) | copy-start | bytes 1540
  368.7 124.1 %reduce-scatter.13.cloned.1.call-start = ((), (), s32[]{:S(2)}) async-start(), calls=%async_computation.15 | async-start | bytes 2359296 | tf_op jit(solution)/shard_map/reduce_scatter | solution.py:282
  452.8 85.4 %reduce-scatter.15.cloned.1.call-start = ((), (), s32[]{:S(2)}) async-start(), calls=%async_computation.16 | async-start | bytes 2359296 | tf_op jit(solution)/shard_map/reduce_scatter | solution.py:288
  456.8 135.1 %reduce-scatter.17.cloned.1.call-start = ((), (), s32[]{:S(2)}) async-start(), calls=%async_computation.17 | async-start | bytes 2621440 | tf_op jit(solution)/shard_map/reduce_scatter | solution.py:320
  545.2 91.8 %reduce-scatter.9.cloned.1.call-start = ((), (), s32[]{:S(2)}) async-start(), calls=%async_computation.11 | async-start | bytes 2621440 | tf_op jit(solution)/shard_map/reduce_scatter | solution.py:233
  553.5 399.9 %all-reduce.4.cloned.1.call-start = ((), (), s32[]{:S(2)}) async-start(), calls=%async_computation.18 | async-start | bytes 50331648 | tf_op jit(solution)/shard_map/psum | solution.py:331
  590.6 46.4 %copy-start.11 = (bf16[2,64,2048]{2,1,0:T(8,128)(2,1)S(1)}, bf16[2,64,2048]{2,1,0:T(8,128)(2,1)}, u32[]{:S(2)}) copy-start(bf16[2,64,2048]{2,1,0:T(8,128)(2,1)} %reduce-scatter.7.cloned.1.call-done) | copy-start | bytes 1572868
  590.6 46.4 %copy-start.22 = (bf16[2,64,2048]{2,1,0:T(8,128)(2,1)S(1)}, bf16[2,64,2048]{2,1,0:T(8,128)(2,1)}, u32[]{:S(2)}) copy-start(bf16[2,64,2048]{2,1,0:T(8,128)(2,1)} %param.19) | copy-start | bytes 1572868
  590.6 46.4 %copy-start.23 = (bf16[2,64,2048]{2,1,0:T(8,128)(2,1)S(1)}, bf16[2,64,2048]{2,1,0:T(8,128)(2,1)}, u32[]{:S(2)}) copy-start(bf16[2,64,2048]{2,1,0:T(8,128)(2,1)} %reduce-scatter.11.cloned.1.call-done) | copy-start | bytes 1572868
  590.7 46.4 %copy-start.47 = (f32[2048]{0:T(1024)S(1)}, f32[2048]{0:T(1024)}, u32[]{:S(2)}) copy-start(f32[2048]{0:T(1024)} %param.28) | copy-start | bytes 24580
  590.7 46.4 %copy-start.53 = (f32[2,64]{1,0:T(2,128)S(1)}, f32[2,64]{1,0:T(2,128)}, u32[]{:S(2)}) copy-start(f32[2,64]{1,0:T(2,128)} %copy-done.52) | copy-start | bytes 1540
  590.7 46.4 %copy-start.58 = (f32[2,64]{1,0:T(2,128)S(1)}, f32[2,64]{1,0:T(2,128)}, u32[]{:S(2)}) copy-start(f32[2,64]{1,0:T(2,128)} %copy-done.57) | copy-start | bytes 1540
  590.7 46.4 %copy-start.60 = (f32[2,64]{1,0:T(2,128)S(1)}, f32[2,64]{1,0:T(2,128)}, u32[]{:S(2)}) copy-start(f32[2,64]{1,0:T(2,128)} %copy-done.59) | copy-start | bytes 1540
  590.7 46.4 %copy-start.63 = (f32[2,64]{1,0:T(2,128)S(1)}, f32[2,64]{1,0:T(2,128)}, u32[]{:S(2)}) copy-start(f32[2,64]{1,0:T(2,128)} %get-tuple-element.311) | copy-start | bytes 1540
  963.3 16.1 %slice-start = ((s8[6291456]{0:T(1024)(128)(4,1)}), s8[4194304]{0:T(1024)(128)(4,1)S(1)}, s32[]{:S(2)}) async-start(s8[6291456]{0:T(1024)(128)(4,1)} %bitcast.357), calls=%async_computation.19 | async-start | bytes 8388608
  (78 other events, 279.6 us)
Sparse Core Ops, SparseCore 0:
  11.9 48.6 all-gather.6
  67.5 26.9 all-gather.10
  96.9 27.8 all-gather.8
  160.3 43.8 reduce-scatter.6
  205.7 45.2 all-gather.14
  253.1 44.6 all-gather.12
  321.0 42.5 reduce-scatter.10
  368.9 45.2 all-gather.16
  452.9 39.9 reduce-scatter.12
  496.9 41.2 reduce-scatter.14
  545.3 43.8 reduce-scatter.16
  592.1 44.0 reduce-scatter.8
  642.4 310.9 all-reduce.3

commit v2 on v0

v2 whole, which is shorter than its diff:
```python
import functools
import math

import jax
import jax.numpy as jnp
from jax import lax
from jax.experimental import pallas as pl
from jax.experimental.pallas import tpu as pltpu
from jax.sharding import PartitionSpec as P

HEAD = 128
EPS = 1e-06
ROPE_BASE = 1000000.0
MASKED = -1e30
LOG2E = math.log2(math.e)
BF = jnp.bfloat16
F32 = jnp.float32
I32 = jnp.int32


def sds(shape, dtype):
    return jax.ShapeDtypeStruct(shape, dtype)


def hbm(shape, dtype):
    return pltpu.HBM(shape, dtype)


def whole(shape):
    return pl.BlockSpec(shape, lambda *_: (0,) * len(shape))


def dot_nn(a, b):
    return lax.dot_general(a, b, (((1,), (0,)), ((), ())), preferred_element_type=F32)


def dot_nt(a, b):
    return lax.dot_general(a, b, (((1,), (1,)), ((), ())), preferred_element_type=F32)


def dot_tn(a, b):
    return lax.dot_general(a, b, (((0,), (0,)), ((), ())), preferred_element_type=F32)


def in_hbm(value):
    return pltpu.with_memory_space_constraint(value, pltpu.HBM)


def call(body, grid, in_specs, out_specs, out_shape, scratch, operands, mib, prefetch=1, after=(), aliases={}):
    after = (*ORDER, *after)
    at, extra = prefetch + len(in_specs), len(after)

    def run(*refs):
        return body(*refs[:at], *refs[at + extra :])

    operands = operands[:prefetch] + tuple(in_hbm(v) for v in operands[prefetch:])
    outs = pl.pallas_call(
        run,
        grid_spec=pltpu.PrefetchScalarGridSpec(
            num_scalar_prefetch=prefetch,
            grid=grid,
            in_specs=in_specs + [pl.BlockSpec(memory_space=pl.ANY)] * extra,
            out_specs=out_specs,
            scratch_shapes=scratch,
        ),
        out_shape=out_shape,
        input_output_aliases=aliases,
        compiler_params=pltpu.CompilerParams(
            vmem_limit_bytes=mib << 20, dimension_semantics=("arbitrary",) * len(grid)
        ),
        cost_estimate=pl.CostEstimate(flops=1, bytes_accessed=1, transcendentals=0),
    )(*operands, *(in_hbm(v) for v in after))
    ORDER[:] = [outs[0]]
    return outs


ORDER = []


def flip(axis, mask):
    return [(i, i ^ mask) for i in range(lax.axis_size(axis))]


def swap(value, axis, mask):
    return lax.ppermute(value, axis, flip(axis, mask))


def gather_tp(share):
    rows, _, width = share.shape
    return lax.all_gather(share, "tp", axis=1, tiled=True).reshape(-1, width)


def scatter_tp(part, row_count):
    part = part.reshape(row_count, -1, part.shape[1])
    return lax.psum_scatter(part, "tp", scatter_dimension=1, tiled=True)


def half_out(x_ref, core, keep_ref, send_ref):
    half = keep_ref.shape[1]
    keep_ref[...] = x_ref[:, pl.ds(pl.multiple_of(core * half, half), half)]
    send_ref[...] = x_ref[:, pl.ds(pl.multiple_of((1 - core) * half, half), half)]


def qkv_kernel(row_count, meta, x, wq, wk, wv, gq, gk, cos, sin, q_out, kv_out, q_raw, k_raw, keep, send, acc_q, acc_k, acc_v):
    j, last = pl.program_id(0), pl.num_programs(0) - 1

    @pl.when(j == 0)
    def _():
        half_out(x, meta[0], keep, send)
        acc_q[...] = jnp.zeros_like(acc_q)
        acc_k[...] = jnp.zeros_like(acc_k)
        acc_v[...] = jnp.zeros_like(acc_v)

    depth = wq.shape[0]
    xs = x[:, pl.ds(pl.multiple_of(j * depth, depth), depth)]
    acc_q[...] += dot_nn(xs, wq[...])
    acc_k[...] += dot_nn(xs, wk[...])
    acc_v[...] += dot_nn(xs, wv[...])

    @pl.when(j == last)
    def _():
        def turn(raw, gain):
            inverse = lax.rsqrt(jnp.mean(raw * raw, axis=-1, keepdims=True) + EPS)
            normed = raw * inverse * gain
            return (normed * cos[...] + pltpu.roll(normed, HEAD // 2, 1) * sin[...]).astype(BF)

        q_raw[...] = acc_q[...]
        k_raw[...] = acc_k[...]
        for h in range(acc_q.shape[1] // HEAD):
            at = slice(h * HEAD, (h + 1) * HEAD)
            q_out[:, at] = turn(acc_q[:, at], gq[...])
        span = kv_out.shape[2]
        for h in range(acc_k.shape[1] // HEAD):
            at = slice(h * HEAD, (h + 1) * HEAD)
            turned = turn(acc_k[:, at], gk[...])
            for r in range(row_count):
                kv_out[r, 0, :, at] = turned[r * span : (r + 1) * span]
        for r in range(row_count):
            kv_out[r, 1] = acc_v[r * span : (r + 1) * span, :].astype(BF)


def qkv_call(meta, row_count, x, weights, gains, tables):
    tokens, width = x.shape
    nq, nk = weights[0].shape[1], weights[1].shape[1]
    depth = width // 4
    row = lambda n: pl.BlockSpec((depth, n), lambda j, *_: (j, 0))
    kv = (row_count, 2, tokens // row_count, nk)
    return call(
        functools.partial(qkv_kernel, row_count),
        (4,),
        [whole((tokens, width)), row(nq), row(nk), row(nk)]
        + [whole((1, HEAD))] * 2
        + [whole((tokens, HEAD))] * 2,
        [whole((tokens, nq)), whole(kv), whole((tokens, nq)), whole((tokens, nk))]
        + [whole((tokens, width // 2))] * 2,
        [hbm((tokens, nq), BF), hbm(kv, BF), hbm((tokens, nq), F32), hbm((tokens, nk), F32)]
        + [hbm((tokens, width // 2), BF)] * 2,
        [pltpu.VMEM((tokens, nq), F32), pltpu.VMEM((tokens, nk), F32), pltpu.VMEM((tokens, nk), F32)],
        (meta, x, *weights, *gains, *tables),
        40,
    )


def stack_heads(ref, group):
    return jnp.concatenate([ref[:, h * HEAD : (h + 1) * HEAD] for h in range(group)], axis=0)


def tall(ref, group):
    return jnp.concatenate([ref[...]] * group, axis=0)


def attend_kernel(slot_count, group, scale, meta, *refs):
    q_ref, refs = refs[0], refs[1:]
    keys, refs = refs[:slot_count], refs[slot_count:]
    q_place, q_start, k_place, wo = refs[:4]
    o_out, lse_out, part_out = refs[4:7]
    scores, acc = refs[7:]
    r, g, last = pl.program_id(0), pl.program_id(1), pl.num_programs(1) - 1
    first = r * slot_count
    bases = pl.num_programs(0) * slot_count
    span = q_ref.shape[0]
    queries = stack_heads(q_ref, group)
    low = tall(q_start, group)
    high = tall(q_place, group)
    top = jnp.full((group * span, HEAD), MASKED, F32)

    for s in range(slot_count):

        def some(top, s=s):
            raw = dot_nt(queries, keys[s][0, 0]) * scale
            place = k_place[...] + meta[bases + s]
            kept = jnp.where((place >= low) & (place <= high), raw, MASKED)
            scores[s] = kept
            for c in range(span // HEAD):
                top = jnp.maximum(top, kept[:, c * HEAD : (c + 1) * HEAD])
            return top

        top = lax.cond(meta[first + s] > 0, some, lambda t: t, top)

    peak = jnp.max(top, axis=-1, keepdims=True)
    total = jnp.zeros((group * span, HEAD), F32)
    out = jnp.zeros((group * span, HEAD), F32)
    for s in range(slot_count):

        def more(carry, s=s):
            total, out = carry
            power = jnp.exp2(scores[s] - peak)
            for c in range(span // HEAD):
                total = total + power[:, c * HEAD : (c + 1) * HEAD]
            return total, out + dot_nn(power.astype(BF), keys[s][0, 1])

        total, out = lax.cond(meta[first + s] > 0, more, lambda t: t, (total, out))

    total = jnp.sum(total, axis=-1, keepdims=True)
    lse_out[0, 0] = peak + jnp.log2(total)
    out = (out / total).astype(BF)
    out = jnp.concatenate([out[h * span : (h + 1) * span] for h in range(group)], axis=1)
    o_out[...] = out
    part = dot_nn(out, wo[...])

    @pl.when(g == 0)
    def _():
        acc[...] = part

    @pl.when(g > 0)
    def _():
        acc[...] += part

    @pl.when(g == last)
    def _():
        part_out[...] = acc[...].astype(BF)


def attend_call(meta, queries, kv_slots, places, wo):
    slot_count = len(kv_slots)
    tokens, nq = queries.shape
    row_count, _, span, nk = kv_slots[0].shape
    heads, group = nk // HEAD, nq // nk
    width = wo.shape[1]
    wide = group * HEAD
    rows = pl.BlockSpec((span, wide), lambda r, g, *_: (r, g))
    column = pl.BlockSpec((span, 1), lambda r, g, *_: (r, 0))
    return call(
        functools.partial(attend_kernel, slot_count, group, HEAD**-0.5 * LOG2E),
        (row_count, heads),
        [rows]
        + [pl.BlockSpec((1, 2, span, HEAD), lambda r, g, *_: (r, 0, 0, g))] * slot_count
        + [column, column, whole((1, span))]
        + [pl.BlockSpec((wide, width), lambda r, g, *_: (g, 0))],
        [
            rows,
            pl.BlockSpec((1, 1, group * span, 1), lambda r, g, *_: (r, g, 0, 0)),
            pl.BlockSpec((span, width), lambda r, g, *_: (r, 0)),
        ],
        [hbm((tokens, nq), BF), hbm((row_count, heads, group * span, 1), F32), hbm((tokens, width), BF)],
        [pltpu.VMEM((slot_count, group * span, span), F32), pltpu.VMEM((span, width), F32)],
        (meta, queries, *kv_slots, *places, wo),
        40,
    )


def ff_kernel(meta, x, og, wg, wu, wd, hm_out, gu_out, grad_out, keep, send, acc):
    j, last = pl.program_id(0), pl.num_programs(0) - 1

    @pl.when(j == 0)
    def _():
        half_out(x, meta[0], keep, send)
        acc[...] = jnp.zeros_like(acc)

    gate = dot_nn(x[...], wg[...])
    up = dot_nn(x[...], wu[...])
    upstream = dot_nt(og[...], wd[...])
    sigmoid = 1.0 / (1.0 + jnp.exp(-gate))
    silu = gate * sigmoid
    gate_grad = (upstream * up * sigmoid * (1.0 + gate * (1.0 - sigmoid))).astype(BF)
    up_grad = (upstream * silu).astype(BF)
    hm_out[...] = (silu * up).astype(BF)
    gu_out[0] = gate_grad
    gu_out[1] = up_grad
    acc[...] += dot_nt(gate_grad, wg[...]) + dot_nt(up_grad, wu[...])

    @pl.when(j == last)
    def _():
        grad_out[...] = acc[...].astype(BF)


def ff_call(meta, x, og, wg, wu, wd, after):
    tokens, width = x.shape
    hidden = wg.shape[1]
    block = 256
    column = pl.BlockSpec((width, block), lambda j, *_: (0, j))
    return call(
        ff_kernel,
        (hidden // block,),
        [whole((tokens, width))] * 2 + [column, column, pl.BlockSpec((block, width), lambda j, *_: (j, 0))],
        [
            pl.BlockSpec((tokens, block), lambda j, *_: (0, j)),
            pl.BlockSpec((2, tokens, block), lambda j, *_: (0, 0, j)),
            whole((tokens, width)),
            whole((tokens, width // 2)),
            whole((tokens, width // 2)),
        ],
        [hbm((tokens, hidden), BF), hbm((2, tokens, hidden), BF), hbm((tokens, width), BF)]
        + [hbm((tokens, width // 2), BF)] * 2,
        [pltpu.VMEM((tokens, width), F32)],
        (meta, x, og, wg, wu, wd),
        48,
        after=after,
    )


def ff_out_kernel(hm, wd, out, acc):
    j, last = pl.program_id(0), pl.num_programs(0) - 1
    part = dot_nn(hm[...], wd[...])

    @pl.when(j == 0)
    def _():
        acc[...] = part

    @pl.when(j > 0)
    def _():
        acc[...] += part

    @pl.when(j == last)
    def _():
        out[...] = acc[...].astype(BF)


def ff_out_call(hm, wd):
    tokens, hidden = hm.shape
    width = wd.shape[1]
    block = hidden // 3
    return call(
        ff_out_kernel,
        (3,),
        [pl.BlockSpec((tokens, block), lambda j: (0, j)), pl.BlockSpec((block, width), lambda j: (j, 0))],
        [whole((tokens, width))],
        [hbm((tokens, width), BF)],
        [pltpu.VMEM((tokens, width), F32)],
        (hm, wd),
        32,
        prefetch=0,
    )[0]


def norm_back(turned, raw, gain, cos, sin):
    upstream = turned * cos - pltpu.roll(turned, HEAD // 2, 1) * sin
    inverse = lax.rsqrt(jnp.mean(raw * raw, axis=-1, keepdims=True) + EPS)
    scaled = upstream * gain
    through = inverse * scaled - raw * (inverse * inverse * inverse) * jnp.mean(
        raw * scaled, axis=-1, keepdims=True
    )
    return through.astype(BF), jnp.sum(upstream * raw * inverse, axis=0, keepdims=True)


def attend_back_kernel(slot_count, group, scale, meta, *refs):
    bg, wo, q_ref, refs = refs[0], refs[1], refs[2], refs[3:]
    keys, refs = refs[:slot_count], refs[slot_count:]
    o_ref, lse_ref, q_place, q_start, k_place, q_raw, gq, cos, sin = refs[:9]
    dq_out, even_out, odd_out, gain_out, keep, send = refs[9:15]
    r, g = pl.program_id(0), pl.program_id(1)
    first = r * slot_count
    bases = pl.num_programs(0) * slot_count

    @pl.when(g == 0)
    def _():
        half_out(bg, meta[bases + slot_count], keep, send)

    @pl.when((r == 0) & (g == 0))
    def _():
        gain_out[...] = jnp.zeros_like(gain_out)

    span = q_ref.shape[0]
    d_out = dot_nt(bg[...], wo[...]).astype(BF)
    d_out = jnp.concatenate([d_out[:, h * HEAD : (h + 1) * HEAD] for h in range(group)], axis=0)
    o_rows = stack_heads(o_ref, group)
    queries = stack_heads(q_ref, group)
    centre = jnp.sum(d_out.astype(F32) * o_rows.astype(F32), axis=-1, keepdims=True)
    lse = lse_ref[0, 0]
    low = tall(q_start, group)
    high = tall(q_place, group)
    dq = jnp.zeros((group * span, HEAD), F32)
    for s in range(slot_count):
        out = (odd_out if s % 2 else even_out).at[s // 2, 0]

        def some(dq, s=s, out=out):
            raw = dot_nt(queries, keys[s][0, 0]) * (scale * LOG2E)
            place = k_place[...] + meta[bases + s]
            probs = jnp.where((place >= low) & (place <= high), jnp.exp2(raw - lse), 0.0)
            d_probs = dot_nt(d_out, keys[s][0, 1])
            d_score = (probs * (d_probs - centre)).astype(BF)
            out[0] = (dot_tn(d_score, queries) * scale).astype(BF)
            out[1] = dot_tn(probs.astype(BF), d_out).astype(BF)
            return dq + dot_nn(d_score, keys[s][0, 0])

        def none(dq, out=out):
            out[...] = jnp.zeros(out.shape, BF)
            return dq

        dq = lax.cond(meta[first + s] > 0, some, none, dq)

    gain = gq[...]
    gain_total = jnp.zeros((1, HEAD), F32)
    for h in range(group):
        rows = dq[h * span : (h + 1) * span] * scale
        d_raw, part = norm_back(rows, q_raw[:, h * HEAD : (h + 1) * HEAD], gain, cos[...], sin[...])
        dq_out[:, h * HEAD : (h + 1) * HEAD] = d_raw
        gain_total = gain_total + part
    gain_out[...] += gain_total


def attend_back_call(meta, bg, wo, queries, kv_slots, attended, lse, places, q_raw, gq, tables):
    slot_count = len(kv_slots)
    tokens, width = bg.shape
    nq = queries.shape[1]
    row_count, _, span, nk = kv_slots[0].shape
    heads, group = nk // HEAD, nq // nk
    wide = group * HEAD
    rows = pl.BlockSpec((span, wide), lambda r, g, *_: (r, g))
    by_row = lambda n: pl.BlockSpec((span, n), lambda r, g, *_: (r, 0))
    kv_out = pl.BlockSpec((slot_count // 2, 1, 2, span, HEAD), lambda r, g, *_: (0, r, 0, 0, g))
    kv_shape = (slot_count // 2, row_count, 2, span, nk)
    return call(
        functools.partial(attend_back_kernel, slot_count, group, HEAD**-0.5),
        (row_count, heads),
        [by_row(width), pl.BlockSpec((wide, width), lambda r, g, *_: (g, 0)), rows]
        + [pl.BlockSpec((1, 2, span, HEAD), lambda r, g, *_: (r, 0, 0, g))] * slot_count
        + [rows, pl.BlockSpec((1, 1, group * span, 1), lambda r, g, *_: (r, g, 0, 0))]
        + [by_row(1), by_row(1), whole((1, span))]
        + [rows, whole((1, HEAD)), by_row(HEAD), by_row(HEAD)],
        [rows, kv_out, kv_out, whole((1, HEAD)), by_row(width // 2), by_row(width // 2)],
        [
            hbm((tokens, nq), BF),
            hbm(kv_shape, BF),
            hbm(kv_shape, BF),
            sds((1, HEAD), F32),
            hbm((tokens, width // 2), BF),
            hbm((tokens, width // 2), BF),
        ],
        [],
        (meta, bg, wo, queries, *kv_slots, attended, lse, *places, q_raw, gq, *tables),
        40,
    )


def back_kernel(count, row_count, *refs):
    pieces, refs = refs[:count], refs[count:]
    dq_ref, k_raw, gk, cos, sin, wq, wk, wv = refs[:8]
    all_out, part_out, gain_out = refs[8:11]
    j = pl.program_id(0)
    nq, nk = wq.shape[1], wk.shape[1]
    span = pieces[0].shape[2]

    @pl.when(j == 0)
    def _():
        all_out[:, :nq] = dq_ref[...]
        gain_total = jnp.zeros((1, HEAD), F32)
        for r in range(row_count):
            rows = slice(r * span, (r + 1) * span)
            for h in range(nk // HEAD):
                at = slice(h * HEAD, (h + 1) * HEAD)
                turned = sum(p[r, 0, :, at].astype(F32) for p in pieces)
                d_raw, part = norm_back(turned, k_raw[rows, at], gk[...], cos[rows], sin[rows])
                all_out[rows, nq + h * HEAD : nq + (h + 1) * HEAD] = d_raw
                gain_total = gain_total + part
            all_out[rows, nq + nk :] = sum(p[r, 1].astype(F32) for p in pieces).astype(BF)
        gain_out[...] = gain_total

    part = (
        dot_nt(all_out[:, :nq], wq[...])
        + dot_nt(all_out[:, nq : nq + nk], wk[...])
        + dot_nt(all_out[:, nq + nk :], wv[...])
    )
    part_out[...] = part.astype(BF)


def back_call(pieces, dq, k_raw, gk, tables, weights):
    tokens, nq = dq.shape
    nk = k_raw.shape[1]
    width = weights[0].shape[0]
    block = width // 4
    row = lambda n: pl.BlockSpec((block, n), lambda j, *_: (j, 0))
    return call(
        functools.partial(back_kernel, len(pieces), pieces[0].shape[0]),
        (4,),
        [whole(pieces[0].shape)] * len(pieces)
        + [whole((tokens, nq)), whole((tokens, nk)), whole((1, HEAD)), whole((tokens, HEAD)), whole((tokens, HEAD))]
        + [row(nq), row(nk), row(nk)],
        [whole((tokens, nq + 2 * nk)), pl.BlockSpec((tokens, block), lambda j, *_: (0, j)), whole((1, HEAD))],
        [hbm((tokens, nq + 2 * nk), BF), hbm((tokens, width), BF), sds((1, HEAD), F32)],
        [],
        (*pieces, dq, k_raw, gk, *tables, *weights),
        40,
        prefetch=0,
    )


def grad_kernel(count, ids, *refs):
    lefts, rights = refs[:count], refs[count : 2 * count]
    a_out, b_out = refs[2 * count :]
    f = pl.program_id(1)

    def put(out):
        if len(out.shape) == 3:
            for n in range(out.shape[0]):
                out[n] = sum(dot_tn(x[...], r[n]) for x, r in zip(lefts, rights)).astype(BF)
        else:
            out[...] = sum(dot_tn(x[...], r[...]) for x, r in zip(lefts, rights)).astype(BF)

    @pl.when(f == 0)
    def _():
        put(a_out)

    @pl.when(f == 1)
    def _():
        put(b_out)


def grad_call(ids, rows, lefts, rights):
    tokens, cols = rights[0].shape[-2:]
    lead = rights[0].shape[:-2]
    zeros = (0,) * len(lead)
    n = math.prod(lead) * cols
    wide = next(w for w in (512, 384, 256, 128) if cols % w == 0)
    out_a = pl.BlockSpec((*lead, rows, wide), lambda c, f, ids: (*zeros, 0, c))
    out_b = pl.BlockSpec((*lead, rows, wide), lambda c, f, ids: (*zeros, 0, jnp.where(f == 0, jnp.maximum(c - 1, 0), c)))
    return call(
        functools.partial(grad_kernel, len(lefts)),
        (cols // wide, 2),
        [pl.BlockSpec((tokens, rows), lambda c, f, ids: (0, ids[f]))] * len(lefts)
        + [pl.BlockSpec((*lead, tokens, wide), lambda c, f, ids: (*zeros, 0, c))] * len(rights),
        [out_a, out_b],
        [hbm((*lead, rows, cols), BF)] * 2,
        [],
        (ids, *lefts, *rights),
        40,
    )


def split_kernel(bits, keep_a, got_a, keep_b, got_b, send_a, next_a, send_b, next_b):
    j = pl.program_id(0)

    def put(out, keep, got):
        out[...] = (keep[...].astype(F32) + got[...].astype(F32)).astype(BF)

    @pl.when(j == 0)
    def _():
        put(send_a, keep_a, got_a)
        put(send_b, keep_b, got_b)

    @pl.when(j == 1)
    def _():
        put(next_a, keep_a, got_a)
        put(next_b, keep_b, got_b)


def split_call(bits, keeps, gots):
    *lead, rows, cols = keeps[0].shape
    zeros = (0,) * len(lead)
    half = (*lead, rows // 2, cols)
    part = lambda f: pl.BlockSpec(half, lambda j, bits: (*zeros, jnp.where(j == 0, 1 - bits[f], bits[f]), 0))
    send_a, next_a, send_b, next_b = call(
        split_kernel,
        (2,),
        [part(0), part(0), part(1), part(1)],
        [whole(half)] * 4,
        [hbm(half, BF)] * 4,
        [],
        (bits, keeps[0], gots[0], keeps[1], gots[1]),
        40,
    )
    return (send_a, send_b), (next_a, next_b)


def add_kernel(keep_a, got_a, keep_b, got_b, out_a, out_b):
    out_a[...] = (keep_a[...].astype(F32) + got_a[...].astype(F32)).astype(BF)
    out_b[...] = (keep_b[...].astype(F32) + got_b[...].astype(F32)).astype(BF)


def add_call(keeps, gots):
    shape = keeps[0].shape
    return call(
        add_kernel,
        (1,),
        [whole(shape)] * 4,
        [whole(shape)] * 2,
        [hbm(shape, BF)] * 2,
        [],
        (keeps[0], gots[0], keeps[1], gots[1]),
        40,
        prefetch=0,
    )


def put_wide(piece, outs, split):
    if len(piece.shape) == 3:
        for n, out in enumerate(outs):
            out[...] = piece[n].astype(F32)
    else:
        at = 0
        for out, wide in zip(outs, split):
            out[...] = piece[:, at : at + wide].astype(F32)
            at += wide


def widen_kernel(count, split, table, *refs):
    pieces, joined, outs = refs[:count], refs[count], refs[count + 1 :]
    j = pl.program_id(0)
    for k, ref in enumerate(pieces):

        @pl.when(j == k)
        def _(ref=ref):
            joined[...] = ref[...]
            put_wide(ref, outs, split)


def widen_split(pieces, shapes, by_rows):
    lead, cols = pieces[0].shape[:-2], pieces[0].shape[-1]
    split = [cols] if not by_rows or lead else [s[1] for s in shapes]
    return split * len(shapes) if lead else split


def widen_call(table, pieces, shapes, by_rows):
    *lead, rows, cols = pieces[0].shape
    zeros = (0,) * len(lead)
    split = widen_split(pieces, shapes, by_rows)
    count = len(pieces)
    return call(
        functools.partial(widen_kernel, count, split),
        (count,),
        [whole(pieces[0].shape)] * count,
        [pl.BlockSpec((*lead, rows, cols), lambda j, t: (*zeros, j, 0))]
        + [pl.BlockSpec((rows, w), lambda j, t: (t[0, j], t[1, j])) for w in split],
        [hbm((*lead, count * rows, cols), BF)] + [hbm(s, F32) for s in shapes],
        [],
        (table, *pieces),
        48,
    )


def widen_other_kernel(count, split, table, joined, *refs):
    put_wide(joined, refs[count:], split)


def widen_other_call(table, joined, outs, by_rows):
    *lead, rows, cols = joined.shape
    zeros = (0,) * len(lead)
    count = table.shape[1]
    shapes = [o.shape for o in outs]
    split = widen_split([joined], shapes, by_rows)
    return call(
        functools.partial(widen_other_kernel, len(outs), split),
        (count,),
        [pl.BlockSpec((*lead, rows // count, cols), lambda j, t: (*zeros, j, 0))]
        + [pl.BlockSpec(memory_space=pl.ANY)] * len(outs),
        [pl.BlockSpec((rows // count, w), lambda j, t: (t[0, j], t[1, j])) for w in split],
        [hbm(s, F32) for s in shapes],
        [],
        (table, joined, *outs),
        40,
        aliases={2 + k: k for k in range(len(outs))},
    )


def norm_kernel(x, gain, out):
    value = x[...].astype(F32)
    inverse = lax.rsqrt(jnp.mean(value * value, axis=-1, keepdims=True) + EPS)
    out[...] = (value * inverse * gain[...]).astype(BF)


def norm_call(x, gain):
    return call(
        norm_kernel,
        (1,),
        [whole(x.shape), whole(gain.shape)],
        [whole(x.shape)],
        [hbm(x.shape, BF)],
        [],
        (x, gain),
        24,
        prefetch=0,
    )[0]


def middle_kernel(x, got, gain, middle, out):
    value = x[...].astype(F32) + got[...].astype(F32)
    inverse = lax.rsqrt(jnp.mean(value * value, axis=-1, keepdims=True) + EPS)
    middle[...] = value
    out[...] = (value * inverse * gain[...]).astype(BF)


def middle_call(x, got, gain, after):
    return call(
        middle_kernel,
        (1,),
        [whole(x.shape), whole(x.shape), whole(gain.shape)],
        [whole(x.shape)] * 2,
        [hbm(x.shape, F32), hbm(x.shape, BF)],
        [],
        (x, got, gain),
        24,
        prefetch=0,
        after=after,
    )


def norm_grad_kernel(x, got, base, gain, *outs):
    value, upstream = x[...].astype(F32), got[...].astype(F32)
    inverse = lax.rsqrt(jnp.mean(value * value, axis=-1, keepdims=True) + EPS)
    scaled = upstream * gain[...]
    through = inverse * scaled - value * (inverse * inverse * inverse) * jnp.mean(
        value * scaled, axis=-1, keepdims=True
    )
    total = base[...].astype(F32) + through
    outs[0][...] = total
    outs[1][...] = jnp.sum(upstream * value * inverse, axis=0, keepdims=True)
    if len(outs) > 2:
        outs[2][...] = total.astype(BF)


def norm_grad_call(x, got, base, gain, low):
    return call(
        norm_grad_kernel,
        (1,),
        [whole(x.shape)] * 3 + [whole(gain.shape)],
        [whole(x.shape), whole(gain.shape)] + [whole(x.shape)] * low,
        [hbm(x.shape, F32), hbm(gain.shape, F32)] + [hbm(x.shape, BF)] * low,
        [],
        (x, got, base, gain),
        24,
        prefetch=0,
    )


def copy_kernel(x, out):
    out[...] = x[...]


def copy_call(x):
    return call(copy_kernel, (1,), [whole(x.shape)], [whole(x.shape)], [hbm(x.shape, x.dtype)], [], (x,), 24, prefetch=0)[0]


def flow_table(masks):
    seq = lax.axis_index("seq")
    slot = jnp.arange(1 << len(masks), dtype=I32)
    block = jnp.zeros_like(slot)
    for level, mask in enumerate(masks):
        shift = len(masks) - 1 - level
        block = block + (((seq & mask) // mask) ^ ((slot >> shift) & 1)) * (1 << shift)
    return block


class WeightSum:
    def __init__(self, lefts, rights, masks, shapes, by_rows):
        self.lefts, self.rights, self.shapes, self.by_rows = lefts, rights, shapes, by_rows
        self.flows = (masks, masks[::-1])
        seq = lax.axis_index("seq")
        core = seq & 1
        self.bits = [jnp.stack([(seq & m[k]) // m[k] for m in self.flows]) for k in range(len(masks))]
        self.level = 0
        slots = 1 << len(masks)
        inner = [flow_table(m) for m in self.flows]
        rows_of = jnp.concatenate([inner[0], slots + inner[1]])
        zero = jnp.zeros_like(rows_of)
        if by_rows:
            self.tables = [jnp.stack([half * 2 * slots + rows_of, zero]) for half in (core, 1 - core)]
        else:
            self.tables = [jnp.stack([rows_of, zero + half]) for half in (core, 1 - core)]

    def swap_level(self, sends):
        self.gots = [swap(s, "seq", m[self.level]) for s, m in zip(sends, self.flows)]
        self.level += 1

    def send(self):
        rows = self.lefts[0].shape[1]
        self.direct = rows % (4 * HEAD) == 0
        if self.direct:
            base = jnp.array([0, 2], I32)
            self.swap_level(grad_call(base + 1 - self.bits[0], rows // 4, self.lefts, self.rights))
        return self

    def keep(self):
        rows = self.lefts[0].shape[1]
        if self.direct:
            base = jnp.array([0, 2], I32)
            self.kept = grad_call(base + self.bits[0], rows // 4, self.lefts, self.rights)
        else:
            self.kept = grad_call(jnp.arange(2, dtype=I32), rows // 2, self.lefts, self.rights)
            half, at = rows // 4, self.kept[0].ndim - 2
            cut = lambda v, b: lax.dynamic_slice_in_dim(v, b * half, half, at)
            self.swap_level([cut(v, 1 - self.bits[0][f]) for f, v in enumerate(self.kept)])
            self.kept = [cut(v, self.bits[0][f]) for f, v in enumerate(self.kept)]
        return self

    def middle(self):
        while self.level < len(self.flows[0]):
            sends, self.kept = split_call(self.bits[self.level], self.kept, self.gots)
            self.swap_level(sends)
        return self

    def last(self):
        self.pieces = []
        for piece, masks in zip(add_call(self.kept, self.gots), self.flows):
            pieces = [piece]
            for mask in reversed(masks):
                pieces = [v for p in pieces for v in (p, None)]
                pieces[1::2] = [swap(p, "seq", mask) for p in pieces[::2]]
            self.pieces.append(pieces)
        return self

    def own(self):
        joined, *self.outs = widen_call(self.tables[0], self.ordered(), self.shapes, self.by_rows)
        self.joined = swap(joined, "seq", 1)
        return self

    def ordered(self):
        found = []
        levels = len(self.flows[0])
        for pieces in self.pieces:
            back = lambda s: sum(((s >> k) & 1) << (levels - 1 - k) for k in range(levels))
            found += [pieces[back(s)] for s in range(len(pieces))]
        return found

    def other(self):
        return widen_other_call(self.tables[1], self.joined, self.outs, self.by_rows)


def halves(value, core):
    half = value.shape[1] // 2
    return (
        lax.dynamic_slice_in_dim(value, core * half, half, 1),
        lax.dynamic_slice_in_dim(value, (1 - core) * half, half, 1),
    )


def body(
    hidden_in,
    output_grad,
    document_lengths,
    attention_gain,
    query_weight,
    key_weight,
    value_weight,
    query_gain,
    key_gain,
    output_weight,
    feedforward_gain,
    gate_weight,
    up_weight,
    down_weight,
):
    ORDER.clear()
    tp, seqs = lax.axis_size("tp"), lax.axis_size("seq")
    seq_at = lax.axis_index("seq")
    core = seq_at & 1
    row_count, share, width = hidden_in.shape
    span = share * tp
    masks = tuple(1 << b for b in range(1, seqs.bit_length() - 1))

    ends = jnp.stack(
        [jnp.sum(document_lengths[:, : n + 1], axis=1) for n in range(document_lengths.shape[1])], axis=1
    )
    starts = ends - document_lengths
    local = jnp.arange(span, dtype=I32)
    places = seq_at * span + local
    inside = (places[None, :, None] >= starts[:, None]) & (places[None, :, None] < ends[:, None])
    begun = jnp.sum(jnp.where(inside, starts[:, None], 0), axis=2)
    slot_seq = jnp.arange(seqs, dtype=I32) ^ seq_at
    needed = (slot_seq <= seq_at)[None] & ((slot_seq + 1)[None] * span > begun[:, :1])
    meta = jnp.concatenate([needed.astype(I32).reshape(-1), slot_seq * span, core[None]])
    place_set = (jnp.tile(places, row_count)[:, None], begun.reshape(-1, 1), local[None, :])
    frequency = ROPE_BASE ** (-2.0 * jnp.arange(HEAD // 2, dtype=F32) / HEAD)
    angles = (places[None] - begun).reshape(-1, 1).astype(F32) * frequency
    cos, sin = jnp.cos(angles), jnp.sin(angles)
    tables = (jnp.concatenate([cos, cos], 1), jnp.concatenate([-sin, sin], 1))
    core_meta = core[None]
    q_gain, k_gain = query_gain[None], key_gain[None]
    qkv_weights = (query_weight, key_weight, value_weight)

    flat = lambda v: v.reshape(-1, width)
    hidden, upward = flat(hidden_in), flat(output_grad)
    attn_gain, ff_gain = attention_gain[None], feedforward_gain[None]
    shares = lambda v: v.reshape(row_count, share, width)
    normed1 = gather_tp(shares(norm_call(hidden, attn_gain)))
    queries, kv, q_raw, k_raw, n1_keep, n1_send = qkv_call(
        core_meta, row_count, normed1, qkv_weights, (q_gain, k_gain), tables
    )
    grads = gather_tp(shares(copy_call(upward)))
    kv_slots = []
    for value in [kv] + [swap(kv, "seq", m) for m in range(2, seqs, 2)]:
        kv_slots += [value, swap(value, "seq", 1)]
    attended, lse, o_part = attend_call(meta, queries, kv_slots, place_set, output_weight)

    def both(own, sent=None):
        return [own, swap(own if sent is None else sent, "seq", 1)]

    o_both = both(attended)
    n1_both = both(n1_keep, n1_send)
    middle, normed2 = middle_call(hidden, flat(scatter_tp(o_part, row_count)), ff_gain, (grads,))
    grads_both = both(*halves(grads, core))
    normed2 = gather_tp(shares(normed2))
    hidden_mid, gate_up, n2_part, n2_keep, n2_send = ff_call(
        core_meta, normed2, grads, gate_weight, up_weight, down_weight, (grads_both[1], o_both[1], n1_both[1])
    )
    n2_got = scatter_tp(n2_part, row_count)

    down = WeightSum(both(hidden_mid), grads_both, masks, [down_weight.shape], False).send()
    gate = WeightSum(both(n2_keep, n2_send), both(gate_up), masks, [gate_weight.shape, up_weight.shape], True).send()
    down.keep()
    gate.keep()
    down.middle()
    middle_grad, ff_gain_grad, branch = norm_grad_call(middle, flat(n2_got), upward, ff_gain, True)
    branch = gather_tp(shares(branch))
    down.last()
    gate.middle()
    dq, even, odd, q_gain_grad, b_keep, b_send = attend_back_call(
        meta,
        branch,
        output_weight,
        queries,
        kv_slots,
        attended,
        lse,
        place_set,
        q_raw,
        q_gain,
        tables,
    )
    gate.last()
    odd = swap(odd, "seq", 1)
    chip = [(even[k].astype(F32) + odd[k].astype(F32)).astype(BF) for k in range(seqs // 2)]
    pieces = [chip[0]] + [swap(chip[m // 2], "seq", m) for m in range(2, seqs, 2)]
    out = WeightSum(o_both, both(b_keep, b_send), masks, [output_weight.shape], False).send().keep()
    ff_part = ff_out_call(hidden_mid, down_weight)
    ff_got = scatter_tp(ff_part, row_count)
    down.own()
    all_grad, n1_part, k_gain_grad = back_call(pieces, dq, k_raw, k_gain, tables, qkv_weights)
    n1_got = scatter_tp(n1_part, row_count)
    out.middle()
    qkv = WeightSum(n1_both, both(all_grad), masks, [w.shape for w in qkv_weights], True).send().keep()
    out.last()
    (down_out,) = down.other()
    qkv.middle()
    qkv.last()
    block_out = shares((middle + flat(ff_got).astype(F32)).astype(BF))
    input_grad, attn_gain_grad = norm_grad_call(hidden, flat(n1_got), middle_grad, attn_gain, False)
    input_grad = shares(input_grad)
    gate.own()
    out.own()
    gate_out, up_out = gate.other()
    (output_out,) = out.other()
    qkv.own()
    query_out, key_out, value_out = qkv.other()

    gains = jnp.concatenate(
        [v.reshape(-1) for v in (attn_gain_grad, ff_gain_grad, q_gain_grad, k_gain_grad)]
    ).reshape(-1, HEAD)
    for axis, size in (("tp", tp), ("seq", seqs)):
        mask = 1
        while mask < size:
            gains = gains + swap(gains, axis, mask)
            mask *= 2
    gains = gains.reshape(-1)
    return (
        block_out,
        input_grad,
        gains[:width],
        query_out,
        key_out,
        value_out,
        gains[2 * width : 2 * width + HEAD],
        gains[2 * width + HEAD :],
        output_out,
        gains[width : 2 * width],
        gate_out,
        up_out,
        down_out,
    )


def solution(mesh):
    tokens, columns, rows = P(None, ("seq", "tp"), None), P(None, "tp"), P("tp", None)
    in_specs = (
        tokens,
        tokens,
        P(),
        P(),
        columns,
        columns,
        columns,
        P(),
        P(),
        rows,
        P(),
        columns,
        columns,
        rows,
    )
    out_specs = (
        tokens,
        tokens,
        P(),
        columns,
        columns,
        columns,
        P(),
        P(),
        rows,
        P(),
        columns,
        columns,
        rows,
    )
    return jax.shard_map(body, mesh=mesh, in_specs=in_specs, out_specs=out_specs, check_vma=False)
```

time: 1370 us -> 690 us (0.50)
  waiting for transfers between devices: 932 us -> 327 us
  Pallas kernels: 0 us -> 239 us
  matrix products: 181 us -> 0 us
  other arithmetic: 113 us -> 9.95 us
  starting transfers between devices: 2.29 us -> 66 us
  local copies, waits for them, and re-layouts: 77.1 us -> 24.2 us
  blocking collectives: 40.8 us -> 0 us
    reduce_scatter x7 -> x4, waiting for transfers between devices: 322 us -> 48.4 us  [scatter_tp(): return lax.psum_scatter(part, 'tp', scatter_dimension=1, tiled=True)]
    psum x1 -> x0, waiting for transfers between devices: 274 us -> none  [body(): lax.psum(query_total.astype(jnp.bfloat16), 'seq').astype(jnp.float32)]
    all_gather x10 -> x4, waiting for transfers between devices: 335 us -> 86.3 us  [gather_tp(): return lax.all_gather(share, 'tp', axis=1, tiled=True).reshape(-1, width)]
    pallas_call x0 -> x35, Pallas kernels: none -> 239 us  [call(): pl.pallas_call(run, grid_spec=pltpu.PrefetchScalarGridSpec(num_scalar_pre...]
    ppermute x0 -> x68, waiting for transfers between devices: none -> 192 us  [swap(): return lax.ppermute(value, axis, flip(axis, mask))]
    dot_general x44 -> x0, matrix products: 181 us -> none  [the longest x12 68.8 us: project(): jnp.einsum('rcd,de->rce', activations, weight_mat, preferred_element_type...]
    ppermute x0 -> x68, starting transfers between devices: none -> 65.3 us  [swap(): return lax.ppermute(value, axis, flip(axis, mask))]
    convert_element_type x19 -> x3, other arithmetic: 55.7 us -> 4.97 us  [the longest x1 2.94 us: body(): (even[k].astype(F32) + odd[k].astype(F32)).astype(BF)]
  transfers between devices with their start and end apart: 18 -> 76, of which waited for: 18 -> 33; matrix products, arithmetic and copies ran while one was open for 10% -> 2% of each run, Pallas kernels for 0% -> 21%
where the time goes in v2:
time: 690 us; the launch traced here: 681 us
  waiting for transfers between devices  327 us (47%)
  Pallas kernels  239 us (35%)
  starting transfers between devices  66 us (10%)
  local copies, waits for them, and re-layouts  24.2 us (4%)
  between operations  15.2 us (2%)
  other arithmetic  9.95 us (1%)
    pallas_call x35, Pallas kernels, call(): pl.pallas_call(run, grid_spec=pltpu.PrefetchScalarGridSpec(num_scalar_pre...  239 us
    ppermute x68, waiting for transfers between devices, swap(): return lax.ppermute(value, axis, flip(axis, mask))  192 us
    all_gather x4, waiting for transfers between devices, gather_tp(): return lax.all_gather(share, 'tp', axis=1, tiled=True).reshape(-1, width)  86.3 us
    ppermute x68, starting transfers between devices, swap(): return lax.ppermute(value, axis, flip(axis, mask))  65.3 us
    reduce_scatter x4, waiting for transfers between devices, scatter_tp(): return lax.psum_scatter(part, 'tp', scatter_dimension=1, tiled=True)  48.4 us
    unnamed x156, local copies, waits for them, and re-layouts  20.4 us
  transfers between devices with their start and end apart: 76, of which 33 were waited for; matrix products, arithmetic and copies ran while one was open for 2% of the time, Pallas kernels for 21%

profile of v2, /device:TPU:0, one launch (start us, length us, event | category | flops | bytes accessed | tf_op | source)
XLA Modules:
  0.0 681.3 jit_solution(10414549999674444642)
XLA Ops:
  14.9 43.9 %all-gather.5.cloned.1.call-done = bf16[2,256,2048]{2,1,0:T(8,128)(2,1)} async-done(((bf16[2,64,2048]{2,1,0:T(8,128)(2,1)}), bf16[2,256,2048]{2,1,0:T(8,128)(2,1)}) %all-gather.5.cloned.1.call-update) | async-done | bytes 2097168 | tf_op jit(solution)/shard_map/all_gather | solution.py:90
  58.8 9.3 %shard_map.310 = (bf16[512,512]{1,0:T(8,128)(2,1)}, bf16[2,2,256,256]{3,2,1,0:T(8,128)(2,1)}, f32[512,512]{1,0:T(8,128)}, f32[512,256]{1,0:T(8,128)}, bf16[512,1...) custom-call(s32[1]{0:T(128)} %bitcast.4.refs_0_, bf16[512,2048]{1,0:T(8,128)(2,1)} %bitcast.100, bf16[2048,512]{1,0:T(8,128)(2,1)} %refs_9_.1, ...), custom_call_target="tpu_custom_call" | custom-call | flops 1 | bytes 1 | tf_op jit(solution)/shard_map/pallas_call | solution.py:57
  73.9 12.1 %collective-permute-done.5.refs_8_.refs_10_ = bf16[2,2,256,256]{3,2,1,0:T(8,128)(2,1)S(1)} collective-permute-done((bf16[2,2,256,256]{3,2,1,0:T(8,128)(2,1)S(1)}, bf16[2,2,256,256]{3,2,1,0:T(8,128)(2,1)S(1)}, u32[]{:S(2)}, u32[]{:S(2)}) %collective-permute-start.5) | collective-permute-done | bytes 524320 | tf_op jit(solution)/shard_map/ppermute | solution.py:85
  86.0 10.0 %collective-permute-done.3.refs_6_.refs_8_ = bf16[2,2,256,256]{3,2,1,0:T(8,128)(2,1)S(1)} collective-permute-done((bf16[2,2,256,256]{3,2,1,0:T(8,128)(2,1)S(1)}, bf16[2,2,256,256]{3,2,1,0:T(8,128)(2,1)S(1)}, u32[]{:S(2)}, u32[]{:S(2)}) %collective-permute-start.3) | collective-permute-done | bytes 524320 | tf_op jit(solution)/shard_map/ppermute | solution.py:85
  99.4 13.2 %shard_map.312 = (bf16[512,512]{1,0:T(8,128)(2,1)}, f32[2,2,512,1]{3,2,1,0:T(8,128)}, bf16[512,2048]{1,0:T(8,128)(2,1)}) custom-call(s32[25]{0:T(128)S(1)} %pad_add_fusion.1.refs_0_, bf16[512,512]{1,0:T(8,128)(2,1)} %get-tuple-element.99.refs_1_.refs_3_, bf16[2,2,256,256]{3,2,1,0:T(8,128)(2,1)} %get-tuple-element.100.refs_2_.refs_4_, ...), custom_call_target="tpu_custom_call" | custom-call | flops 1 | bytes 1 | tf_op jit(solution)/shard_map/pallas_call | solution.py:57
  114.9 48.3 %reduce-scatter.5.cloned.1.call-done = bf16[2,64,2048]{2,1,0:T(8,128)(2,1)} async-done(((bf16[2,256,2048]{2,1,0:T(8,128)(2,1)}), bf16[2,64,2048]{2,1,0:T(8,128)(2,1)}) %reduce-scatter.5.cloned.1.call-update) | async-done | bytes 524304 | tf_op jit(solution)/shard_map/reduce_scatter | solution.py:95
  171.1 40.2 %all-gather.9.cloned.1.call-done = bf16[2,256,2048]{2,1,0:T(8,128)(2,1)} async-done(((bf16[2,64,2048]{2,1,0:T(8,128)(2,1)}), bf16[2,256,2048]{2,1,0:T(8,128)(2,1)}) %all-gather.9.cloned.1.call-update) | async-done | bytes 2097168 | tf_op jit(solution)/shard_map/all_gather | solution.py:90
  211.3 36.9 %shard_map.314 = (bf16[512,1536]{1,0:T(8,128)(2,1)}, bf16[2,512,1536]{2,1,0:T(8,128)(2,1)}, bf16[512,2048]{1,0:T(8,128)(2,1)}, bf16[512,1024]{1,0:T(8,128)(2,1)}, bf16[512,1024]{1,0:T(8,128)(2,1)}) custom-call(s32[1]{0:T(128)} %bitcast.4.refs_0_, bf16[512,2048]{1,0:T(8,128)(2,1)} %bitcast.93, bf16[512,2048]{1,0:T(8,128)(2,1)} %bitcast.81, ...), custom_call_target="tpu_custom_call" | custom-call | flops 1 | bytes 1 | tf_op jit(solution)/shard_map/pallas_call | solution.py:57
  250.2 7.6 %collective-permute-done.10.refs_2_ = bf16[512,1536]{1,0:T(8,128)(2,1)S(1)} collective-permute-done((bf16[512,1536]{1,0:T(8,128)(2,1)S(1)}, bf16[512,1536]{1,0:T(8,128)(2,1)S(1)}, u32[]{:S(2)}, u32[]{:S(2)}) %collective-permute-start.10) | collective-permute-done | bytes 1572896 | tf_op jit(solution)/shard_map/ppermute | solution.py:85
  258.9 6.4 shard_map.315
  268.3 10.2 %shard_map.316 = (bf16[2,256,1536]{2,1,0:T(8,128)(2,1)}, bf16[2,256,1536]{2,1,0:T(8,128)(2,1)}) custom-call(s32[2]{0:T(128)S(1)} %get-tuple-element.210.refs_0_, bf16[512,1024]{1,0:T(8,128)(2,1)} %get-tuple-element.108.refs_1_, bf16[512,1024]{1,0:T(8,128)(2,1)} %collective-permute-done.11.refs_2_, bf16[2,512,1536]{2,1,0:T(8,128)(2,1)} %get-tuple-element.110.refs_3_, ...), custom_call_target="tpu_custom_call" | custom-call | flops 1 | bytes 1 | tf_op jit(solution)/shard_map/pallas_call | solution.py:57
  278.6 6.4 shard_map.317
  284.9 10.2 %shard_map.318 = (bf16[2,256,1536]{2,1,0:T(8,128)(2,1)}, bf16[2,256,1536]{2,1,0:T(8,128)(2,1)}) custom-call(s32[2]{0:T(128)S(1)} %get-tuple-element.211.refs_0_, bf16[512,1024]{1,0:T(8,128)(2,1)} %get-tuple-element.108.refs_1_, bf16[512,1024]{1,0:T(8,128)(2,1)} %collective-permute-done.11.refs_2_, bf16[2,512,1536]{2,1,0:T(8,128)(2,1)} %get-tuple-element.110.refs_3_, ...), custom_call_target="tpu_custom_call" | custom-call | flops 1 | bytes 1 | tf_op jit(solution)/shard_map/pallas_call | solution.py:57
  308.2 41.0 %collective-permute-done.18.refs_3_ = bf16[192,1024]{1,0:T(8,128)(2,1)S(1)} collective-permute-done((bf16[192,1024]{1,0:T(8,128)(2,1)S(1)}, bf16[192,1024]{1,0:T(8,128)(2,1)S(1)}, u32[]{:S(2)}, u32[]{:S(2)}) %collective-permute-start.18) | collective-permute-done | bytes 393248 | tf_op jit(solution)/shard_map/ppermute | solution.py:85
  360.1 12.9 %shard_map.323 = (bf16[512,512]{1,0:T(8,128)(2,1)}, bf16[4,2,2,256,256]{4,3,2,1,0:T(8,128)(2,1)}, bf16[4,2,2,256,256]{4,3,2,1,0:T(8,128)(2,1)}, f32[1,128]{1,0:T...) custom-call(s32[25]{0:T(128)S(1)} %pad_add_fusion.1.refs_0_, bf16[512,2048]{1,0:T(8,128)(2,1)} %bitcast.99, ...), custom_call_target="tpu_custom_call" | custom-call | flops 1 | bytes 1 | tf_op jit(solution)/shard_map/pallas_call | solution.py:57
  374.1 11.8 %collective-permute-start.30 = (bf16[192,1024]{1,0:T(8,128)(2,1)S(1)}, bf16[192,1024]{1,0:T(8,128)(2,1)S(1)}, u32[]{:S(2)}, u32[]{:S(2)}) collective-permute-start(bf16[192,1024]{1,0:T(8,128)(2,1)S(1)} %copy-done.40), channel_id=1, source_target_pairs={{0,16},{4,20},{8,24},{12,28},{16,0},{20,4},{24,8},{28,12},{1,17},{... | collective-permute-start | bytes 1179656 | tf_op jit(solution)/shard_map/ppermute | solution.py:85
  388.1 7.5 %collective-permute-done.30.refs_7_ = bf16[192,1024]{1,0:T(8,128)(2,1)S(1)} collective-permute-done((bf16[192,1024]{1,0:T(8,128)(2,1)S(1)}, bf16[192,1024]{1,0:T(8,128)(2,1)S(1)}, u32[]{:S(2)}, u32[]{:S(2)}) %collective-permute-start.30) | collective-permute-done | bytes 393248 | tf_op jit(solution)/shard_map/ppermute | solution.py:85
  401.8 20.9 %collective-permute-done.27.refs_3_ = bf16[192,1024]{1,0:T(8,128)(2,1)S(1)} collective-permute-done((bf16[192,1024]{1,0:T(8,128)(2,1)S(1)}, bf16[192,1024]{1,0:T(8,128)(2,1)S(1)}, u32[]{:S(2)}, u32[]{:S(2)}) %collective-permute-start.27) | collective-permute-done | bytes 393248 | tf_op jit(solution)/shard_map/ppermute | solution.py:85
  441.0 8.4 %shard_map.327.refs_9_ = bf16[512,2048]{1,0:T(8,128)(2,1)} custom-call(bf16[512,1536]{1,0:T(8,128)(2,1)} %get-tuple-element.106.refs_1_.refs_5_.refs_0_, bf16[1536,2048]{1,0:T(8,128)(2,1)} %refs_1_.1, bf16[128,1024]{1,0:T(8,128)(2,1)} %get-tuple-element.137.refs_2_.refs_1_), custom_call_target="tpu_custom_call" | custom-call | flops 1 | bytes 1 | tf_op jit(solution)/shard_map/pallas_call | solution.py:57
  449.5 6.8 collective-permute-done.31.refs_8_
  457.1 7.2 %shard_map.328 = (bf16[1536,1024]{1,0:T(8,128)(2,1)}, f32[1536,2048]{1,0:T(8,128)}) custom-call(s32[2,8]{1,0:T(2,128)S(1)} %get-tuple-element.205.refs_0_, bf16[192,1024]{1,0:T(8,128)(2,1)} %get-tuple-element.127.refs_5_.refs_1_, bf16[192,1024]{1,0:T(8,128)(2,1)} %copy-done.44, bf16[192,1024]{1,0:T(8,128)(2,1)} %copy-done.43, bf16[192,1024]{1,0:T(8,128)(2,1)} %copy-done.47, ...), custom_call_target="tpu_custom_call" | custom-call | flops 1 | bytes 1 | tf_op jit(solution)/shard_map/pallas_call | solution.py:57
  465.5 7.8 %shard_map.329 = (bf16[512,1024]{1,0:T(8,128)(2,1)}, bf16[512,2048]{1,0:T(8,128)(2,1)}, f32[1,128]{1,0:T(1,128)S(1)}) custom-call(bf16[2,2,256,256]{3,2,1,0:T(8,128)(2,1)} %get-tuple-element.188.refs_0_, bf16[2,2,256,256]{3,2,1,0:T(8,128)(2,1)} %copy-done.37, bf16[2,2,256,256]{3,2,1,0:T(8,128)(2,1)} %copy-done.36, bf16[2,2,256,256]{3,2,1,0:T(8,128)(2,1)} %copy-done.35, ...), custom_call_target="tpu_custom_call" | custom-call | flops 1 | bytes 1 | tf_op jit(solution)/shard_map/pallas_call | solution.py:57
  477.5 6.3 collective-permute-done.34.refs_4_
  484.8 15.9 %collective-permute-done.33.refs_2_ = bf16[128,1024]{1,0:T(8,128)(2,1)S(1)} collective-permute-done((bf16[128,1024]{1,0:T(8,128)(2,1)}, bf16[128,1024]{1,0:T(8,128)(2,1)S(1)}, u32[]{:S(2)}, u32[]{:S(2)}) %collective-permute-start.33) | collective-permute-done | bytes 262176 | tf_op jit(solution)/shard_map/ppermute | solution.py:85
  514.8 13.1 %collective-permute-done.39.refs_3_ = bf16[64,1024]{1,0:T(8,128)(2,1)S(1)} collective-permute-done((bf16[64,1024]{1,0:T(8,128)(2,1)S(1)}, bf16[64,1024]{1,0:T(8,128)(2,1)S(1)}, u32[]{:S(2)}, u32[]{:S(2)}) %collective-permute-start.39) | collective-permute-done | bytes 131104 | tf_op jit(solution)/shard_map/ppermute | solution.py:85
  539.6 7.2 %shard_map.334.refs_5_ = f32[1536,2048]{1,0:T(8,128)} custom-call(s32[2,8]{1,0:T(2,128)S(1)} %get-tuple-element.204.refs_0_, bf16[1536,1024]{1,0:T(8,128)(2,1)} %copy-done.12, f32[1536,2048]{1,0:T(8,128)} %get-tuple-element.153.refs_2_, bf16[64,1024]{1,0:T(8,128)(2,1)} %get-tuple-element.157.refs_3_.refs_1_), custom_call_target="tpu_custom_call", output_to_operand_aliasing={{}: (2, {})} | custom-call | flops 1 | bytes 1 | tf_op jit(solution)/shard_map/pallas_call | solution.py:57
  551.7 17.1 %collective-permute-done.41.refs_3_ = bf16[128,1024]{1,0:T(8,128)(2,1)S(1)} collective-permute-done((bf16[128,1024]{1,0:T(8,128)(2,1)}, bf16[128,1024]{1,0:T(8,128)(2,1)S(1)}, u32[]{:S(2)}, u32[]{:S(2)}) %collective-permute-start.41) | collective-permute-done | bytes 262176 | tf_op jit(solution)/shard_map/ppermute | solution.py:85
  581.5 10.3 %shard_map.338 = (bf16[2,1024,1536]{2,1,0:T(8,128)(2,1)}, f32[2048,1536]{1,0:T(8,128)}, f32[2048,1536]{1,0:T(8,128)}) custom-call(s32[2,8]{1,0:T(2,128)S(1)} %stack.38.refs_0_, bf16[2,128,1536]{2,1,0:T(8,128)(2,1)} %get-tuple-element.135.refs_5_.refs_1_, bf16[2,128,1536]{2,1,0:T(8,128)(2,1)} %collective-permute-done.59.refs_2_, ...), custom_call_target="tpu_custom_call" | custom-call | flops 1 | bytes 1 | tf_op jit(solution)/shard_map/pallas_call | solution.py:57
  623.4 9.3 %shard_map.340 = (f32[2048,1536]{1,0:T(8,128)}, f32[2048,1536]{1,0:T(8,128)}) custom-call(s32[2,8]{1,0:T(2,128)S(1)} %stack.37.refs_0_, bf16[2,1024,1536]{2,1,0:T(8,128)(2,1)} %collective-permute-done.66.refs_1_, f32[2048,1536]{1,0:T(8,128)} %get-tuple-element.174.refs_2_, ...), custom_call_target="tpu_custom_call", output_to_operand_aliasing={{0}: (2, {}), {1}: (3, {})} | custom-call | flops 1 | bytes 1 | tf_op jit(solution)/shard_map/pallas_call | solution.py:57
  633.7 6.0 shard_map.341.refs_9_
  641.3 6.1 shard_map.342
  667.5 6.6 shard_map.343
  (360 shorter events, 189.1 us)
Async XLA Ops:
  7.2 51.7 %all-gather.5.cloned.1.call-start = ((), (), s32[]{:S(2)}) async-start(), calls=%async_computation.4 | async-start | bytes 2621440 | tf_op jit(solution)/shard_map/all_gather | solution.py:90
  9.3 105.6 %all-gather.7.cloned.1.call-start = ((), (), s32[]{:S(2)}) async-start(), calls=%async_computation.6 | async-start | bytes 2621440 | tf_op jit(solution)/shard_map/all_gather | solution.py:90
  70.1 93.1 %reduce-scatter.5.cloned.1.call-start = ((), (), s32[]{:S(2)}) async-start(), calls=%async_computation.5 | async-start | bytes 2621440 | tf_op jit(solution)/shard_map/reduce_scatter | solution.py:95
  112.7 98.6 %all-gather.9.cloned.1.call-start = ((), (), s32[]{:S(2)}) async-start(), calls=%async_computation.7 | async-start | bytes 2621440 | tf_op jit(solution)/shard_map/all_gather | solution.py:90
  165.9 134.2 %reduce-scatter.7.cloned.1.call-start = ((), (), s32[]{:S(2)}) async-start(), calls=%async_computation.8 | async-start | bytes 2621440 | tf_op jit(solution)/shard_map/reduce_scatter | solution.py:95
  248.3 111.2 %all-gather.11.cloned.1.call-start = ((), (), s32[]{:S(2)}) async-start(), calls=%async_computation.9 | async-start | bytes 2621440 | tf_op jit(solution)/shard_map/all_gather | solution.py:90
  265.3 29.8 %collective-permute-start.14 = (bf16[384,1024]{1,0:T(8,128)(2,1)}, bf16[384,1024]{1,0:T(8,128)(2,1)S(1)}, u32[]{:S(2)}, u32[]{:S(2)}) collective-permute-start(bf16[384,1024]{1,0:T(8,128)(2,1)} %get-tuple-element.115), channel_id=1, source_target_pairs={{0,16},{4,20},{8,24},{12,28},{16,0},{20,4},{24,8},{28,12},{1,17},{... | collective-permute-start | bytes 2359304 | tf_op jit(solution)/shard_map/ppermute | solution.py:85
  266.8 28.4 %collective-permute-start.13 = (bf16[384,1024]{1,0:T(8,128)(2,1)}, bf16[384,1024]{1,0:T(8,128)(2,1)S(1)}, u32[]{:S(2)}, u32[]{:S(2)}) collective-permute-start(bf16[384,1024]{1,0:T(8,128)(2,1)} %get-tuple-element.111.refs_5_), channel_id=1, source_target_pairs={{0,8},{4,12},{8,0},{12,4},{16,24},{20,28},{24,16},{28,20},{1,9},{5... | collective-permute-start | bytes 2359304 | tf_op jit(solution)/shard_map/ppermute | solution.py:85
  303.8 273.7 %reduce-scatter.11.cloned.1.call-start = ((), (), s32[]{:S(2)}) async-start(), calls=%async_computation.11 | async-start | bytes 2621440 | tf_op jit(solution)/shard_map/reduce_scatter | solution.py:95
  304.1 48.4 %collective-permute-start.16 = (bf16[2,256,1536]{2,1,0:T(8,128)(2,1)}, bf16[2,256,1536]{2,1,0:T(8,128)(2,1)S(1)}, u32[]{:S(2)}, u32[]{:S(2)}) collective-permute-start(bf16[2,256,1536]{2,1,0:T(8,128)(2,1)} %get-tuple-element.122), channel_id=1, source_target_pairs={{0,16},{4,20},{8,24},{12,28},{16,0},{20,4},{24,8},{28,12},{1,17},{... | collective-permute-start | bytes 4718600 | tf_op jit(solution)/shard_map/ppermute | solution.py:85
  305.1 47.3 %collective-permute-start.15 = (bf16[2,256,1536]{2,1,0:T(8,128)(2,1)S(1)}, bf16[2,256,1536]{2,1,0:T(8,128)(2,1)S(1)}, u32[]{:S(2)}, u32[]{:S(2)}) collective-permute-start(bf16[2,256,1536]{2,1,0:T(8,128)(2,1)S(1)} %copy-done.20), channel_id=1, source_target_pairs={{0,8},{4,12},{8,0},{12,4},{16,24},{20,28},{24,16},{28,20},{1,9},{5... | collective-permute-start | bytes 4718600 | tf_op jit(solution)/shard_map/ppermute | solution.py:85
  305.2 43.9 %collective-permute-start.18 = (bf16[192,1024]{1,0:T(8,128)(2,1)S(1)}, bf16[192,1024]{1,0:T(8,128)(2,1)S(1)}, u32[]{:S(2)}, u32[]{:S(2)}) collective-permute-start(bf16[192,1024]{1,0:T(8,128)(2,1)S(1)} %copy-done.73), channel_id=1, source_target_pairs={{0,8},{4,12},{8,0},{12,4},{16,24},{20,28},{24,16},{28,20},{1,9},{5... | collective-permute-start | bytes 1179656 | tf_op jit(solution)/shard_map/ppermute | solution.py:85
  307.1 42.0 %collective-permute-start.17 = (bf16[192,1024]{1,0:T(8,128)(2,1)S(1)}, bf16[192,1024]{1,0:T(8,128)(2,1)S(1)}, u32[]{:S(2)}, u32[]{:S(2)}) collective-permute-start(bf16[192,1024]{1,0:T(8,128)(2,1)S(1)} %copy-done.46), channel_id=1, source_target_pairs={{0,16},{4,20},{8,24},{12,28},{16,0},{20,4},{24,8},{28,12},{1,17},{... | collective-permute-start | bytes 1179656 | tf_op jit(solution)/shard_map/ppermute | solution.py:85
  385.9 40.5 %collective-permute-start.19 = (bf16[512,1024]{1,0:T(8,128)(2,1)}, bf16[512,1024]{1,0:T(8,128)(2,1)S(1)}, u32[]{:S(2)}, u32[]{:S(2)}) collective-permute-start(bf16[512,1024]{1,0:T(8,128)(2,1)} %get-tuple-element.130), channel_id=1, source_target_pairs={{0,4},{4,0},{8,12},{12,8},{16,20},{20,16},{24,28},{28,24},{1,5},{5... | collective-permute-start | bytes 3145736 | tf_op jit(solution)/shard_map/ppermute | solution.py:85
  386.8 38.3 %collective-permute-start.21 = (bf16[2,128,1536]{2,1,0:T(8,128)(2,1)S(1)}, bf16[2,128,1536]{2,1,0:T(8,128)(2,1)S(1)}, u32[]{:S(2)}, u32[]{:S(2)}) collective-permute-start(bf16[2,128,1536]{2,1,0:T(8,128)(2,1)S(1)} %copy-done.72), channel_id=1, source_target_pairs={{0,8},{4,12},{8,0},{12,4},{16,24},{20,28},{24,16},{28,20},{1,9},{5... | collective-permute-start | bytes 2359304 | tf_op jit(solution)/shard_map/ppermute | solution.py:85
  395.6 30.6 %collective-permute-start.20 = (bf16[2,128,1536]{2,1,0:T(8,128)(2,1)S(1)}, bf16[2,128,1536]{2,1,0:T(8,128)(2,1)S(1)}, u32[]{:S(2)}, u32[]{:S(2)}) collective-permute-start(bf16[2,128,1536]{2,1,0:T(8,128)(2,1)S(1)} %copy-done.26), channel_id=1, source_target_pairs={{0,16},{4,20},{8,24},{12,28},{16,0},{20,4},{24,8},{28,12},{1,17},{... | collective-permute-start | bytes 2359304 | tf_op jit(solution)/shard_map/ppermute | solution.py:85
  422.7 41.6 %collective-permute-start.25 = (bf16[2,2,256,256]{3,2,1,0:T(8,128)(2,1)S(1)}, bf16[2,2,256,256]{3,2,1,0:T(8,128)(2,1)S(1)}, u32[]{:S(2)}, u32[]{:S(2)}) collective-permute-start(bf16[2,2,256,256]{3,2,1,0:T(8,128)(2,1)S(1)} %get-tuple-element.185), channel_id=1, source_target_pairs={{0,24},{4,28},{8,16},{12,20},{16,8},{20,12},{24,0},{28,4},{1,25},{... | collective-permute-start | bytes 1572872 | tf_op jit(solution)/shard_map/ppermute | solution.py:85
  423.3 41.0 %collective-permute-start.24 = (bf16[2,2,256,256]{3,2,1,0:T(8,128)(2,1)S(1)}, bf16[2,2,256,256]{3,2,1,0:T(8,128)(2,1)S(1)}, u32[]{:S(2)}, u32[]{:S(2)}) collective-permute-start(bf16[2,2,256,256]{3,2,1,0:T(8,128)(2,1)S(1)} %get-tuple-element.186), channel_id=1, source_target_pairs={{0,16},{4,20},{8,24},{12,28},{16,0},{20,4},{24,8},{28,12},{1,17},{... | collective-permute-start | bytes 1572872 | tf_op jit(solution)/shard_map/ppermute | solution.py:85
  425.1 39.3 %collective-permute-start.23 = (bf16[2,2,256,256]{3,2,1,0:T(8,128)(2,1)S(1)}, bf16[2,2,256,256]{3,2,1,0:T(8,128)(2,1)S(1)}, u32[]{:S(2)}, u32[]{:S(2)}) collective-permute-start(bf16[2,2,256,256]{3,2,1,0:T(8,128)(2,1)S(1)} %get-tuple-element.187), channel_id=1, source_target_pairs={{0,8},{4,12},{8,0},{12,4},{16,24},{20,28},{24,16},{28,20},{1,9},{5... | collective-permute-start | bytes 1572872 | tf_op jit(solution)/shard_map/ppermute | solution.py:85
  426.2 30.0 %collective-permute-start.31 = (bf16[192,1024]{1,0:T(8,128)(2,1)S(1)}, bf16[192,1024]{1,0:T(8,128)(2,1)S(1)}, u32[]{:S(2)}, u32[]{:S(2)}) collective-permute-start(bf16[192,1024]{1,0:T(8,128)(2,1)S(1)} %collective-permute-done.29.refs_6_), channel_id=1, source_target_pairs={{0,16},{4,20},{8,24},{12,28},{16,0},{20,4},{24,8},{28,12},{1,17},{... | collective-permute-start | bytes 1179656 | tf_op jit(solution)/shard_map/ppermute | solution.py:85
  426.4 29.9 %collective-permute-start.28 = (bf16[192,1024]{1,0:T(8,128)(2,1)S(1)}, bf16[192,1024]{1,0:T(8,128)(2,1)S(1)}, u32[]{:S(2)}, u32[]{:S(2)}) collective-permute-start(bf16[192,1024]{1,0:T(8,128)(2,1)S(1)} %collective-permute-done.26.refs_2_), channel_id=1, source_target_pairs={{0,8},{4,12},{8,0},{12,4},{16,24},{20,28},{24,16},{28,20},{1,9},{5... | collective-permute-start | bytes 1179656 | tf_op jit(solution)/shard_map/ppermute | solution.py:85
  473.3 188.9 %reduce-scatter.9.cloned.1.call-start = ((), (), s32[]{:S(2)}) async-start(), calls=%async_computation.10 | async-start | bytes 2621440 | tf_op jit(solution)/shard_map/reduce_scatter | solution.py:95
  473.3 57.6 %collective-permute-start.37 = (bf16[1536,1024]{1,0:T(8,128)(2,1)}, bf16[1536,1024]{1,0:T(8,128)(2,1)S(1)}, u32[]{:S(2)}, u32[]{:S(2)}) collective-permute-start(bf16[1536,1024]{1,0:T(8,128)(2,1)} %get-tuple-element.142.refs_12_), channel_id=1, source_target_pairs={{0,4},{4,0},{8,12},{12,8},{16,20},{20,16},{24,28},{28,24},{1,5},{5... | collective-permute-start | bytes 9437192 | tf_op jit(solution)/shard_map/ppermute | solution.py:85
  474.5 29.6 %collective-permute-start.32 = (bf16[512,1024]{1,0:T(8,128)(2,1)S(1)}, bf16[512,1024]{1,0:T(8,128)(2,1)S(1)}, u32[]{:S(2)}, u32[]{:S(2)}) collective-permute-start(bf16[512,1024]{1,0:T(8,128)(2,1)S(1)} %copy-done.3), channel_id=1, source_target_pairs={{0,4},{4,0},{8,12},{12,8},{16,20},{20,16},{24,28},{28,24},{1,5},{5... | collective-permute-start | bytes 3145736 | tf_op jit(solution)/shard_map/ppermute | solution.py:85
  475.4 37.5 %collective-permute-start.62 = (bf16[2,128,1536]{2,1,0:T(8,128)(2,1)S(1)}, bf16[2,128,1536]{2,1,0:T(8,128)(2,1)S(1)}, u32[]{:S(2)}, u32[]{:S(2)}) collective-permute-start(bf16[2,128,1536]{2,1,0:T(8,128)(2,1)S(1)} %copy-done.31), channel_id=1, source_target_pairs={{0,8},{4,12},{8,0},{12,4},{16,24},{20,28},{24,16},{28,20},{1,9},{5... | collective-permute-start | bytes 2359304 | tf_op jit(solution)/shard_map/ppermute | solution.py:85
  476.4 37.5 %collective-permute-start.59 = (bf16[2,128,1536]{2,1,0:T(8,128)(2,1)S(1)}, bf16[2,128,1536]{2,1,0:T(8,128)(2,1)}, u32[]{:S(2)}, u32[]{:S(2)}) collective-permute-start(bf16[2,128,1536]{2,1,0:T(8,128)(2,1)S(1)} %copy-done.11), channel_id=1, source_target_pairs={{0,16},{4,20},{8,24},{12,28},{16,0},{20,4},{24,8},{28,12},{1,17},{... | collective-permute-start | bytes 2359304 | tf_op jit(solution)/shard_map/ppermute | solution.py:85
  511.9 34.9 %collective-permute-start.35 = (bf16[256,1024]{1,0:T(8,128)(2,1)}, bf16[256,1024]{1,0:T(8,128)(2,1)S(1)}, u32[]{:S(2)}, u32[]{:S(2)}) collective-permute-start(bf16[256,1024]{1,0:T(8,128)(2,1)} %get-tuple-element.149.refs_5_), channel_id=1, source_target_pairs={{0,8},{4,12},{8,0},{12,4},{16,24},{20,28},{24,16},{28,20},{1,9},{5... | collective-permute-start | bytes 1572872 | tf_op jit(solution)/shard_map/ppermute | solution.py:85
  527.9 52.7 %collective-permute-start.63 = (bf16[2,128,1536]{2,1,0:T(8,128)(2,1)S(1)}, bf16[2,128,1536]{2,1,0:T(8,128)(2,1)S(1)}, u32[]{:S(2)}, u32[]{:S(2)}) collective-permute-start(bf16[2,128,1536]{2,1,0:T(8,128)(2,1)S(1)} %copy-done.31), channel_id=1, source_target_pairs={{0,16},{4,20},{8,24},{12,28},{16,0},{20,4},{24,8},{28,12},{1,17},{... | collective-permute-start | bytes 2359304 | tf_op jit(solution)/shard_map/ppermute | solution.py:85
  528.8 51.8 %collective-permute-start.60 = (bf16[2,128,1536]{2,1,0:T(8,128)(2,1)S(1)}, bf16[2,128,1536]{2,1,0:T(8,128)(2,1)}, u32[]{:S(2)}, u32[]{:S(2)}) collective-permute-start(bf16[2,128,1536]{2,1,0:T(8,128)(2,1)S(1)} %copy-done.11), channel_id=1, source_target_pairs={{0,8},{4,12},{8,0},{12,4},{16,24},{20,28},{24,16},{28,20},{1,9},{5... | collective-permute-start | bytes 2359304 | tf_op jit(solution)/shard_map/ppermute | solution.py:85
  529.9 50.8 %collective-permute-start.64 = (bf16[2,128,1536]{2,1,0:T(8,128)(2,1)S(1)}, bf16[2,128,1536]{2,1,0:T(8,128)(2,1)}, u32[]{:S(2)}, u32[]{:S(2)}) collective-permute-start(bf16[2,128,1536]{2,1,0:T(8,128)(2,1)S(1)} %collective-permute-done.62.refs_6_), channel_id=1, source_target_pairs={{0,16},{4,20},{8,24},{12,28},{16,0},{20,4},{24,8},{28,12},{1,17},{... | collective-permute-start | bytes 2359304 | tf_op jit(solution)/shard_map/ppermute | solution.py:85
  531.0 49.7 %collective-permute-start.61 = (bf16[2,128,1536]{2,1,0:T(8,128)(2,1)}, bf16[2,128,1536]{2,1,0:T(8,128)(2,1)}, u32[]{:S(2)}, u32[]{:S(2)}) collective-permute-start(bf16[2,128,1536]{2,1,0:T(8,128)(2,1)} %collective-permute-done.59.refs_2_), channel_id=1, source_target_pairs={{0,8},{4,12},{8,0},{12,4},{16,24},{20,28},{24,16},{28,20},{1,9},{5... | collective-permute-start | bytes 2359304 | tf_op jit(solution)/shard_map/ppermute | solution.py:85
  591.9 30.6 %collective-permute-start.66 = (bf16[2,1024,1536]{2,1,0:T(8,128)(2,1)}, bf16[2,1024,1536]{2,1,0:T(8,128)(2,1)}, u32[]{:S(2)}, u32[]{:S(2)}) collective-permute-start(bf16[2,1024,1536]{2,1,0:T(8,128)(2,1)} %get-tuple-element.171.refs_9_), channel_id=1, source_target_pairs={{0,4},{4,0},{8,12},{12,8},{16,20},{20,16},{24,28},{28,24},{1,5},{5... | collective-permute-start | bytes 18874376 | tf_op jit(solution)/shard_map/ppermute | solution.py:85
  (119 other events, 1200.0 us)
Sparse Core Ops, SparseCore 0:
  10.2 48.6 all-gather.4
  70.2 44.6 all-gather.6
  117.8 45.4 reduce-scatter.4
  166.0 45.2 all-gather.8
  248.4 42.5 reduce-scatter.6
  303.9 43.1 all-gather.10
  473.4 41.4 reduce-scatter.10
  592.1 42.2 reduce-scatter.8

commit v3 on v2

v3 whole, which is shorter than its diff:
```python
import functools
import math

import jax
import jax.numpy as jnp
from jax import lax
from jax.experimental import pallas as pl
from jax.experimental.pallas import tpu as pltpu
from jax.sharding import PartitionSpec as P

HEAD = 128
EPS = 1e-06
ROPE_BASE = 1000000.0
MASKED = -1e30
LOG2E = math.log2(math.e)
BF = jnp.bfloat16
F32 = jnp.float32
I32 = jnp.int32


def sds(shape, dtype):
    return jax.ShapeDtypeStruct(shape, dtype)


def hbm(shape, dtype):
    return pltpu.HBM(shape, dtype)


def whole(shape):
    return pl.BlockSpec(shape, lambda *_: (0,) * len(shape))


def dot_nn(a, b):
    return lax.dot_general(a, b, (((1,), (0,)), ((), ())), preferred_element_type=F32)


def dot_nt(a, b):
    return lax.dot_general(a, b, (((1,), (1,)), ((), ())), preferred_element_type=F32)


def dot_tn(a, b):
    return lax.dot_general(a, b, (((0,), (0,)), ((), ())), preferred_element_type=F32)


def in_hbm(value):
    return pltpu.with_memory_space_constraint(value, pltpu.HBM)


def call(body, grid, in_specs, out_specs, out_shape, scratch, operands, mib, prefetch=1, after=(), aliases={}):
    after = (*ORDER, *after)
    at, extra = prefetch + len(in_specs), len(after)

    def run(*refs):
        return body(*refs[:at], *refs[at + extra :])

    operands = operands[:prefetch] + tuple(in_hbm(v) for v in operands[prefetch:])
    outs = pl.pallas_call(
        run,
        grid_spec=pltpu.PrefetchScalarGridSpec(
            num_scalar_prefetch=prefetch,
            grid=grid,
            in_specs=in_specs + [pl.BlockSpec(memory_space=pl.ANY)] * extra,
            out_specs=out_specs,
            scratch_shapes=scratch,
        ),
        out_shape=out_shape,
        input_output_aliases=aliases,
        compiler_params=pltpu.CompilerParams(
            vmem_limit_bytes=mib << 20, dimension_semantics=("arbitrary",) * len(grid)
        ),
        cost_estimate=pl.CostEstimate(flops=1, bytes_accessed=1, transcendentals=0),
    )(*operands, *(in_hbm(v) for v in after))
    ORDER[:] = [outs[0]]
    return outs


ORDER = []


def flip(axis, mask):
    return [(i, i ^ mask) for i in range(lax.axis_size(axis))]


def swap(value, axis, mask):
    return lax.ppermute(value, axis, flip(axis, mask))


def gather_tp(share):
    rows, _, width = share.shape
    return lax.all_gather(share, "tp", axis=1, tiled=True).reshape(-1, width)


def scatter_tp(part, row_count):
    part = part.reshape(row_count, -1, part.shape[1])
    return lax.psum_scatter(part, "tp", scatter_dimension=1, tiled=True)


def half_out(x_ref, core, keep_ref, send_ref):
    half = keep_ref.shape[1]
    keep_ref[...] = x_ref[:, pl.ds(pl.multiple_of(core * half, half), half)]
    send_ref[...] = x_ref[:, pl.ds(pl.multiple_of((1 - core) * half, half), half)]


def qkv_kernel(row_count, meta, x, wq, wk, wv, gq, gk, cos, sin, q_out, kv_out, q_raw, k_raw, keep, send, acc_q, acc_k, acc_v):
    j, last = pl.program_id(0), pl.num_programs(0) - 1

    @pl.when(j == 0)
    def _():
        half_out(x, meta[0], keep, send)
        acc_q[...] = jnp.zeros_like(acc_q)
        acc_k[...] = jnp.zeros_like(acc_k)
        acc_v[...] = jnp.zeros_like(acc_v)

    depth = wq.shape[0]
    xs = x[:, pl.ds(pl.multiple_of(j * depth, depth), depth)]
    acc_q[...] += dot_nn(xs, wq[...])
    acc_k[...] += dot_nn(xs, wk[...])
    acc_v[...] += dot_nn(xs, wv[...])

    @pl.when(j == last)
    def _():
        def turn(raw, gain):
            inverse = lax.rsqrt(jnp.mean(raw * raw, axis=-1, keepdims=True) + EPS)
            normed = raw * inverse * gain
            return (normed * cos[...] + pltpu.roll(normed, HEAD // 2, 1) * sin[...]).astype(BF)

        q_raw[...] = acc_q[...]
        k_raw[...] = acc_k[...]
        for h in range(acc_q.shape[1] // HEAD):
            at = slice(h * HEAD, (h + 1) * HEAD)
            q_out[:, at] = turn(acc_q[:, at], gq[...])
        span = kv_out.shape[2]
        for h in range(acc_k.shape[1] // HEAD):
            at = slice(h * HEAD, (h + 1) * HEAD)
            turned = turn(acc_k[:, at], gk[...])
            for r in range(row_count):
                kv_out[r, 0, :, at] = turned[r * span : (r + 1) * span]
        for r in range(row_count):
            kv_out[r, 1] = acc_v[r * span : (r + 1) * span, :].astype(BF)


def qkv_call(meta, row_count, x, weights, gains, tables):
    tokens, width = x.shape
    nq, nk = weights[0].shape[1], weights[1].shape[1]
    depth = width // 4
    row = lambda n: pl.BlockSpec((depth, n), lambda j, *_: (j, 0))
    kv = (row_count, 2, tokens // row_count, nk)
    return call(
        functools.partial(qkv_kernel, row_count),
        (4,),
        [whole((tokens, width)), row(nq), row(nk), row(nk)]
        + [whole((1, HEAD))] * 2
        + [whole((tokens, HEAD))] * 2,
        [whole((tokens, nq)), whole(kv), whole((tokens, nq)), whole((tokens, nk))]
        + [whole((tokens, width // 2))] * 2,
        [hbm((tokens, nq), BF), hbm(kv, BF), hbm((tokens, nq), F32), hbm((tokens, nk), F32)]
        + [hbm((tokens, width // 2), BF)] * 2,
        [pltpu.VMEM((tokens, nq), F32), pltpu.VMEM((tokens, nk), F32), pltpu.VMEM((tokens, nk), F32)],
        (meta, x, *weights, *gains, *tables),
        40,
    )


def stack_heads(ref, group):
    return jnp.concatenate([ref[:, h * HEAD : (h + 1) * HEAD] for h in range(group)], axis=0)


def bounds(meta, at, row, docs, span, group):
    place = meta[at] + lax.broadcasted_iota(I32, (span, 1), 0)
    begin = jnp.zeros_like(place)
    for d in range(docs):
        start = meta[at + 1 + row * docs + d]
        begin = jnp.where(place >= start, start, begin)
    return jnp.concatenate([place] * group, axis=0), jnp.concatenate([begin] * group, axis=0)


def attend_kernel(slot_count, docs, group, scale, meta, *refs):
    q_ref, refs = refs[0], refs[1:]
    keys, refs = refs[:slot_count], refs[slot_count:]
    wo = refs[0]
    o_out, lse_out, part_out = refs[1:4]
    scores, acc = refs[4:]
    r, g, last = pl.program_id(0), pl.program_id(1), pl.num_programs(1) - 1
    first = r * slot_count
    bases = pl.num_programs(0) * slot_count
    span = q_ref.shape[0]
    queries = stack_heads(q_ref, group)
    high, low = bounds(meta, bases + slot_count + 1, r, docs, span, group)
    k_place = lax.broadcasted_iota(I32, (1, span), 1)
    top = jnp.full((group * span, HEAD), MASKED, F32)

    for s in range(slot_count):

        def some(top, s=s):
            raw = dot_nt(queries, keys[s][0, 0]) * scale
            place = k_place + meta[bases + s]
            kept = jnp.where((place >= low) & (place <= high), raw, MASKED)
            scores[s] = kept
            for c in range(span // HEAD):
                top = jnp.maximum(top, kept[:, c * HEAD : (c + 1) * HEAD])
            return top

        top = lax.cond(meta[first + s] > 0, some, lambda t: t, top)

    peak = jnp.max(top, axis=-1, keepdims=True)
    total = jnp.zeros((group * span, HEAD), F32)
    out = jnp.zeros((group * span, HEAD), F32)
    for s in range(slot_count):

        def more(carry, s=s):
            total, out = carry
            power = jnp.exp2(scores[s] - peak)
            for c in range(span // HEAD):
                total = total + power[:, c * HEAD : (c + 1) * HEAD]
            return total, out + dot_nn(power.astype(BF), keys[s][0, 1])

        total, out = lax.cond(meta[first + s] > 0, more, lambda t: t, (total, out))

    total = jnp.sum(total, axis=-1, keepdims=True)
    lse_out[0, 0] = peak + jnp.log2(total)
    out = (out / total).astype(BF)
    out = jnp.concatenate([out[h * span : (h + 1) * span] for h in range(group)], axis=1)
    o_out[...] = out
    part = dot_nn(out, wo[...])

    @pl.when(g == 0)
    def _():
        acc[...] = part

    @pl.when(g > 0)
    def _():
        acc[...] += part

    @pl.when(g == last)
    def _():
        part_out[...] = acc[...].astype(BF)


def attend_call(meta, docs, queries, kv_slots, wo):
    slot_count = len(kv_slots)
    tokens, nq = queries.shape
    row_count, _, span, nk = kv_slots[0].shape
    heads, group = nk // HEAD, nq // nk
    width = wo.shape[1]
    wide = group * HEAD
    rows = pl.BlockSpec((span, wide), lambda r, g, *_: (r, g))
    return call(
        functools.partial(attend_kernel, slot_count, docs, group, HEAD**-0.5 * LOG2E),
        (row_count, heads),
        [rows]
        + [pl.BlockSpec((1, 2, span, HEAD), lambda r, g, *_: (r, 0, 0, g))] * slot_count
        + [pl.BlockSpec((wide, width), lambda r, g, *_: (g, 0))],
        [
            rows,
            pl.BlockSpec((1, 1, group * span, 1), lambda r, g, *_: (r, g, 0, 0)),
            pl.BlockSpec((span, width), lambda r, g, *_: (r, 0)),
        ],
        [hbm((tokens, nq), BF), hbm((row_count, heads, group * span, 1), F32), hbm((tokens, width), BF)],
        [pltpu.VMEM((slot_count, group * span, span), F32), pltpu.VMEM((span, width), F32)],
        (meta, queries, *kv_slots, wo),
        40,
    )


def ff_kernel(meta, x, og, wg, wu, wd, out, keep, send):
    @pl.when(pl.program_id(0) == 0)
    def _():
        half_out(x, meta[0], keep, send)

    gate = dot_nn(x[...], wg[...])
    up = dot_nn(x[...], wu[...])
    upstream = dot_nt(og[...], wd[...])
    sigmoid = 1.0 / (1.0 + jnp.exp(-gate))
    silu = gate * sigmoid
    out[0] = (silu * up).astype(BF)
    out[1] = (upstream * up * sigmoid * (1.0 + gate * (1.0 - sigmoid))).astype(BF)
    out[2] = (upstream * silu).astype(BF)


def ff_call(meta, x, og, wg, wu, wd, after):
    tokens, width = x.shape
    hidden = wg.shape[1]
    block = 256
    column = pl.BlockSpec((width, block), lambda j, *_: (0, j))
    return call(
        ff_kernel,
        (hidden // block,),
        [whole((tokens, width))] * 2 + [column, column, pl.BlockSpec((block, width), lambda j, *_: (j, 0))],
        [pl.BlockSpec((3, tokens, block), lambda j, *_: (0, 0, j))] + [whole((tokens, width // 2))] * 2,
        [hbm((3, tokens, hidden), BF)] + [hbm((tokens, width // 2), BF)] * 2,
        [],
        (meta, x, og, wg, wu, wd),
        48,
        after=after,
    )


def ff_back_kernel(gate, up, wg, wu, out):
    out[...] = (dot_nt(gate[0], wg[...]) + dot_nt(up[0], wu[...])).astype(BF)


def ff_back_call(planes, wg, wu):
    _, tokens, hidden = planes.shape
    width = wg.shape[0]
    block = 512
    row = pl.BlockSpec((block, hidden), lambda j: (j, 0))
    plane = lambda n: pl.BlockSpec((1, tokens, hidden), lambda j: (n, 0, 0))
    return call(
        ff_back_kernel,
        (width // block,),
        [plane(1), plane(2), row, row],
        [pl.BlockSpec((tokens, block), lambda j: (0, j))],
        [hbm((tokens, width), BF)],
        [],
        (planes, planes, wg, wu),
        40,
        prefetch=0,
    )[0]


def ff_out_kernel(hm, wd, out):
    out[...] = dot_nn(hm[0], wd[...]).astype(BF)


def ff_out_call(planes, wd):
    _, tokens, hidden = planes.shape
    width = wd.shape[1]
    block = 512
    return call(
        ff_out_kernel,
        (width // block,),
        [pl.BlockSpec((1, tokens, hidden), lambda j: (0, 0, 0)), pl.BlockSpec((hidden, block), lambda j: (0, j))],
        [pl.BlockSpec((tokens, block), lambda j: (0, j))],
        [hbm((tokens, width), BF)],
        [],
        (planes, wd),
        32,
        prefetch=0,
    )[0]


def norm_back(turned, raw, gain, cos, sin):
    upstream = turned * cos - pltpu.roll(turned, HEAD // 2, 1) * sin
    inverse = lax.rsqrt(jnp.mean(raw * raw, axis=-1, keepdims=True) + EPS)
    scaled = upstream * gain
    through = inverse * scaled - raw * (inverse * inverse * inverse) * jnp.mean(
        raw * scaled, axis=-1, keepdims=True
    )
    return through.astype(BF), jnp.sum(upstream * raw * inverse, axis=0, keepdims=True)


def attend_back_kernel(slot_count, docs, group, scale, meta, *refs):
    bg, wo, q_ref, refs = refs[0], refs[1], refs[2], refs[3:]
    keys, refs = refs[:slot_count], refs[slot_count:]
    o_ref, lse_ref, q_raw, gq, cos, sin = refs[:6]
    dq_out, even_out, odd_low, odd_high, gain_out, keep, send = refs[6:]
    r, g = pl.program_id(0), pl.program_id(1)
    first = r * slot_count
    bases = pl.num_programs(0) * slot_count

    @pl.when(g == 0)
    def _():
        half_out(bg, meta[bases + slot_count], keep, send)

    @pl.when((r == 0) & (g == 0))
    def _():
        gain_out[...] = jnp.zeros_like(gain_out)

    span = q_ref.shape[0]
    d_out = dot_nt(bg[...], wo[...]).astype(BF)
    d_out = jnp.concatenate([d_out[:, h * HEAD : (h + 1) * HEAD] for h in range(group)], axis=0)
    o_rows = stack_heads(o_ref, group)
    queries = stack_heads(q_ref, group)
    centre = jnp.sum(d_out.astype(F32) * o_rows.astype(F32), axis=-1, keepdims=True)
    lse = lse_ref[0, 0]
    high, low = bounds(meta, bases + slot_count + 1, r, docs, span, group)
    k_place = lax.broadcasted_iota(I32, (1, span), 1)
    dq = jnp.zeros((group * span, HEAD), F32)
    for s in range(slot_count):
        half = slot_count // 4
        if s % 2 == 0:
            out = even_out.at[s // 2, 0]
        else:
            out = (odd_low if s // 2 < half else odd_high).at[s // 2 % half, 0]

        def some(dq, s=s, out=out):
            raw = dot_nt(queries, keys[s][0, 0]) * (scale * LOG2E)
            place = k_place + meta[bases + s]
            probs = jnp.where((place >= low) & (place <= high), jnp.exp2(raw - lse), 0.0)
            d_probs = dot_nt(d_out, keys[s][0, 1])
            d_score = (probs * (d_probs - centre)).astype(BF)
            out[0] = (dot_tn(d_score, queries) * scale).astype(BF)
            out[1] = dot_tn(probs.astype(BF), d_out).astype(BF)
            return dq + dot_nn(d_score, keys[s][0, 0])

        def none(dq, out=out):
            out[...] = jnp.zeros(out.shape, BF)
            return dq

        dq = lax.cond(meta[first + s] > 0, some, none, dq)

    gain = gq[...]
    gain_total = jnp.zeros((1, HEAD), F32)
    for h in range(group):
        rows = dq[h * span : (h + 1) * span] * scale
        d_raw, part = norm_back(rows, q_raw[:, h * HEAD : (h + 1) * HEAD], gain, cos[...], sin[...])
        dq_out[:, h * HEAD : (h + 1) * HEAD] = d_raw
        gain_total = gain_total + part
    gain_out[...] += gain_total


def attend_back_call(meta, docs, bg, wo, queries, kv_slots, attended, lse, q_raw, gq, tables, after):
    slot_count = len(kv_slots)
    tokens, width = bg.shape
    nq = queries.shape[1]
    row_count, _, span, nk = kv_slots[0].shape
    heads, group = nk // HEAD, nq // nk
    wide = group * HEAD
    rows = pl.BlockSpec((span, wide), lambda r, g, *_: (r, g))
    by_row = lambda n: pl.BlockSpec((span, n), lambda r, g, *_: (r, 0))
    kv_out = lambda n: pl.BlockSpec((n, 1, 2, span, HEAD), lambda r, g, *_: (0, r, 0, 0, g))
    kv_shape = lambda n: hbm((n, row_count, 2, span, nk), BF)
    half, quarter = slot_count // 2, slot_count // 4
    return call(
        functools.partial(attend_back_kernel, slot_count, docs, group, HEAD**-0.5),
        (row_count, heads),
        [by_row(width), pl.BlockSpec((wide, width), lambda r, g, *_: (g, 0)), rows]
        + [pl.BlockSpec((1, 2, span, HEAD), lambda r, g, *_: (r, 0, 0, g))] * slot_count
        + [rows, pl.BlockSpec((1, 1, group * span, 1), lambda r, g, *_: (r, g, 0, 0))]
        + [rows, whole((1, HEAD)), by_row(HEAD), by_row(HEAD)],
        [rows, kv_out(half), kv_out(quarter), kv_out(quarter), whole((1, HEAD)), by_row(width // 2), by_row(width // 2)],
        [
            hbm((tokens, nq), BF),
            kv_shape(half),
            kv_shape(quarter),
            kv_shape(quarter),
            sds((1, HEAD), F32),
            hbm((tokens, width // 2), BF),
            hbm((tokens, width // 2), BF),
        ],
        [],
        (meta, bg, wo, queries, *kv_slots, attended, lse, q_raw, gq, *tables),
        40,
        after=after,
    )


def key_back_kernel(count, row_count, *refs):
    pieces, refs = refs[:count], refs[count:]
    dq_ref, k_raw, gk, cos, sin, all_out, gain_out = refs
    span, nk = pieces[0].shape[2:]
    nq = dq_ref.shape[1]
    all_out[:, :nq] = dq_ref[...]
    gain_total = jnp.zeros((1, HEAD), F32)
    for r in range(row_count):
        rows = slice(r * span, (r + 1) * span)
        for h in range(nk // HEAD):
            at = slice(h * HEAD, (h + 1) * HEAD)
            turned = sum(p[r, 0, :, at].astype(F32) for p in pieces)
            d_raw, part = norm_back(turned, k_raw[rows, at], gk[...], cos[rows], sin[rows])
            all_out[rows, nq + h * HEAD : nq + (h + 1) * HEAD] = d_raw
            gain_total = gain_total + part
        all_out[rows, nq + nk :] = sum(p[r, 1].astype(F32) for p in pieces).astype(BF)
    gain_out[...] = gain_total


def key_back_call(pieces, dq, k_raw, gk, tables, after):
    tokens, nq = dq.shape
    nk = k_raw.shape[1]
    return call(
        functools.partial(key_back_kernel, len(pieces), pieces[0].shape[0]),
        (1,),
        [whole(pieces[0].shape)] * len(pieces)
        + [whole((tokens, nq)), whole((tokens, nk)), whole((1, HEAD)), whole((tokens, HEAD)), whole((tokens, HEAD))],
        [whole((tokens, nq + 2 * nk)), whole((1, HEAD))],
        [hbm((tokens, nq + 2 * nk), BF), hbm((1, HEAD), F32)],
        [],
        (*pieces, dq, k_raw, gk, *tables),
        40,
        prefetch=0,
        after=after,
    )


def back_kernel(grads, wq, wk, wv, out):
    nq, nk = wq.shape[1], wk.shape[1]
    part = (
        dot_nt(grads[:, :nq], wq[...])
        + dot_nt(grads[:, nq : nq + nk], wk[...])
        + dot_nt(grads[:, nq + nk :], wv[...])
    )
    out[...] = part.astype(BF)


def back_call(grads, weights):
    tokens, cols = grads.shape
    width = weights[0].shape[0]
    block = width // 4
    return call(
        back_kernel,
        (4,),
        [whole((tokens, cols))] + [pl.BlockSpec((block, w.shape[1]), lambda j: (j, 0)) for w in weights],
        [pl.BlockSpec((tokens, block), lambda j: (0, j))],
        [hbm((tokens, width), BF)],
        [],
        (grads, *weights),
        40,
        prefetch=0,
    )[0]


def turn_rows(ids, parts, left_refs, turned):
    tokens, rows = left_refs[0].shape
    part = turned.shape[0] // parts
    for k, ref in enumerate(left_refs):
        for n in range(parts):
            block = ref[:, pl.ds(pl.multiple_of(ids[n] * part, HEAD), part)]
            turned[n * part : (n + 1) * part, k * tokens : (k + 1) * tokens] = block.T


def put_rows(total, outs, at):
    part = total.shape[0] // len(outs)
    for n, out in enumerate(outs):
        out[at] = total[n * part : (n + 1) * part].astype(BF)


def ff_grad_kernel(ids, og0, og1, x0, x1, p0, p1, *refs):
    outs, turned = refs[:-1], refs[-1]

    @pl.when(pl.program_id(0) == 0)
    def _():
        turn_rows(ids, len(outs), (og0, og1), turned.at[0])
        turn_rows(ids, len(outs), (x0, x1), turned.at[1])

    for n in range(3):
        right = jnp.concatenate([p0[n], p1[n]], axis=0)
        put_rows(dot_nn(turned[min(n, 1)], right), outs, n)


def ff_grad_call(ids, ogs, xs, planes):
    tokens, rows = xs[0].shape
    hidden = planes[0].shape[2]
    wide = next(w for w in (512, 384, 256, 128) if hidden % w == 0)
    part = rows // 4
    count = ids.shape[0]
    return call(
        ff_grad_kernel,
        (hidden // wide,),
        [whole((tokens, rows))] * 4 + [pl.BlockSpec((3, tokens, wide), lambda c, ids: (0, 0, c))] * 2,
        [pl.BlockSpec((3, part, wide), lambda c, ids: (0, 0, c))] * count,
        [hbm((3, part, hidden), BF)] * count,
        [pltpu.VMEM((2, count * part, 2 * tokens), BF)],
        (ids, *ogs, *xs, *planes),
        48,
    )


def attn_grad_kernel(steps, ids, x0, x1, b0, b1, g0, g1, o0, o1, *refs):
    outs, turned = refs[:-1], refs[-1]
    c = pl.program_id(0)

    @pl.when(c == 0)
    def _():
        turn_rows(ids, len(outs), (x0, x1), turned)

    @pl.when(c == steps)
    def _():
        turn_rows(ids, len(outs), (b0, b1), turned)

    @pl.when(c < steps)
    def _():
        put_rows(dot_nn(turned[...], jnp.concatenate([g0[...], g1[...]], axis=0)), outs, 0)

    @pl.when(c >= steps)
    def _():
        put_rows(dot_nn(turned[...], jnp.concatenate([o0[...], o1[...]], axis=0)), outs, 0)


def attn_grad_call(ids, xs, bs, grads, outs):
    tokens, rows = xs[0].shape
    wide = outs[0].shape[1] if grads[0].shape[1] % outs[0].shape[1] == 0 else HEAD
    steps = grads[0].shape[1] // wide
    more = outs[0].shape[1] // wide
    part = rows // 4
    count = ids.shape[0]
    cols = (steps + more) * wide
    return call(
        functools.partial(attn_grad_kernel, steps),
        (steps + more,),
        [whole((tokens, rows))] * 4
        + [pl.BlockSpec((tokens, wide), lambda c, ids: (0, jnp.minimum(c, steps - 1)))] * 2
        + [pl.BlockSpec((tokens, wide), lambda c, ids: (0, jnp.maximum(c - steps, 0)))] * 2,
        [pl.BlockSpec((1, part, wide), lambda c, ids: (0, 0, c))] * count,
        [hbm((1, part, cols), BF)] * count,
        [pltpu.VMEM((count * part, 2 * tokens), BF)],
        (ids, *xs, *bs, *grads, *outs),
        48,
    )


def split_kernel(bits, keep_a, got_a, keep_b, got_b, send_a, next_a, send_b, next_b):
    j = pl.program_id(0)

    def put(out, keep, got):
        out[...] = (keep[...].astype(F32) + got[...].astype(F32)).astype(BF)

    @pl.when(j == 0)
    def _():
        put(send_a, keep_a, got_a)
        put(send_b, keep_b, got_b)

    @pl.when(j == 1)
    def _():
        put(next_a, keep_a, got_a)
        put(next_b, keep_b, got_b)


def split_call(bits, keeps, gots, after):
    *lead, rows, cols = keeps[0].shape
    zeros = (0,) * len(lead)
    half = (*lead, rows // 2, cols)
    part = lambda f: pl.BlockSpec(half, lambda j, bits: (*zeros, jnp.where(j == 0, 1 - bits[f], bits[f]), 0))
    send_a, next_a, send_b, next_b = call(
        split_kernel,
        (2,),
        [part(0), part(0), part(1), part(1)],
        [whole(half)] * 4,
        [hbm(half, BF)] * 4,
        [],
        (bits, keeps[0], gots[0], keeps[1], gots[1]),
        40,
        after=after,
    )
    return (send_a, send_b), (next_a, next_b)


def sum_kernel(bits, *refs):
    count = (len(refs) - 2) // 2
    for f, out in enumerate(refs[2 * count :]):
        total = refs[f * count][...].astype(F32)
        for ref in refs[f * count + 1 : (f + 1) * count]:
            total = total + ref[...].astype(F32)
        out[...] = total.astype(BF)


def sum_call(bits, flows, after=()):
    rows = min(v.shape[1] for v in flows[0])
    planes, _, cols = flows[0][0].shape
    block = (planes, rows // 2, cols)

    def part(v, f):
        long = v.shape[1] > rows
        return pl.BlockSpec(block, lambda j, bits: (0, j + (2 * bits[f] if long else 0), 0))

    return call(
        sum_kernel,
        (2,),
        [part(v, f) for f, vs in enumerate(flows) for v in vs],
        [pl.BlockSpec(block, lambda j, bits: (0, j, 0))] * 2,
        [hbm((planes, rows, cols), BF)] * 2,
        [],
        (bits, *flows[0], *flows[1]),
        40,
        after=after,
    )


def half_sum_call(bits, keeps, gots):
    planes, rows, cols = keeps[0].shape
    block = (planes, rows // 4, cols)
    part = lambda f: pl.BlockSpec(block, lambda j, bits: (0, j + 2 * bits[f], 0))
    return call(
        sum_kernel,
        (2,),
        [part(0), part(0), part(1), part(1)],
        [pl.BlockSpec(block, lambda j, bits: (0, j, 0))] * 2,
        [hbm((planes, rows // 2, cols), BF)] * 2,
        [],
        (bits, keeps[0], gots[0], keeps[1], gots[1]),
        40,
    )


def widen_kernel(count, planes, turned, table, *refs):
    pieces, outs = refs[: count * planes], refs[count * planes :]

    def put(refs):
        at, plane = 0, 0
        for k, out in enumerate(outs):
            if k in turned:
                wide = out.shape[0]
                out[...] = refs[plane][0, :, at : at + wide].T.astype(F32)
            else:
                wide = out.shape[1]
                out[...] = refs[plane][0, :, at : at + wide].astype(F32)
            at += wide
            if at == refs[plane].shape[2]:
                at, plane = 0, plane + 1

    for k in range(count):

        @pl.when(pl.program_id(0) == k)
        def _(k=k):
            put(pieces[k * planes : (k + 1) * planes])


def widen_call(table, pieces, planes, shapes, turned, after):
    _, rows, cols = pieces[0].shape
    count = len(pieces)
    place = lambda n: pl.BlockSpec((1, rows, cols), lambda j, t: (n, 0, 0), pipeline_mode=pl.Buffered(1))
    by_row = lambda s: pl.BlockSpec((rows, s[1]), lambda j, t: (t[j], 0))
    by_col = lambda s: pl.BlockSpec((s[0], rows), lambda j, t: (0, t[j]))
    return call(
        functools.partial(widen_kernel, count, len(planes), turned),
        (count,),
        [place(n) for _ in range(count) for n in planes],
        [by_col(s) if k in turned else by_row(s) for k, s in enumerate(shapes)],
        [hbm(s, F32) for s in shapes],
        [],
        (table, *(p for p in pieces for _ in planes)),
        56,
        after=after,
    )


def norm_kernel(x, gain, out):
    value = x[...].astype(F32)
    inverse = lax.rsqrt(jnp.mean(value * value, axis=-1, keepdims=True) + EPS)
    out[...] = (value * inverse * gain[...]).astype(BF)


def norm_call(x, gain):
    return call(
        norm_kernel,
        (1,),
        [whole(x.shape), whole(gain.shape)],
        [whole(x.shape)],
        [hbm(x.shape, BF)],
        [],
        (x, gain),
        24,
        prefetch=0,
    )[0]


def middle_kernel(x, got, gain, middle, out):
    value = x[...].astype(F32) + got[...].astype(F32)
    inverse = lax.rsqrt(jnp.mean(value * value, axis=-1, keepdims=True) + EPS)
    middle[...] = value
    out[...] = (value * inverse * gain[...]).astype(BF)


def middle_call(x, got, gain, after):
    return call(
        middle_kernel,
        (1,),
        [whole(x.shape), whole(x.shape), whole(gain.shape)],
        [whole(x.shape)] * 2,
        [hbm(x.shape, F32), hbm(x.shape, BF)],
        [],
        (x, got, gain),
        24,
        prefetch=0,
        after=after,
    )


def norm_grad_kernel(x, got, base, gain, *outs):
    value, upstream = x[...].astype(F32), got[...].astype(F32)
    inverse = lax.rsqrt(jnp.mean(value * value, axis=-1, keepdims=True) + EPS)
    scaled = upstream * gain[...]
    through = inverse * scaled - value * (inverse * inverse * inverse) * jnp.mean(
        value * scaled, axis=-1, keepdims=True
    )
    total = base[...].astype(F32) + through
    outs[0][...] = total
    outs[1][...] = jnp.sum(upstream * value * inverse, axis=0, keepdims=True)
    if len(outs) > 2:
        outs[2][...] = total.astype(BF)


def norm_grad_call(x, got, base, gain, low, after=()):
    return call(
        norm_grad_kernel,
        (1,),
        [whole(x.shape)] * 3 + [whole(gain.shape)],
        [whole(x.shape), whole(gain.shape)] + [whole(x.shape)] * low,
        [hbm(x.shape, F32), hbm(gain.shape, F32)] + [hbm(x.shape, BF)] * low,
        [],
        (x, got, base, gain),
        24,
        prefetch=0,
        after=after,
    )


class WeightSum:
    def __init__(self, masks):
        self.flows = (masks, masks[::-1])
        seq = lax.axis_index("seq")
        self.core = seq & 1
        self.bits = [jnp.stack([(seq & m[k]) // m[k] for m in self.flows]) for k in range(len(masks))]
        base = jnp.array([0, 2], I32)
        self.send_ids, self.keep_ids = base + 1 - self.bits[0], base + self.bits[0]
        self.level = 0

    def swap_level(self, sends):
        self.gots = [swap(s, "seq", m[self.level]) for s, m in zip(sends, self.flows)]
        self.level += 1

    def begin(self, sends):
        self.swap_level(sends)

    def middle(self):
        count = len(self.flows[0])
        self.terms = [[k] for k in self.kept]
        while self.level < count:
            bits = self.bits[self.level]
            if self.level < count - 1:
                sends, kept = split_call(bits, self.kept, self.gots, ())
                self.kept = kept
            else:
                sends = half_sum_call(1 - bits, self.kept, self.gots)
                self.terms = [[k, g] for k, g in zip(self.kept, self.gots)]
            self.swap_level(sends)
        self.terms = [t + [g] for t, g in zip(self.terms, self.gots)]

    def last(self, after=()):
        parts = sum_call(self.bits[-1], self.terms, after)
        for level in range(len(self.flows[0]) - 1, 0, -1):
            gots = [swap(p, "seq", m[level]) for p, m in zip(parts, self.flows)]
            parts = [
                jnp.where(self.bits[level][f] == 0, *(jnp.concatenate(v, axis=1) for v in ((p, g), (g, p))))
                for f, (p, g) in enumerate(zip(parts, gots))
            ]
        self.parts = parts
        self.ends = [v for p, m in zip(parts, self.flows) for v in (p, swap(p, "seq", m[0]))]
        self.others = [swap(v, "seq", 1) for v in self.ends]

    def widen(self, planes, shapes, turned, after=()):
        blocks = jnp.stack([h for f in range(2) for h in (2 * f + self.bits[0][f], 2 * f + 1 - self.bits[0][f])])
        table = jnp.concatenate([self.core * 4 + blocks, (1 - self.core) * 4 + blocks])
        return widen_call(table, (*self.ends, *self.others), planes, shapes, turned, after)


def halves(value, core):
    half = value.shape[1] // 2
    return (
        lax.dynamic_slice_in_dim(value, core * half, half, 1),
        lax.dynamic_slice_in_dim(value, (1 - core) * half, half, 1),
    )


def body(
    hidden_in,
    output_grad,
    document_lengths,
    attention_gain,
    query_weight,
    key_weight,
    value_weight,
    query_gain,
    key_gain,
    output_weight,
    feedforward_gain,
    gate_weight,
    up_weight,
    down_weight,
):
    ORDER.clear()
    tp, seqs = lax.axis_size("tp"), lax.axis_size("seq")
    seq_at = lax.axis_index("seq")
    core = seq_at & 1
    row_count, share, width = hidden_in.shape
    span = share * tp
    masks = tuple(1 << b for b in range(1, seqs.bit_length() - 1))

    ends = jnp.stack(
        [jnp.sum(document_lengths[:, : n + 1], axis=1) for n in range(document_lengths.shape[1])], axis=1
    )
    starts = ends - document_lengths
    docs = document_lengths.shape[1]
    places = seq_at * span + jnp.arange(span, dtype=I32)
    inside = (places[None, :, None] >= starts[:, None]) & (places[None, :, None] < ends[:, None])
    begun = jnp.sum(jnp.where(inside, starts[:, None], 0), axis=2)
    slot_seq = jnp.arange(seqs, dtype=I32) ^ seq_at
    needed = (slot_seq <= seq_at)[None] & ((slot_seq + 1)[None] * span > begun[:, :1])
    meta = jnp.concatenate(
        [needed.astype(I32).reshape(-1), slot_seq * span, core[None], places[:1], starts.reshape(-1)]
    )
    frequency = ROPE_BASE ** (-2.0 * jnp.arange(HEAD // 2, dtype=F32) / HEAD)
    angles = (places[None] - begun).reshape(-1, 1).astype(F32) * frequency
    cos, sin = jnp.cos(angles), jnp.sin(angles)
    tables = (jnp.concatenate([cos, cos], 1), jnp.concatenate([-sin, sin], 1))
    core_meta = core[None]
    q_gain, k_gain = query_gain[None], key_gain[None]
    qkv_weights = (query_weight, key_weight, value_weight)

    flat = lambda v: v.reshape(-1, width)
    hidden, upward = flat(hidden_in), flat(output_grad)
    attn_gain, ff_gain = attention_gain[None], feedforward_gain[None]
    shares = lambda v: v.reshape(row_count, share, width)
    normed1 = gather_tp(shares(norm_call(hidden, attn_gain)))
    queries, kv, q_raw, k_raw, n1_keep, n1_send = qkv_call(
        core_meta, row_count, normed1, qkv_weights, (q_gain, k_gain), tables
    )
    grads = gather_tp(output_grad)
    kv_slots = []
    for value in [kv] + [swap(kv, "seq", m) for m in range(2, seqs, 2)]:
        kv_slots += [value, swap(value, "seq", 1)]
    attended, lse, o_part = attend_call(meta, docs, queries, kv_slots, output_weight)

    def both(own, sent=None):
        return [own, swap(own if sent is None else sent, "seq", 1)]

    o_both = both(attended)
    n1_both = both(n1_keep, n1_send)
    middle, normed2 = middle_call(hidden, flat(scatter_tp(o_part, row_count)), ff_gain, (grads,))
    grads_both = both(*halves(grads, core))
    normed2 = gather_tp(shares(normed2))
    planes, n2_keep, n2_send = ff_call(
        core_meta, normed2, grads, gate_weight, up_weight, down_weight, (grads_both[1], o_both[1], n1_both[1])
    )
    planes_both, n2_both = both(planes), both(n2_keep, n2_send)
    n2_got = scatter_tp(ff_back_call(planes, gate_weight, up_weight), row_count)

    ff = WeightSum(masks)
    ff.begin(ff_grad_call(ff.send_ids, grads_both, n2_both, planes_both))
    ff.kept = ff_grad_call(ff.keep_ids, grads_both, n2_both, planes_both)
    middle_grad, ff_gain_grad, branch = norm_grad_call(middle, flat(n2_got), upward, ff_gain, True, ff.gots)
    branch = gather_tp(shares(branch))
    ff.middle()
    ff_got = scatter_tp(ff_out_call(planes, down_weight), row_count)
    ff.last()
    dq, even, odd_low, odd_high, q_gain_grad, b_keep, b_send = attend_back_call(
        meta,
        docs,
        branch,
        output_weight,
        queries,
        kv_slots,
        attended,
        lse,
        q_raw,
        q_gain,
        tables,
        ff.parts,
    )
    odd = [v[k] for v in (swap(odd_low, "seq", 1), swap(odd_high, "seq", 1)) for k in range(seqs // 4)]
    chip = [(even[k].astype(F32) + odd[k].astype(F32)).astype(BF) for k in range(seqs // 2)]
    pieces = [chip[0]] + [swap(chip[m // 2], "seq", m) for m in range(2, seqs, 2)]
    bg_both = both(b_keep, b_send)
    all_grad, k_gain_grad = key_back_call(pieces, dq, k_raw, k_gain, tables, (*ff.ends, ff_got, bg_both[1]))
    all_both = both(all_grad)
    n1_part = back_call(all_grad, qkv_weights)
    n1_got = scatter_tp(n1_part, row_count)
    attn = WeightSum(masks)
    ids = jnp.concatenate([attn.send_ids, attn.keep_ids])
    parts = attn_grad_call(ids, n1_both, bg_both, all_both, o_both)
    attn.kept = parts[2:]
    attn.begin(parts[:2])
    gate_out, up_out = ff.widen((1, 2), [gate_weight.shape, up_weight.shape], ())
    attn.middle()
    input_grad, attn_gain_grad = norm_grad_call(hidden, flat(n1_got), middle_grad, attn_gain, False)
    gains = jnp.concatenate(
        [v.reshape(-1) for v in (attn_gain_grad, ff_gain_grad, q_gain_grad, k_gain_grad)]
    ).reshape(-1, HEAD)
    sums = [gains]
    for axis, size in (("tp", tp), ("seq", seqs)):
        for level in range(size.bit_length() - 1):
            sums.append(sums[-1] + swap(sums[-1], axis, 1 << level))
    gains = sums[-1]
    input_grad = shares(input_grad)
    block_out = shares((middle + flat(ff_got).astype(F32)).astype(BF))
    attn.last()
    (down_out,) = ff.widen((0,), [down_weight.shape], (0,))
    query_out, key_out, value_out, output_out = attn.widen(
        (0,), [w.shape for w in (*qkv_weights, output_weight)], (3,), sums[-1:]
    )
    gains = gains.reshape(-1)
    return (
        block_out,
        input_grad,
        gains[:width],
        query_out,
        key_out,
        value_out,
        gains[2 * width : 2 * width + HEAD],
        gains[2 * width + HEAD :],
        output_out,
        gains[width : 2 * width],
        gate_out,
        up_out,
        down_out,
    )


def solution(mesh):
    tokens, columns, rows = P(None, ("seq", "tp"), None), P(None, "tp"), P("tp", None)
    in_specs = (
        tokens,
        tokens,
        P(),
        P(),
        columns,
        columns,
        columns,
        P(),
        P(),
        rows,
        P(),
        columns,
        columns,
        rows,
    )
    out_specs = (
        tokens,
        tokens,
        P(),
        columns,
        columns,
        columns,
        P(),
        P(),
        rows,
        P(),
        columns,
        columns,
        rows,
    )
    return jax.shard_map(body, mesh=mesh, in_specs=in_specs, out_specs=out_specs, check_vma=False)
```

time: 690 us -> 598 us (0.87)
  Pallas kernels: 239 us -> 173 us
  starting transfers between devices: 66 us -> 44.4 us
  local copies, waits for them, and re-layouts: 24.2 us -> 13.4 us
  other arithmetic: 9.95 us -> 18 us
    pallas_call x35 -> x22, Pallas kernels: 239 us -> 173 us  [call(): pl.pallas_call(run, grid_spec=pltpu.PrefetchScalarGridSpec(num_scalar_pre...]
    ppermute x68 -> x48, starting transfers between devices: 65.3 us -> 43.7 us  [swap(): return lax.ppermute(value, axis, flip(axis, mask))]
    reduce_scatter x4, waiting for transfers between devices: 48.4 us -> 62.6 us  [scatter_tp(): return lax.psum_scatter(part, 'tp', scatter_dimension=1, tiled=True)]
    ppermute x68 -> x48, waiting for transfers between devices: 192 us -> 179 us  [swap(): return lax.ppermute(value, axis, flip(axis, mask))]
    unnamed x156 -> x86, local copies, waits for them, and re-layouts: 20.4 us -> 9.39 us
    select_n x0 -> x4, other arithmetic: none -> 8.29 us  [last(): jnp.where(self.bits[level][f] == 0, *(jnp.concatenate(v, axis=1) for v in...]
  transfers between devices with their start and end apart: 76 -> 56, of which waited for: 33 -> 31; matrix products, arithmetic and copies ran while one was open for 2% -> 4% of each run, Pallas kernels for 21% -> 21%
where the time goes in v3:
time: 598 us; the launch traced here: 589 us
  waiting for transfers between devices  325 us (54%)
  Pallas kernels  173 us (29%)
  starting transfers between devices  44.4 us (7%)
  other arithmetic  18 us (3%)
  between operations  15 us (3%)
  local copies, waits for them, and re-layouts  13.4 us (2%)
    ppermute x48, waiting for transfers between devices, swap(): return lax.ppermute(value, axis, flip(axis, mask))  179 us
    pallas_call x22, Pallas kernels, call(): pl.pallas_call(run, grid_spec=pltpu.PrefetchScalarGridSpec(num_scalar_pre...  173 us
    all_gather x4, waiting for transfers between devices, gather_tp(): return lax.all_gather(share, 'tp', axis=1, tiled=True).reshape(-1, width)  82.3 us
    reduce_scatter x4, waiting for transfers between devices, scatter_tp(): return lax.psum_scatter(part, 'tp', scatter_dimension=1, tiled=True)  62.6 us
    ppermute x48, starting transfers between devices, swap(): return lax.ppermute(value, axis, flip(axis, mask))  43.7 us
  transfers between devices with their start and end apart: 56, of which 31 were waited for; matrix products, arithmetic and copies ran while one was open for 4% of the time, Pallas kernels for 21%

profile of v3, /device:TPU:0, one launch (start us, length us, event | category | flops | bytes accessed | tf_op | source)
XLA Modules:
  0.0 588.8 jit_solution(16377354418179083854)
XLA Ops:
  15.6 43.2 %all-gather.5.cloned.1.call-done = bf16[2,256,2048]{2,1,0:T(8,128)(2,1)} async-done(((bf16[2,64,2048]{2,1,0:T(8,128)(2,1)}), bf16[2,256,2048]{2,1,0:T(8,128)(2,1)}) %all-gather.5.cloned.1.call-update) | async-done | bytes 2097168 | tf_op jit(solution)/shard_map/all_gather | solution.py:90
  58.8 9.3 %shard_map.256 = (bf16[512,512]{1,0:T(8,128)(2,1)}, bf16[2,2,256,256]{3,2,1,0:T(8,128)(2,1)}, f32[512,512]{1,0:T(8,128)}, f32[512,256]{1,0:T(8,128)}, bf16[512,1...) custom-call(s32[1]{0:T(128)} %bitcast.4.refs_0_, bf16[512,2048]{1,0:T(8,128)(2,1)} %bitcast.79, bf16[2048,512]{1,0:T(8,128)(2,1)} %refs_1_.3, ...), custom_call_target="tpu_custom_call" | custom-call | flops 1 | bytes 1 | tf_op jit(solution)/shard_map/pallas_call | solution.py:57
  72.2 11.9 %collective-permute-done.5.refs_8_.refs_10_ = bf16[2,2,256,256]{3,2,1,0:T(8,128)(2,1)S(1)} collective-permute-done((bf16[2,2,256,256]{3,2,1,0:T(8,128)(2,1)}, bf16[2,2,256,256]{3,2,1,0:T(8,128)(2,1)S(1)}, u32[]{:S(2)}, u32[]{:S(2)}) %collective-permute-start.5) | collective-permute-done | bytes 524320 | tf_op jit(solution)/shard_map/ppermute | solution.py:85
  84.1 10.0 %collective-permute-done.3.refs_6_.refs_8_ = bf16[2,2,256,256]{3,2,1,0:T(8,128)(2,1)S(1)} collective-permute-done((bf16[2,2,256,256]{3,2,1,0:T(8,128)(2,1)}, bf16[2,2,256,256]{3,2,1,0:T(8,128)(2,1)S(1)}, u32[]{:S(2)}, u32[]{:S(2)}) %collective-permute-start.3) | collective-permute-done | bytes 524320 | tf_op jit(solution)/shard_map/ppermute | solution.py:85
  96.9 13.3 %shard_map.257 = (bf16[512,512]{1,0:T(8,128)(2,1)}, f32[2,2,512,1]{3,2,1,0:T(8,128)}, bf16[512,2048]{1,0:T(8,128)(2,1)}) custom-call(s32[34]{0:T(128)S(1)} %concatenate.76.refs_0_, bf16[512,512]{1,0:T(8,128)(2,1)} %get-tuple-element.63.refs_1_.refs_11_.refs_3_, bf16[2,2,256,256]{3,2,1,0:T(8,128)(2,1)} %get-tuple-element.64.refs_2_.refs_4_, ...), custom_call_target="tpu_custom_call" | custom-call | flops 1 | bytes 1 | tf_op jit(solution)/shard_map/pallas_call | solution.py:57
  110.4 49.8 %reduce-scatter.5.cloned.1.call-done = bf16[2,64,2048]{2,1,0:T(8,128)(2,1)} async-done(((bf16[2,256,2048]{2,1,0:T(8,128)(2,1)}), bf16[2,64,2048]{2,1,0:T(8,128)(2,1)}) %reduce-scatter.5.cloned.1.call-update) | async-done | bytes 524304 | tf_op jit(solution)/shard_map/reduce_scatter | solution.py:95
  169.0 39.1 %all-gather.9.cloned.1.call-done = bf16[2,256,2048]{2,1,0:T(8,128)(2,1)} async-done(((bf16[2,64,2048]{2,1,0:T(8,128)(2,1)}), bf16[2,256,2048]{2,1,0:T(8,128)(2,1)}) %all-gather.9.cloned.1.call-update) | async-done | bytes 2097168 | tf_op jit(solution)/shard_map/all_gather | solution.py:90
  208.1 16.5 %shard_map.259 = (bf16[3,512,1536]{2,1,0:T(8,128)(2,1)}, bf16[512,1024]{1,0:T(8,128)(2,1)}, bf16[512,1024]{1,0:T(8,128)(2,1)}) custom-call(s32[1]{0:T(128)} %bitcast.4.refs_0_, bf16[512,2048]{1,0:T(8,128)(2,1)} %bitcast.77, bf16[512,2048]{1,0:T(8,128)(2,1)} %bitcast.67, bf16[2048,1536]{1,0:T(8,128)(2,1)} %refs_2_.5, bf16[2048,1536]{1,0:T(8,128)(2,1)} %refs_3_.6, ...), custom_call_target="tpu_custom_call" | custom-call | flops 1 | bytes 1 | tf_op jit(solution)/shard_map/pallas_call | solution.py:57
  224.6 11.3 %shard_map.260.refs_7_ = bf16[512,2048]{1,0:T(8,128)(2,1)} custom-call(bf16[3,512,1536]{2,1,0:T(8,128)(2,1)} %get-tuple-element.70.refs_0_.refs_1_.refs_4_.refs_5_, bf16[3,512,1536]{2,1,0:T(8,128)(2,1)} %get-tuple-element.70.refs_0_.refs_1_.refs_4_.refs_5_, bf16[2048,1536]{1,0:T(8,128)(2,1)} %refs_2_.5, bf16[2048,1536]{1,0:T(8,128)(2,1)} %refs_3_.6, ...), custom_call_target="tpu_custom_call" | custom-call | flops 1 | bytes 1 | tf_op jit(solution)/shard_map/pallas_call | solution.py:57
  239.8 11.7 %shard_map.261 = (bf16[3,256,1536]{2,1,0:T(8,128)(2,1)}, bf16[3,256,1536]{2,1,0:T(8,128)(2,1)}) custom-call(s32[2]{0:T(128)S(1)} %get-tuple-element.136.refs_0_, bf16[512,1024]{1,0:T(8,128)(2,1)} %get-tuple-element.123.refs_1_, bf16[512,1024]{1,0:T(8,128)(2,1)} %copy-done.5, bf16[512,1024]{1,0:T(8,128)(2,1)} %get-tuple-element.71.refs_3_, ...), custom_call_target="tpu_custom_call" | custom-call | flops 1 | bytes 1 | tf_op jit(solution)/shard_map/pallas_call | solution.py:57
  254.5 11.5 %shard_map.262 = (bf16[3,256,1536]{2,1,0:T(8,128)(2,1)}, bf16[3,256,1536]{2,1,0:T(8,128)(2,1)}) custom-call(s32[2]{0:T(128)S(1)} %get-tuple-element.137.refs_0_, bf16[512,1024]{1,0:T(8,128)(2,1)} %get-tuple-element.123.refs_1_, bf16[512,1024]{1,0:T(8,128)(2,1)} %copy-done.5, bf16[512,1024]{1,0:T(8,128)(2,1)} %get-tuple-element.71.refs_3_, ...), custom_call_target="tpu_custom_call" | custom-call | flops 1 | bytes 1 | tf_op jit(solution)/shard_map/pallas_call | solution.py:57
  266.0 12.8 %reduce-scatter.7.cloned.1.call-done = bf16[2,64,2048]{2,1,0:T(8,128)(2,1)} async-done(((bf16[2,256,2048]{2,1,0:T(8,128)(2,1)}), bf16[2,64,2048]{2,1,0:T(8,128)(2,1)}) %reduce-scatter.7.cloned.1.call-update) | async-done | bytes 524304 | tf_op jit(solution)/shard_map/reduce_scatter | solution.py:95
  278.8 26.4 %collective-permute-done.13.refs_6_.refs_4_.refs_5_ = bf16[3,256,1536]{2,1,0:T(8,128)(2,1)S(1)} collective-permute-done((bf16[3,256,1536]{2,1,0:T(8,128)(2,1)}, bf16[3,256,1536]{2,1,0:T(8,128)(2,1)S(1)}, u32[]{:S(2)}, u32[]{:S(2)}) %collective-permute-start.13) | collective-permute-done | bytes 2359328 | tf_op jit(solution)/shard_map/ppermute | solution.py:85
  310.2 4.2 shard_map.264
  317.4 7.4 %shard_map.265.refs_7_ = bf16[512,2048]{1,0:T(8,128)(2,1)} custom-call(bf16[3,512,1536]{2,1,0:T(8,128)(2,1)} %get-tuple-element.70.refs_0_.refs_1_.refs_4_.refs_5_, bf16[1536,2048]{1,0:T(8,128)(2,1)} %refs_1_.2, bf16[3,128,1536]{2,1,0:T(8,128)(2,1)} %get-tuple-element.78.refs_2_), custom_call_target="tpu_custom_call" | custom-call | flops 1 | bytes 1 | tf_op jit(solution)/shard_map/pallas_call | solution.py:57
  325.1 17.0 %collective-permute-done.15.refs_6_ = bf16[3,128,1536]{2,1,0:T(8,128)(2,1)S(1)} collective-permute-done((bf16[3,128,1536]{2,1,0:T(8,128)(2,1)}, bf16[3,128,1536]{2,1,0:T(8,128)(2,1)S(1)}, u32[]{:S(2)}, u32[]{:S(2)}) %collective-permute-start.15) | collective-permute-done | bytes 1179680 | tf_op jit(solution)/shard_map/ppermute | solution.py:85
  344.3 5.1 shard_map.266
  351.5 24.5 %collective-permute-done.16 = bf16[3,128,1536]{2,1,0:T(8,128)(2,1)} collective-permute-done((bf16[3,128,1536]{2,1,0:T(8,128)(2,1)}, bf16[3,128,1536]{2,1,0:T(8,128)(2,1)}, u32[]{:S(2)}, u32[]{:S(2)}) %collective-permute-start.16) | collective-permute-done | bytes 1179680 | tf_op jit(solution)/shard_map/ppermute | solution.py:85
  384.2 12.8 %shard_map.267 = (bf16[512,512]{1,0:T(8,128)(2,1)}, bf16[4,2,2,256,256]{4,3,2,1,0:T(8,128)(2,1)}, bf16[2,2,2,256,256]{4,3,2,1,0:T(8,128)(2,1)}, bf16[2,2,2,256,2...) custom-call(s32[34]{0:T(128)S(1)} %concatenate.76.refs_0_, ...), custom_call_target="tpu_custom_call" | custom-call | flops 1 | bytes 1 | tf_op jit(solution)/shard_map/pallas_call | solution.py:57
  404.7 12.8 %collective-permute-start.22 = (bf16[2,2,256,256]{3,2,1,0:T(8,128)(2,1)}, bf16[2,2,256,256]{3,2,1,0:T(8,128)(2,1)}, u32[]{:S(2)}, u32[]{:S(2)}) collective-permute-start(bf16[2,2,256,256]{3,2,1,0:T(8,128)(2,1)} %get-tuple-element.117), channel_id=1, source_target_pairs={{0,24},{4,28},{8,16},{12,20},{16,8},{20,12},{24,0},{28,4},{1,25},{... | collective-permute-start | bytes 1572872 | tf_op jit(solution)/shard_map/ppermute | solution.py:85
  418.1 27.2 %collective-permute-done.22.refs_3_ = bf16[2,2,256,256]{3,2,1,0:T(8,128)(2,1)} collective-permute-done((bf16[2,2,256,256]{3,2,1,0:T(8,128)(2,1)}, bf16[2,2,256,256]{3,2,1,0:T(8,128)(2,1)}, u32[]{:S(2)}, u32[]{:S(2)}) %collective-permute-start.22) | collective-permute-done | bytes 524320 | tf_op jit(solution)/shard_map/ppermute | solution.py:85
  445.3 11.0 %collective-permute-done.21.refs_2_ = bf16[2,2,256,256]{3,2,1,0:T(8,128)(2,1)} collective-permute-done((bf16[2,2,256,256]{3,2,1,0:T(8,128)(2,1)}, bf16[2,2,256,256]{3,2,1,0:T(8,128)(2,1)}, u32[]{:S(2)}, u32[]{:S(2)}) %collective-permute-start.21) | collective-permute-done | bytes 524320 | tf_op jit(solution)/shard_map/ppermute | solution.py:85
  456.3 3.8 shard_map.268
  460.1 6.3 %shard_map.269.refs_9_ = bf16[512,2048]{1,0:T(8,128)(2,1)} custom-call(bf16[512,1024]{1,0:T(8,128)(2,1)} %get-tuple-element.91.refs_0_.refs_4_.refs_5_, bf16[2048,512]{1,0:T(8,128)(2,1)} %refs_1_.3, bf16[2048,256]{1,0:T(8,128)(2,1)} %refs_2_.7, bf16[2048,256]{1,0:T(8,128)(2,1)} %refs_3_.7, bf16[512,1024]{1,0:T(8,128)(2,1)} %get-tuple-element.91.refs_0_.refs_4_.refs_5_), custom_call_target="tpu_custom_call" | custom-call | flops 1 | bytes 1 | tf_op jit(solution)/shard_map/pallas_call | solution.py:57
  467.7 8.9 %collective-permute-done.26.refs_6_ = bf16[512,1024]{1,0:T(8,128)(2,1)S(1)} collective-permute-done((bf16[512,1024]{1,0:T(8,128)(2,1)S(1)}, bf16[512,1024]{1,0:T(8,128)(2,1)S(1)}, u32[]{:S(2)}, u32[]{:S(2)}) %collective-permute-start.26) | collective-permute-done | bytes 1048608 | tf_op jit(solution)/shard_map/ppermute | solution.py:85
  477.6 10.0 %shard_map.270 = (bf16[1,256,1536]{2,1,0:T(8,128)(2,1)}, bf16[1,256,1536]{2,1,0:T(8,128)(2,1)}, bf16[1,256,1536]{2,1,0:T(8,128)(2,1)}, bf16[1,256,1536]{2,1,0:T(8,128)(2,1)}) custom-call(s32[4]{0:T(128)S(1)} %pad_add_fusion.3.refs_0_, bf16[512,1024]{1,0:T(8,128)(2,1)} %get-tuple-element.92.refs_1_, bf16[512,1024]{1,0:T(8,128)(2,1)} %copy-done.9, ...), custom_call_target="tpu_custom_call" | custom-call | flops 1 | bytes 1 | tf_op jit(solution)/shard_map/pallas_call | solution.py:57
  492.2 14.0 %shard_map.271 = (f32[2048,1536]{1,0:T(8,128)}, f32[2048,1536]{1,0:T(8,128)}) custom-call(s32[8]{0:T(128)} %pad_add_fusion.5.refs_0_, bf16[3,256,1536]{2,1,0:T(8,128)(2,1)} %copy-done, bf16[3,256,1536]{2,1,0:T(8,128)(2,1)} %copy-done, bf16[3,256,1536]{2,1,0:T(8,128)(2,1)} %collective-permute-done.23.refs_11_.refs_3_.refs_4_.refs_2_, ...), custom_call_target="tpu_custom_call" | custom-call | flops 1 | bytes 1 | tf_op jit(solution)/shard_map/pallas_call | solution.py:57
  518.4 5.6 collective-permute-done.39.refs_6_
  530.4 7.4 %collective-permute-done.40 = bf16[1,128,1536]{2,1,0:T(8,128)(2,1)S(1)} collective-permute-done((bf16[1,128,1536]{2,1,0:T(8,128)(2,1)}, bf16[1,128,1536]{2,1,0:T(8,128)(2,1)S(1)}, u32[]{:S(2)}, u32[]{:S(2)}) %collective-permute-start.40) | collective-permute-done | bytes 393248 | tf_op jit(solution)/shard_map/ppermute | solution.py:85
  542.6 3.6 collective-permute-done.33
  559.3 9.7 %shard_map.275.refs_9_ = f32[1536,2048]{1,0:T(8,128)} custom-call(s32[8]{0:T(128)} %pad_add_fusion.5.refs_0_, bf16[3,256,1536]{2,1,0:T(8,128)(2,1)} %copy-done, bf16[3,256,1536]{2,1,0:T(8,128)(2,1)} %collective-permute-done.23.refs_11_.refs_3_.refs_4_.refs_2_, bf16[3,256,1536]{2,1,0:T(8,128)(2,1)} %maximum_select_fusion.1.refs_20_.refs_12_.refs_5_.refs_6_.refs_3_, ...), custom_call_target="tpu_custom_call" | custom-call | flops 1 | bytes 1 | tf_op jit(solution)/shard_map/pallas_call | solution.py:57
  572.4 9.2 %shard_map.276 = (f32[2048,512]{1,0:T(8,128)}, f32[2048,256]{1,0:T(8,128)}, f32[2048,256]{1,0:T(8,128)}, f32[512,2048]{1,0:T(8,128)}) custom-call(s32[8]{0:T(128)} %pad_add_fusion.5.refs_0_, bf16[1,256,1536]{2,1,0:T(8,128)(2,1)} %copy-done.14, bf16[1,256,1536]{2,1,0:T(8,128)(2,1)} %copy-done.28, bf16[1,256,1536]{2,1,0:T(8,128)(2,1)} %copy-done.15, ...), custom_call_target="tpu_custom_call" | custom-call | flops 1 | bytes 1 | tf_op jit(solution)/shard_map/pallas_call | solution.py:57
  (239 shorter events, 106.7 us)
Async XLA Ops:
  7.2 51.7 %all-gather.5.cloned.1.call-start = ((), (), s32[]{:S(2)}) async-start(), calls=%async_computation.4 | async-start | bytes 2621440 | tf_op jit(solution)/shard_map/all_gather | solution.py:90
  9.3 101.0 %all-gather.7.cloned.1.call-start = ((), (), s32[]{:S(2)}) async-start(), calls=%async_computation.6 | async-start | bytes 2621440 | tf_op jit(solution)/shard_map/all_gather | solution.py:90
  10.1 150.1 %reduce-scatter.5.cloned.1.call-start = ((), (), s32[]{:S(2)}) async-start(), calls=%async_computation.5 | async-start | bytes 2621440 | tf_op jit(solution)/shard_map/reduce_scatter | solution.py:95
  68.1 16.0 %collective-permute-start.5 = (bf16[2,2,256,256]{3,2,1,0:T(8,128)(2,1)}, bf16[2,2,256,256]{3,2,1,0:T(8,128)(2,1)S(1)}, u32[]{:S(2)}, u32[]{:S(2)}) collective-permute-start(bf16[2,2,256,256]{3,2,1,0:T(8,128)(2,1)} %get-tuple-element.64.refs_2_.refs_4_), channel_id=1, source_target_pairs={{0,24},{4,28},{8,16},{12,20},{16,8},{20,12},{24,0},{28,4},{1,25},{... | collective-permute-start | bytes 1572872 | tf_op jit(solution)/shard_map/ppermute | solution.py:85
  70.5 23.6 %collective-permute-start.3 = (bf16[2,2,256,256]{3,2,1,0:T(8,128)(2,1)}, bf16[2,2,256,256]{3,2,1,0:T(8,128)(2,1)S(1)}, u32[]{:S(2)}, u32[]{:S(2)}) collective-permute-start(bf16[2,2,256,256]{3,2,1,0:T(8,128)(2,1)} %get-tuple-element.64.refs_2_.refs_4_), channel_id=1, source_target_pairs={{0,16},{4,20},{8,24},{12,28},{16,0},{20,4},{24,8},{28,12},{1,17},{... | collective-permute-start | bytes 1572872 | tf_op jit(solution)/shard_map/ppermute | solution.py:85
  71.1 23.2 %collective-permute-start.1 = (bf16[2,2,256,256]{3,2,1,0:T(8,128)(2,1)}, bf16[2,2,256,256]{3,2,1,0:T(8,128)(2,1)S(1)}, u32[]{:S(2)}, u32[]{:S(2)}) collective-permute-start(bf16[2,2,256,256]{3,2,1,0:T(8,128)(2,1)} %get-tuple-element.64.refs_2_.refs_4_), channel_id=1, source_target_pairs={{0,8},{4,12},{8,0},{12,4},{16,24},{20,28},{24,16},{28,20},{1,9},{5... | collective-permute-start | bytes 1572872 | tf_op jit(solution)/shard_map/ppermute | solution.py:85
  72.2 23.4 %collective-permute-start = (bf16[2,2,256,256]{3,2,1,0:T(8,128)(2,1)}, bf16[2,2,256,256]{3,2,1,0:T(8,128)(2,1)S(1)}, u32[]{:S(2)}, u32[]{:S(2)}) collective-permute-start(bf16[2,2,256,256]{3,2,1,0:T(8,128)(2,1)} %get-tuple-element.64.refs_2_.refs_4_), channel_id=1, source_target_pairs={{0,4},{4,0},{8,12},{12,8},{16,20},{20,16},{24,28},{28,24},{1,5},{5... | collective-permute-start | bytes 1572872 | tf_op jit(solution)/shard_map/ppermute | solution.py:85
  110.3 97.8 %all-gather.9.cloned.1.call-start = ((), (), s32[]{:S(2)}) async-start(), calls=%async_computation.7 | async-start | bytes 2621440 | tf_op jit(solution)/shard_map/all_gather | solution.py:90
  162.7 116.1 %reduce-scatter.7.cloned.1.call-start = ((), (), s32[]{:S(2)}) async-start(), calls=%async_computation.8 | async-start | bytes 2621440 | tf_op jit(solution)/shard_map/reduce_scatter | solution.py:95
  236.0 148.3 %all-gather.11.cloned.1.call-start = ((), (), s32[]{:S(2)}) async-start(), calls=%async_computation.10 | async-start | bytes 2621440 | tf_op jit(solution)/shard_map/all_gather | solution.py:90
  251.4 53.7 %collective-permute-start.13 = (bf16[3,256,1536]{2,1,0:T(8,128)(2,1)}, bf16[3,256,1536]{2,1,0:T(8,128)(2,1)S(1)}, u32[]{:S(2)}, u32[]{:S(2)}) collective-permute-start(bf16[3,256,1536]{2,1,0:T(8,128)(2,1)} %get-tuple-element.76), channel_id=1, source_target_pairs={{0,16},{4,20},{8,24},{12,28},{16,0},{20,4},{24,8},{28,12},{1,17},{... | collective-permute-start | bytes 7077896 | tf_op jit(solution)/shard_map/ppermute | solution.py:85
  253.0 53.5 %collective-permute-start.12 = (bf16[3,256,1536]{2,1,0:T(8,128)(2,1)}, bf16[3,256,1536]{2,1,0:T(8,128)(2,1)}, u32[]{:S(2)}, u32[]{:S(2)}) collective-permute-start(bf16[3,256,1536]{2,1,0:T(8,128)(2,1)} %get-tuple-element.73.refs_7_), channel_id=1, source_target_pairs={{0,8},{4,12},{8,0},{12,4},{16,24},{20,28},{24,16},{28,20},{1,9},{5... | collective-permute-start | bytes 7077896 | tf_op jit(solution)/shard_map/ppermute | solution.py:85
  310.0 108.0 %reduce-scatter.9.cloned.1.call-start = ((), (), s32[]{:S(2)}) async-start(), calls=%async_computation.9 | async-start | bytes 2621440 | tf_op jit(solution)/shard_map/reduce_scatter | solution.py:95
  314.3 27.7 %collective-permute-start.15 = (bf16[3,128,1536]{2,1,0:T(8,128)(2,1)}, bf16[3,128,1536]{2,1,0:T(8,128)(2,1)S(1)}, u32[]{:S(2)}, u32[]{:S(2)}) collective-permute-start(bf16[3,128,1536]{2,1,0:T(8,128)(2,1)} %get-tuple-element.82), channel_id=1, source_target_pairs={{0,8},{4,12},{8,0},{12,4},{16,24},{20,28},{24,16},{28,20},{1,9},{5... | collective-permute-start | bytes 3538952 | tf_op jit(solution)/shard_map/ppermute | solution.py:85
  315.9 27.4 %collective-permute-start.14 = (bf16[3,128,1536]{2,1,0:T(8,128)(2,1)}, bf16[3,128,1536]{2,1,0:T(8,128)(2,1)S(1)}, u32[]{:S(2)}, u32[]{:S(2)}) collective-permute-start(bf16[3,128,1536]{2,1,0:T(8,128)(2,1)} %get-tuple-element.78.refs_2_), channel_id=1, source_target_pairs={{0,16},{4,20},{8,24},{12,28},{16,0},{20,4},{24,8},{28,12},{1,17},{... | collective-permute-start | bytes 3538952 | tf_op jit(solution)/shard_map/ppermute | solution.py:85
  324.8 190.5 %reduce-scatter.11.cloned.1.call-start = ((), (), s32[]{:S(2)}) async-start(), calls=%async_computation.11 | async-start | bytes 2621440 | tf_op jit(solution)/shard_map/reduce_scatter | solution.py:95
  349.4 26.7 %collective-permute-start.16 = (bf16[3,128,1536]{2,1,0:T(8,128)(2,1)}, bf16[3,128,1536]{2,1,0:T(8,128)(2,1)}, u32[]{:S(2)}, u32[]{:S(2)}) collective-permute-start(bf16[3,128,1536]{2,1,0:T(8,128)(2,1)} %get-tuple-element.83.refs_18_), channel_id=1, source_target_pairs={{0,16},{4,20},{8,24},{12,28},{16,0},{20,4},{24,8},{28,12},{1,17},{... | collective-permute-start | bytes 3538952 | tf_op jit(solution)/shard_map/ppermute | solution.py:85
  350.8 29.0 %collective-permute-start.17 = (bf16[3,128,1536]{2,1,0:T(8,128)(2,1)}, bf16[3,128,1536]{2,1,0:T(8,128)(2,1)}, u32[]{:S(2)}, u32[]{:S(2)}) collective-permute-start(bf16[3,128,1536]{2,1,0:T(8,128)(2,1)} %get-tuple-element.84), channel_id=1, source_target_pairs={{0,8},{4,12},{8,0},{12,4},{16,24},{20,28},{24,16},{28,20},{1,9},{5... | collective-permute-start | bytes 3538952 | tf_op jit(solution)/shard_map/ppermute | solution.py:85
  378.8 77.5 %collective-permute-start.23 = (bf16[3,256,1536]{2,1,0:T(8,128)(2,1)S(1)}, bf16[3,256,1536]{2,1,0:T(8,128)(2,1)}, u32[]{:S(2)}, u32[]{:S(2)}) collective-permute-start(bf16[3,256,1536]{2,1,0:T(8,128)(2,1)S(1)} %maximum_select_fusion.refs_19_.refs_10_.refs_1_.refs_2_), channel_id=1, source_target_pairs={{0,8},{4,12},{8,0},{12,4},{16,24},{20,28},{24,16},{28,20},{1,9},{5... | collective-permute-start | bytes 7077896 | tf_op jit(solution)/shard_map/ppermute | solution.py:85
  382.8 73.5 %collective-permute-start.24 = (bf16[3,256,1536]{2,1,0:T(8,128)(2,1)}, bf16[3,256,1536]{2,1,0:T(8,128)(2,1)}, u32[]{:S(2)}, u32[]{:S(2)}) collective-permute-start(bf16[3,256,1536]{2,1,0:T(8,128)(2,1)} %maximum_select_fusion.1.refs_20_.refs_12_.refs_5_.refs_6_.refs_3_), channel_id=1, source_target_pairs={{0,16},{4,20},{8,24},{12,28},{16,0},{20,4},{24,8},{28,12},{1,17},{... | collective-permute-start | bytes 7077896 | tf_op jit(solution)/shard_map/ppermute | solution.py:85
  397.6 19.9 %collective-permute-start.25 = (bf16[512,1024]{1,0:T(8,128)(2,1)}, bf16[512,1024]{1,0:T(8,128)(2,1)S(1)}, u32[]{:S(2)}, u32[]{:S(2)}) collective-permute-start(bf16[512,1024]{1,0:T(8,128)(2,1)} %get-tuple-element.90), channel_id=1, source_target_pairs={{0,4},{4,0},{8,12},{12,8},{16,20},{20,16},{24,28},{28,24},{1,5},{5... | collective-permute-start | bytes 3145736 | tf_op jit(solution)/shard_map/ppermute | solution.py:85
  404.7 40.6 %collective-permute-start.22 = (bf16[2,2,256,256]{3,2,1,0:T(8,128)(2,1)}, bf16[2,2,256,256]{3,2,1,0:T(8,128)(2,1)}, u32[]{:S(2)}, u32[]{:S(2)}) collective-permute-start(bf16[2,2,256,256]{3,2,1,0:T(8,128)(2,1)} %get-tuple-element.117), channel_id=1, source_target_pairs={{0,24},{4,28},{8,16},{12,20},{16,8},{20,12},{24,0},{28,4},{1,25},{... | collective-permute-start | bytes 1572872 | tf_op jit(solution)/shard_map/ppermute | solution.py:85
  417.5 38.8 %collective-permute-start.21 = (bf16[2,2,256,256]{3,2,1,0:T(8,128)(2,1)}, bf16[2,2,256,256]{3,2,1,0:T(8,128)(2,1)}, u32[]{:S(2)}, u32[]{:S(2)}) collective-permute-start(bf16[2,2,256,256]{3,2,1,0:T(8,128)(2,1)} %get-tuple-element.118), channel_id=1, source_target_pairs={{0,16},{4,20},{8,24},{12,28},{16,0},{20,4},{24,8},{28,12},{1,17},{... | collective-permute-start | bytes 1572872 | tf_op jit(solution)/shard_map/ppermute | solution.py:85
  417.5 38.8 %collective-permute-start.19 = (bf16[2,2,256,256]{3,2,1,0:T(8,128)(2,1)}, bf16[2,2,256,256]{3,2,1,0:T(8,128)(2,1)}, u32[]{:S(2)}, u32[]{:S(2)}) collective-permute-start(bf16[2,2,256,256]{3,2,1,0:T(8,128)(2,1)} %get-tuple-element.122), channel_id=1, source_target_pairs={{0,8},{4,12},{8,0},{12,4},{16,24},{20,28},{24,16},{28,20},{1,9},{5... | collective-permute-start | bytes 1572872 | tf_op jit(solution)/shard_map/ppermute | solution.py:85
  466.4 22.7 %collective-permute-start.29 = (bf16[3,256,1536]{2,1,0:T(8,128)(2,1)S(1)}, bf16[3,256,1536]{2,1,0:T(8,128)(2,1)S(1)}, u32[]{:S(2)}, u32[]{:S(2)}) collective-permute-start(bf16[3,256,1536]{2,1,0:T(8,128)(2,1)S(1)} %copy-done.1), channel_id=1, source_target_pairs={{0,4},{4,0},{8,12},{12,8},{16,20},{20,16},{24,28},{28,24},{1,5},{5... | collective-permute-start | bytes 7077896 | tf_op jit(solution)/shard_map/ppermute | solution.py:85
  466.5 25.7 %collective-permute-start.31 = (bf16[3,256,1536]{2,1,0:T(8,128)(2,1)}, bf16[3,256,1536]{2,1,0:T(8,128)(2,1)}, u32[]{:S(2)}, u32[]{:S(2)}) collective-permute-start(bf16[3,256,1536]{2,1,0:T(8,128)(2,1)} %maximum_select_fusion.1.refs_20_.refs_12_.refs_5_.refs_6_.refs_3_), channel_id=1, source_target_pairs={{0,4},{4,0},{8,12},{12,8},{16,20},{20,16},{24,28},{28,24},{1,5},{5... | collective-permute-start | bytes 7077896 | tf_op jit(solution)/shard_map/ppermute | solution.py:85
  467.0 25.2 %collective-permute-start.30 = (bf16[3,256,1536]{2,1,0:T(8,128)(2,1)}, bf16[3,256,1536]{2,1,0:T(8,128)(2,1)}, u32[]{:S(2)}, u32[]{:S(2)}) collective-permute-start(bf16[3,256,1536]{2,1,0:T(8,128)(2,1)} %collective-permute-done.23.refs_11_.refs_3_.refs_4_.refs_2_), channel_id=1, source_target_pairs={{0,4},{4,0},{8,12},{12,8},{16,20},{20,16},{24,28},{28,24},{1,5},{5... | collective-permute-start | bytes 7077896 | tf_op jit(solution)/shard_map/ppermute | solution.py:85
  467.1 25.2 %collective-permute-start.32 = (bf16[3,256,1536]{2,1,0:T(8,128)(2,1)}, bf16[3,256,1536]{2,1,0:T(8,128)(2,1)}, u32[]{:S(2)}, u32[]{:S(2)}) collective-permute-start(bf16[3,256,1536]{2,1,0:T(8,128)(2,1)} %collective-permute-done.24.refs_13_.refs_7_.refs_8_.refs_4_), channel_id=1, source_target_pairs={{0,4},{4,0},{8,12},{12,8},{16,20},{20,16},{24,28},{28,24},{1,5},{5... | collective-permute-start | bytes 7077896 | tf_op jit(solution)/shard_map/ppermute | solution.py:85
  487.6 19.9 %collective-permute-start.28 = (bf16[1,256,1536]{2,1,0:T(8,128)(2,1)}, bf16[1,256,1536]{2,1,0:T(8,128)(2,1)S(1)}, u32[]{:S(2)}, u32[]{:S(2)}) collective-permute-start(bf16[1,256,1536]{2,1,0:T(8,128)(2,1)} %get-tuple-element.97), channel_id=1, source_target_pairs={{0,16},{4,20},{8,24},{12,28},{16,0},{20,4},{24,8},{28,12},{1,17},{... | collective-permute-start | bytes 2359304 | tf_op jit(solution)/shard_map/ppermute | solution.py:85
  490.5 19.5 %collective-permute-start.27 = (bf16[1,256,1536]{2,1,0:T(8,128)(2,1)}, bf16[1,256,1536]{2,1,0:T(8,128)(2,1)S(1)}, u32[]{:S(2)}, u32[]{:S(2)}) collective-permute-start(bf16[1,256,1536]{2,1,0:T(8,128)(2,1)} %get-tuple-element.95.refs_17_), channel_id=1, source_target_pairs={{0,8},{4,12},{8,0},{12,4},{16,24},{20,28},{24,16},{28,20},{1,9},{5... | collective-permute-start | bytes 2359304 | tf_op jit(solution)/shard_map/ppermute | solution.py:85
  539.1 18.7 %collective-permute-start.41 = (bf16[1,256,1536]{2,1,0:T(8,128)(2,1)S(1)}, bf16[1,256,1536]{2,1,0:T(8,128)(2,1)S(1)}, u32[]{:S(2)}, u32[]{:S(2)}) collective-permute-start(bf16[1,256,1536]{2,1,0:T(8,128)(2,1)S(1)} %maximum_select_fusion.2.refs_1_), channel_id=1, source_target_pairs={{0,8},{4,12},{8,0},{12,4},{16,24},{20,28},{24,16},{28,20},{1,9},{5... | collective-permute-start | bytes 2359304 | tf_op jit(solution)/shard_map/ppermute | solution.py:85
  541.5 16.4 %collective-permute-start.43 = (bf16[1,256,1536]{2,1,0:T(8,128)(2,1)S(1)}, bf16[1,256,1536]{2,1,0:T(8,128)(2,1)S(1)}, u32[]{:S(2)}, u32[]{:S(2)}) collective-permute-start(bf16[1,256,1536]{2,1,0:T(8,128)(2,1)S(1)} %maximum_select_fusion.3.refs_3_), channel_id=1, source_target_pairs={{0,16},{4,20},{8,24},{12,28},{16,0},{20,4},{24,8},{28,12},{1,17},{... | collective-permute-start | bytes 2359304 | tf_op jit(solution)/shard_map/ppermute | solution.py:85
  (66 other events, 669.3 us)
Sparse Core Ops, SparseCore 0:
  10.2 48.6 all-gather.4
  60.4 44.6 all-gather.6
  110.4 49.6 reduce-scatter.4
  162.8 45.2 all-gather.8
  236.1 42.6 reduce-scatter.6
  310.1 44.8 all-gather.10
  357.9 42.5 reduce-scatter.8
  466.5 43.0 reduce-scatter.10

commit v4 on v3

--- a/solution.py
+++ b/solution.py
@@ -46,14 +46,15 @@
     return pltpu.with_memory_space_constraint(value, pltpu.HBM)
 
 
-def call(body, grid, in_specs, out_specs, out_shape, scratch, operands, mib, prefetch=1, after=(), aliases={}):
+def call(body, grid, in_specs, out_specs, out_shape, scratch, operands, mib, prefetch=1, after=(), free=False, aliases={}):
     after = (*ORDER, *after)
     at, extra = prefetch + len(in_specs), len(after)
 
     def run(*refs):
         return body(*refs[:at], *refs[at + extra :])
 
-    operands = operands[:prefetch] + tuple(in_hbm(v) for v in operands[prefetch:])
+    if not free:
+        operands = operands[:prefetch] + tuple(in_hbm(v) for v in operands[prefetch:])
     outs = pl.pallas_call(
         run,
         grid_spec=pltpu.PrefetchScalarGridSpec(
@@ -85,6 +86,18 @@
     return lax.ppermute(value, axis, flip(axis, mask))
 
 
+def sum_copies(value, axis, masks):
+    while masks:
+        if len(masks) % 2:
+            value = value + swap(value, axis, masks[0])
+            masks = masks[1:]
+        else:
+            a, b = masks[:2]
+            value = (value + swap(value, axis, a)) + (swap(value, axis, b) + swap(value, axis, a | b))
+            masks = masks[2:]
+    return value
+
+
 def gather_tp(share):
     rows, _, width = share.shape
     return lax.all_gather(share, "tp", axis=1, tiled=True).reshape(-1, width)
@@ -552,6 +565,7 @@
         [pltpu.VMEM((2, count * part, 2 * tokens), BF)],
         (ids, *ogs, *xs, *planes),
         48,
+        free=True,
     )
 
 
@@ -659,9 +673,10 @@
         [pl.BlockSpec(block, lambda j, bits: (0, j, 0))] * 2,
         [hbm((planes, rows, cols), BF)] * 2,
         [],
-        (bits, *flows[0], *flows[1]),
+        (bits, *(v for f in flows for v in (*(in_hbm(k) for k in f[:-1]), f[-1]))),
         40,
         after=after,
+        free=True,
     )
 
 
@@ -678,21 +693,24 @@
         [],
         (bits, keeps[0], gots[0], keeps[1], gots[1]),
         40,
-    )
-
-
-def widen_kernel(count, planes, turned, table, *refs):
-    pieces, outs = refs[: count * planes], refs[count * planes :]
-
-    def put(refs):
+        free=planes == 1,
+    )
+
+
+def widen_kernel(count, size, planes, turned, onto, table, *refs):
+    pieces, outs = refs[: count * size * planes], refs[count * size * planes + onto :]
+
+    def put(refs, at_row):
+        rows = refs[0].shape[1]
+        at_row = slice(None) if size == 1 else pl.ds(pl.multiple_of(at_row * rows, rows), rows)
         at, plane = 0, 0
         for k, out in enumerate(outs):
+            wide = out.shape[0 if k in turned else 1]
+            value = refs[plane][0, :, at : at + wide]
             if k in turned:
-                wide = out.shape[0]
-                out[...] = refs[plane][0, :, at : at + wide].T.astype(F32)
+                out[:, at_row] = value.T.astype(F32)
             else:
-                wide = out.shape[1]
-                out[...] = refs[plane][0, :, at : at + wide].astype(F32)
+                out[at_row, :] = value.astype(F32)
             at += wide
             if at == refs[plane].shape[2]:
                 at, plane = 0, plane + 1
@@ -701,25 +719,49 @@
 
         @pl.when(pl.program_id(0) == k)
         def _(k=k):
-            put(pieces[k * planes : (k + 1) * planes])
-
-
-def widen_call(table, pieces, planes, shapes, turned, after):
-    _, rows, cols = pieces[0].shape
-    count = len(pieces)
+            for n in range(k * size, (k + 1) * size):
+                put(pieces[n * planes : (n + 1) * planes], table[count + n])
+
+
+def widen_call(blocks, spots, groups, planes, shapes, turned, onto, after):
+    count, size = len(groups), len(groups[0])
+    _, rows, cols = groups[0][0].shape
     place = lambda n: pl.BlockSpec((1, rows, cols), lambda j, t: (n, 0, 0), pipeline_mode=pl.Buffered(1))
-    by_row = lambda s: pl.BlockSpec((rows, s[1]), lambda j, t: (t[j], 0))
-    by_col = lambda s: pl.BlockSpec((s[0], rows), lambda j, t: (0, t[j]))
-    return call(
-        functools.partial(widen_kernel, count, len(planes), turned),
+    by_row = lambda s: pl.BlockSpec((size * rows, s[1]), lambda j, t: (t[j], 0))
+    by_col = lambda s: pl.BlockSpec((s[0], size * rows), lambda j, t: (0, t[j]))
+    return call(
+        functools.partial(widen_kernel, count, size, len(planes), turned, len(onto)),
         (count,),
-        [place(n) for _ in range(count) for n in planes],
+        [place(n) for _ in range(count * size) for n in planes] + [pl.BlockSpec(memory_space=pl.ANY)] * len(onto),
         [by_col(s) if k in turned else by_row(s) for k, s in enumerate(shapes)],
         [hbm(s, F32) for s in shapes],
         [],
-        (table, *(p for p in pieces for _ in planes)),
+        (jnp.concatenate([blocks, spots]), *(p for g in groups for p in g for _ in planes), *onto),
         56,
         after=after,
+        free=True,
+        aliases={1 + count * size * len(planes) + k: k for k in range(len(onto))},
+    )
+
+
+def hold_kernel(a, b, a_out, b_out):
+    a_out[...] = a[...]
+    b_out[...] = b[...]
+
+
+def hold_call(values):
+    planes, rows, cols = values[0].shape
+    block = pl.BlockSpec((1, rows, cols), lambda j: (j, 0, 0))
+    return call(
+        hold_kernel,
+        (planes,),
+        [block] * 2,
+        [block] * 2,
+        [hbm(values[0].shape, BF)] * 2,
+        [],
+        tuple(values),
+        24,
+        prefetch=0,
     )
 
 
@@ -833,14 +875,37 @@
                 jnp.where(self.bits[level][f] == 0, *(jnp.concatenate(v, axis=1) for v in ((p, g), (g, p))))
                 for f, (p, g) in enumerate(zip(parts, gots))
             ]
-        self.parts = parts
-        self.ends = [v for p, m in zip(parts, self.flows) for v in (p, swap(p, "seq", m[0]))]
-        self.others = [swap(v, "seq", 1) for v in self.ends]
-
-    def widen(self, planes, shapes, turned, after=()):
+        self.parts, self.spots = parts, jnp.zeros((8,), I32)
+        ends = [v for p, m in zip(parts, self.flows) for v in (p, swap(p, "seq", m[0]))]
+        self.groups = [(v,) for v in (*ends, *(self.other(v) for v in ends))]
+        self.soon = ends
+
+    def other(self, value):
+        return swap(value, "seq", 1)
+
+    def last_in_pieces(self):
+        self.own = sum_call(self.bits[-1], self.terms)
+        self.near = [swap(p, "seq", m[1]) for p, m in zip(self.own, self.flows)]
+        self.parts = [self.other(v) for v in (*self.own, *self.near)]
+        self.far = [swap(p, "seq", m[0]) for p, m in zip(self.own, self.flows)]
+        self.soon = [self.other(v) for v in self.far]
+
+    def finish(self):
+        last = [swap(p, "seq", m[0]) for p, m in zip(hold_call(self.near), self.flows)]
+        own, other = [], []
+        for f in range(2):
+            own += [(self.own[f], self.near[f]), (self.far[f], last[f])]
+            other += [(self.parts[f], self.parts[2 + f]), (self.soon[f], self.other(last[f]))]
+        self.groups = own + other
+        spots = jnp.stack([s for b in self.bits[1] for s in (b, 1 - b, b, 1 - b)])
+        self.spots = jnp.concatenate([spots, spots])
+
+    def widen(self, planes, shapes, turned, early=False, onto=(), after=()):
         blocks = jnp.stack([h for f in range(2) for h in (2 * f + self.bits[0][f], 2 * f + 1 - self.bits[0][f])])
         table = jnp.concatenate([self.core * 4 + blocks, (1 - self.core) * 4 + blocks])
-        return widen_call(table, (*self.ends, *self.others), planes, shapes, turned, after)
+        half = slice(None) if not early and not onto else slice(0 if early else 1, None, 2)
+        spots = self.spots.reshape(8, -1)[half].reshape(-1)
+        return widen_call(table[half], spots, self.groups[half], planes, shapes, turned, tuple(onto), after)
 
 
 def halves(value, core):
@@ -931,7 +996,11 @@
     branch = gather_tp(shares(branch))
     ff.middle()
     ff_got = scatter_tp(ff_out_call(planes, down_weight), row_count)
-    ff.last()
+    in_pieces = len(masks) == 2
+    if in_pieces:
+        ff.last_in_pieces()
+    else:
+        ff.last()
     dq, even, odd_low, odd_high, q_gain_grad, b_keep, b_send = attend_back_call(
         meta,
         docs,
@@ -950,33 +1019,34 @@
     chip = [(even[k].astype(F32) + odd[k].astype(F32)).astype(BF) for k in range(seqs // 2)]
     pieces = [chip[0]] + [swap(chip[m // 2], "seq", m) for m in range(2, seqs, 2)]
     bg_both = both(b_keep, b_send)
-    all_grad, k_gain_grad = key_back_call(pieces, dq, k_raw, k_gain, tables, (*ff.ends, ff_got, bg_both[1]))
+    all_grad, k_gain_grad = key_back_call(pieces, dq, k_raw, k_gain, tables, (*ff.soon, ff_got, bg_both[1]))
     all_both = both(all_grad)
-    n1_part = back_call(all_grad, qkv_weights)
-    n1_got = scatter_tp(n1_part, row_count)
+    n1_got = scatter_tp(back_call(all_grad, qkv_weights), row_count)
+    if in_pieces:
+        ff.finish()
     attn = WeightSum(masks)
     ids = jnp.concatenate([attn.send_ids, attn.keep_ids])
     parts = attn_grad_call(ids, n1_both, bg_both, all_both, o_both)
     attn.kept = parts[2:]
     attn.begin(parts[:2])
-    gate_out, up_out = ff.widen((1, 2), [gate_weight.shape, up_weight.shape], ())
+    gate_up = ((1, 2), [gate_weight.shape, up_weight.shape], ())
+    down = ((0,), [down_weight.shape], (0,))
+    attend = ((0,), [w.shape for w in (*qkv_weights, output_weight)], (3,))
+    gate_up_out, down_out = ff.widen(*gate_up, early=True), ff.widen(*down, early=True)
     attn.middle()
     input_grad, attn_gain_grad = norm_grad_call(hidden, flat(n1_got), middle_grad, attn_gain, False)
     gains = jnp.concatenate(
         [v.reshape(-1) for v in (attn_gain_grad, ff_gain_grad, q_gain_grad, k_gain_grad)]
     ).reshape(-1, HEAD)
-    sums = [gains]
-    for axis, size in (("tp", tp), ("seq", seqs)):
-        for level in range(size.bit_length() - 1):
-            sums.append(sums[-1] + swap(sums[-1], axis, 1 << level))
-    gains = sums[-1]
+    gains = sum_copies(gains, "tp", [1 << level for level in range(tp.bit_length() - 1)])
+    for level in range(seqs.bit_length() - 1):
+        gains = sum_copies(gains, "seq", [1 << level])
     input_grad = shares(input_grad)
     block_out = shares((middle + flat(ff_got).astype(F32)).astype(BF))
+    gate_out, up_out = ff.widen(*gate_up, onto=gate_up_out)
     attn.last()
-    (down_out,) = ff.widen((0,), [down_weight.shape], (0,))
-    query_out, key_out, value_out, output_out = attn.widen(
-        (0,), [w.shape for w in (*qkv_weights, output_weight)], (3,), sums[-1:]
-    )
+    (down_out,) = ff.widen(*down, onto=down_out)
+    query_out, key_out, value_out, output_out = attn.widen(*attend)
     gains = gains.reshape(-1)
     return (
         block_out,

time: 598 us -> 587 us (0.982)
  other arithmetic: 18 us -> 11.7 us
  Pallas kernels: 173 us -> 179 us
    ppermute x48 -> x55, waiting for transfers between devices: 179 us -> 170 us  [swap(): return lax.ppermute(value, axis, flip(axis, mask))]
    pallas_call x22 -> x25, Pallas kernels: 173 us -> 179 us  [call(): pl.pallas_call(run, grid_spec=pltpu.PrefetchScalarGridSpec(num_scalar_pre...]
    ppermute x48 -> x55, starting transfers between devices: 43.7 us -> 41.2 us  [swap(): return lax.ppermute(value, axis, flip(axis, mask))]
  transfers between devices with their start and end apart: 56 -> 63, of which waited for: 31 -> 32; matrix products, arithmetic and copies ran while one was open for 4% -> 3% of each run, Pallas kernels for 21% -> 23%
where the time goes in v4:
time: 587 us; the launch traced here: 580 us
  waiting for transfers between devices  323 us (55%)
  Pallas kernels  179 us (30%)
  starting transfers between devices  41.9 us (7%)
  between operations  15.1 us (3%)
  other arithmetic  11.7 us (2%)
  local copies, waits for them, and re-layouts  9.17 us (2%)
    pallas_call x25, Pallas kernels, call(): pl.pallas_call(run, grid_spec=pltpu.PrefetchScalarGridSpec(num_scalar_pre...  179 us
    ppermute x55, waiting for transfers between devices, swap(): return lax.ppermute(value, axis, flip(axis, mask))  170 us
    all_gather x4, waiting for transfers between devices, gather_tp(): return lax.all_gather(share, 'tp', axis=1, tiled=True).reshape(-1, width)  85.9 us
    reduce_scatter x4, waiting for transfers between devices, scatter_tp(): return lax.psum_scatter(part, 'tp', scatter_dimension=1, tiled=True)  65.8 us
    ppermute x55, starting transfers between devices, swap(): return lax.ppermute(value, axis, flip(axis, mask))  41.2 us
  transfers between devices with their start and end apart: 63, of which 32 were waited for; matrix products, arithmetic and copies ran while one was open for 3% of the time, Pallas kernels for 23%

profile of v4, /device:TPU:0, one launch (start us, length us, event | category | flops | bytes accessed | tf_op | source)
XLA Modules:
  0.0 579.6 jit_solution(2500636064073164912)
XLA Ops:
  12.9 45.9 %all-gather.5.cloned.1.call-done = bf16[2,256,2048]{2,1,0:T(8,128)(2,1)} async-done(((bf16[2,64,2048]{2,1,0:T(8,128)(2,1)}), bf16[2,256,2048]{2,1,0:T(8,128)(2,1)}) %all-gather.5.cloned.1.call-update) | async-done | bytes 2097168 | tf_op jit(solution)/shard_map/all_gather | solution.py:103
  58.8 9.3 %shard_map.256 = (bf16[512,512]{1,0:T(8,128)(2,1)}, bf16[2,2,256,256]{3,2,1,0:T(8,128)(2,1)}, f32[512,512]{1,0:T(8,128)}, f32[512,256]{1,0:T(8,128)}, bf16[512,1...) custom-call(s32[1]{0:T(128)} %bitcast.4.refs_0_, bf16[512,2048]{1,0:T(8,128)(2,1)} %bitcast.77, bf16[2048,512]{1,0:T(8,128)(2,1)} %refs_1_.3, ...), custom_call_target="tpu_custom_call" | custom-call | flops 1 | bytes 1 | tf_op jit(solution)/shard_map/pallas_call | solution.py:58
  72.2 11.9 %collective-permute-done.5.refs_8_.refs_10_ = bf16[2,2,256,256]{3,2,1,0:T(8,128)(2,1)S(1)} collective-permute-done((bf16[2,2,256,256]{3,2,1,0:T(8,128)(2,1)}, bf16[2,2,256,256]{3,2,1,0:T(8,128)(2,1)S(1)}, u32[]{:S(2)}, u32[]{:S(2)}) %collective-permute-start.5) | collective-permute-done | bytes 524320 | tf_op jit(solution)/shard_map/ppermute | solution.py:86
  84.1 10.0 %collective-permute-done.3.refs_6_.refs_8_ = bf16[2,2,256,256]{3,2,1,0:T(8,128)(2,1)S(1)} collective-permute-done((bf16[2,2,256,256]{3,2,1,0:T(8,128)(2,1)}, bf16[2,2,256,256]{3,2,1,0:T(8,128)(2,1)S(1)}, u32[]{:S(2)}, u32[]{:S(2)}) %collective-permute-start.3) | collective-permute-done | bytes 524320 | tf_op jit(solution)/shard_map/ppermute | solution.py:86
  97.0 13.3 %shard_map.257 = (bf16[512,512]{1,0:T(8,128)(2,1)}, f32[2,2,512,1]{3,2,1,0:T(8,128)}, bf16[512,2048]{1,0:T(8,128)(2,1)}) custom-call(s32[34]{0:T(128)S(1)} %concatenate.80.refs_0_, bf16[512,512]{1,0:T(8,128)(2,1)} %get-tuple-element.67.refs_1_.refs_11_.refs_3_, bf16[2,2,256,256]{3,2,1,0:T(8,128)(2,1)} %get-tuple-element.68.refs_2_.refs_4_, ...), custom_call_target="tpu_custom_call" | custom-call | flops 1 | bytes 1 | tf_op jit(solution)/shard_map/pallas_call | solution.py:58
  110.3 51.4 %reduce-scatter.5.cloned.1.call-done = bf16[2,64,2048]{2,1,0:T(8,128)(2,1)} async-done(((bf16[2,256,2048]{2,1,0:T(8,128)(2,1)}), bf16[2,64,2048]{2,1,0:T(8,128)(2,1)}) %reduce-scatter.5.cloned.1.call-update) | async-done | bytes 524304 | tf_op jit(solution)/shard_map/reduce_scatter | solution.py:108
  169.9 40.0 %all-gather.9.cloned.1.call-done = bf16[2,256,2048]{2,1,0:T(8,128)(2,1)} async-done(((bf16[2,64,2048]{2,1,0:T(8,128)(2,1)}), bf16[2,256,2048]{2,1,0:T(8,128)(2,1)}) %all-gather.9.cloned.1.call-update) | async-done | bytes 2097168 | tf_op jit(solution)/shard_map/all_gather | solution.py:103
  209.9 16.5 %shard_map.259 = (bf16[3,512,1536]{2,1,0:T(8,128)(2,1)}, bf16[512,1024]{1,0:T(8,128)(2,1)}, bf16[512,1024]{1,0:T(8,128)(2,1)}) custom-call(s32[1]{0:T(128)} %bitcast.4.refs_0_, bf16[512,2048]{1,0:T(8,128)(2,1)} %bitcast.75, bf16[512,2048]{1,0:T(8,128)(2,1)} %bitcast.65, bf16[2048,1536]{1,0:T(8,128)(2,1)} %refs_2_.5, bf16[2048,1536]{1,0:T(8,128)(2,1)} %refs_3_.6, ...), custom_call_target="tpu_custom_call" | custom-call | flops 1 | bytes 1 | tf_op jit(solution)/shard_map/pallas_call | solution.py:58
  226.4 11.3 %shard_map.260.refs_7_ = bf16[512,2048]{1,0:T(8,128)(2,1)} custom-call(bf16[3,512,1536]{2,1,0:T(8,128)(2,1)} %get-tuple-element.74.refs_0_.refs_1_.refs_4_.refs_5_, bf16[3,512,1536]{2,1,0:T(8,128)(2,1)} %get-tuple-element.74.refs_0_.refs_1_.refs_4_.refs_5_, bf16[2048,1536]{1,0:T(8,128)(2,1)} %refs_2_.5, bf16[2048,1536]{1,0:T(8,128)(2,1)} %refs_3_.6, ...), custom_call_target="tpu_custom_call" | custom-call | flops 1 | bytes 1 | tf_op jit(solution)/shard_map/pallas_call | solution.py:58
  240.9 11.3 %shard_map.261 = (bf16[3,256,1536]{2,1,0:T(8,128)(2,1)}, bf16[3,256,1536]{2,1,0:T(8,128)(2,1)}) custom-call(s32[2]{0:T(128)S(1)} %get-tuple-element.144.refs_0_, bf16[512,1024]{1,0:T(8,128)(2,1)S(1)} %get-tuple-element.131.refs_1_, bf16[512,1024]{1,0:T(8,128)(2,1)S(1)} %copy-done.1, bf16[512,1024]{1,0:T(8,128)(2,1)S(1)} %copy-done.2, ...), custom_call_target="tpu_custom_call" | custom-call | flops 1 | bytes 1 | tf_op jit(solution)/shard_map/pallas_call | solution.py:58
  255.2 11.0 %shard_map.262 = (bf16[3,256,1536]{2,1,0:T(8,128)(2,1)}, bf16[3,256,1536]{2,1,0:T(8,128)(2,1)}) custom-call(s32[2]{0:T(128)S(1)} %get-tuple-element.145.refs_0_, bf16[512,1024]{1,0:T(8,128)(2,1)S(1)} %get-tuple-element.131.refs_1_, bf16[512,1024]{1,0:T(8,128)(2,1)S(1)} %copy-done.1, bf16[512,1024]{1,0:T(8,128)(2,1)S(1)} %copy-done.2, ...), custom_call_target="tpu_custom_call" | custom-call | flops 1 | bytes 1 | tf_op jit(solution)/shard_map/pallas_call | solution.py:58
  266.1 14.4 %reduce-scatter.7.cloned.1.call-done = bf16[2,64,2048]{2,1,0:T(8,128)(2,1)} async-done(((bf16[2,256,2048]{2,1,0:T(8,128)(2,1)}), bf16[2,64,2048]{2,1,0:T(8,128)(2,1)}) %reduce-scatter.7.cloned.1.call-update) | async-done | bytes 524304 | tf_op jit(solution)/shard_map/reduce_scatter | solution.py:108
  280.5 25.6 %collective-permute-done.13.refs_6_.refs_4_.refs_5_ = bf16[3,256,1536]{2,1,0:T(8,128)(2,1)} collective-permute-done((bf16[3,256,1536]{2,1,0:T(8,128)(2,1)}, bf16[3,256,1536]{2,1,0:T(8,128)(2,1)}, u32[]{:S(2)}, u32[]{:S(2)}) %collective-permute-start.13) | collective-permute-done | bytes 2359328 | tf_op jit(solution)/shard_map/ppermute | solution.py:86
  317.2 7.4 %shard_map.265.refs_7_ = bf16[512,2048]{1,0:T(8,128)(2,1)} custom-call(bf16[3,512,1536]{2,1,0:T(8,128)(2,1)} %get-tuple-element.74.refs_0_.refs_1_.refs_4_.refs_5_, bf16[1536,2048]{1,0:T(8,128)(2,1)} %refs_1_.2, bf16[3,128,1536]{2,1,0:T(8,128)(2,1)} %get-tuple-element.82.refs_2_), custom_call_target="tpu_custom_call" | custom-call | flops 1 | bytes 1 | tf_op jit(solution)/shard_map/pallas_call | solution.py:58
  324.6 18.0 %collective-permute-done.15.refs_6_ = bf16[3,128,1536]{2,1,0:T(8,128)(2,1)S(1)} collective-permute-done((bf16[3,128,1536]{2,1,0:T(8,128)(2,1)}, bf16[3,128,1536]{2,1,0:T(8,128)(2,1)S(1)}, u32[]{:S(2)}, u32[]{:S(2)}) %collective-permute-start.15) | collective-permute-done | bytes 1179680 | tf_op jit(solution)/shard_map/ppermute | solution.py:86
  343.8 4.4 shard_map.266
  350.2 24.4 %collective-permute-done.20.refs_1_.refs_7_.refs_8_.refs_4_ = bf16[3,128,1536]{2,1,0:T(8,128)(2,1)} collective-permute-done((bf16[3,128,1536]{2,1,0:T(8,128)(2,1)}, bf16[3,128,1536]{2,1,0:T(8,128)(2,1)}, u32[]{:S(2)}, u32[]{:S(2)}) %collective-permute-start.20) | collective-permute-done | bytes 1179680 | tf_op jit(solution)/shard_map/ppermute | solution.py:86
  379.5 12.7 %shard_map.267 = (bf16[512,512]{1,0:T(8,128)(2,1)}, bf16[4,2,2,256,256]{4,3,2,1,0:T(8,128)(2,1)}, bf16[2,2,2,256,256]{4,3,2,1,0:T(8,128)(2,1)}, bf16[2,2,2,256,2...) custom-call(s32[34]{0:T(128)S(1)} %concatenate.80.refs_0_, ...), custom_call_target="tpu_custom_call" | custom-call | flops 1 | bytes 1 | tf_op jit(solution)/shard_map/pallas_call | solution.py:58
  395.1 8.5 %collective-permute-done.29.refs_5_.refs_6_.refs_3_ = bf16[3,128,1536]{2,1,0:T(8,128)(2,1)} collective-permute-done((bf16[3,128,1536]{2,1,0:T(8,128)(2,1)}, bf16[3,128,1536]{2,1,0:T(8,128)(2,1)}, u32[]{:S(2)}, u32[]{:S(2)}) %collective-permute-start.29) | collective-permute-done | bytes 1179680 | tf_op jit(solution)/shard_map/ppermute | solution.py:86
  407.6 7.6 %collective-permute-start.26 = (bf16[2,2,256,256]{3,2,1,0:T(8,128)(2,1)}, bf16[2,2,256,256]{3,2,1,0:T(8,128)(2,1)}, u32[]{:S(2)}, u32[]{:S(2)}) collective-permute-start(bf16[2,2,256,256]{3,2,1,0:T(8,128)(2,1)} %get-tuple-element.125), channel_id=1, source_target_pairs={{0,24},{4,28},{8,16},{12,20},{16,8},{20,12},{24,0},{28,4},{1,25},{... | collective-permute-start | bytes 1572872 | tf_op jit(solution)/shard_map/ppermute | solution.py:86
  415.8 12.5 %collective-permute-done.26.refs_3_ = bf16[2,2,256,256]{3,2,1,0:T(8,128)(2,1)} collective-permute-done((bf16[2,2,256,256]{3,2,1,0:T(8,128)(2,1)}, bf16[2,2,256,256]{3,2,1,0:T(8,128)(2,1)}, u32[]{:S(2)}, u32[]{:S(2)}) %collective-permute-start.26) | collective-permute-done | bytes 524320 | tf_op jit(solution)/shard_map/ppermute | solution.py:86
  428.3 10.9 %collective-permute-done.25.refs_2_ = bf16[2,2,256,256]{3,2,1,0:T(8,128)(2,1)} collective-permute-done((bf16[2,2,256,256]{3,2,1,0:T(8,128)(2,1)}, bf16[2,2,256,256]{3,2,1,0:T(8,128)(2,1)}, u32[]{:S(2)}, u32[]{:S(2)}) %collective-permute-start.25) | collective-permute-done | bytes 524320 | tf_op jit(solution)/shard_map/ppermute | solution.py:86
  443.0 6.2 %shard_map.269.refs_2_ = bf16[512,2048]{1,0:T(8,128)(2,1)} custom-call(bf16[512,1024]{1,0:T(8,128)(2,1)} %get-tuple-element.95.refs_0_.refs_4_.refs_5_, bf16[2048,512]{1,0:T(8,128)(2,1)} %refs_1_.3, bf16[2048,256]{1,0:T(8,128)(2,1)} %refs_2_.7, bf16[2048,256]{1,0:T(8,128)(2,1)} %refs_3_.7, bf16[512,1024]{1,0:T(8,128)(2,1)} %get-tuple-element.95.refs_0_.refs_4_.refs_5_), custom_call_target="tpu_custom_call" | custom-call | flops 1 | bytes 1 | tf_op jit(solution)/shard_map/pallas_call | solution.py:58
  459.1 10.1 %shard_map.271 = (bf16[1,256,1536]{2,1,0:T(8,128)(2,1)}, bf16[1,256,1536]{2,1,0:T(8,128)(2,1)}, bf16[1,256,1536]{2,1,0:T(8,128)(2,1)}, bf16[1,256,1536]{2,1,0:T(8,128)(2,1)}) custom-call(s32[4]{0:T(128)S(1)} %pad_add_fusion.3.refs_0_, bf16[512,1024]{1,0:T(8,128)(2,1)} %get-tuple-element.96.refs_1_, bf16[512,1024]{1,0:T(8,128)(2,1)} %copy-done.16, ...), custom_call_target="tpu_custom_call" | custom-call | flops 1 | bytes 1 | tf_op jit(solution)/shard_map/pallas_call | solution.py:58
  471.0 11.3 %collective-permute-done.44.refs_7_.refs_8_.refs_4_ = bf16[3,128,1536]{2,1,0:T(8,128)(2,1)} collective-permute-done((bf16[3,128,1536]{2,1,0:T(8,128)(2,1)}, bf16[3,128,1536]{2,1,0:T(8,128)(2,1)}, u32[]{:S(2)}, u32[]{:S(2)}) %collective-permute-start.44) | collective-permute-done | bytes 1179680 | tf_op jit(solution)/shard_map/ppermute | solution.py:86
  484.1 8.3 %shard_map.272 = (f32[2048,1536]{1,0:T(8,128)}, f32[2048,1536]{1,0:T(8,128)}) custom-call(s32[12]{0:T(128)} %pad_add_fusion.6.refs_0_, bf16[3,128,1536]{2,1,0:T(8,128)(2,1)} %get-tuple-element.87.refs_18_.refs_1_.refs_2_, bf16[3,128,1536]{2,1,0:T(8,128)(2,1)} %get-tuple-element.87.refs_18_.refs_1_.refs_2_, ...), custom_call_target="tpu_custom_call" | custom-call | flops 1 | bytes 1 | tf_op jit(solution)/shard_map/pallas_call | solution.py:58
  492.4 6.0 %shard_map.273.refs_5_.refs_9_ = f32[1536,2048]{1,0:T(8,128)} custom-call(s32[12]{0:T(128)} %pad_add_fusion.6.refs_0_, bf16[3,128,1536]{2,1,0:T(8,128)(2,1)} %get-tuple-element.87.refs_18_.refs_1_.refs_2_, bf16[3,128,1536]{2,1,0:T(8,128)(2,1)} %collective-permute-done.18.refs_0_.refs_3_.refs_4_.refs_2_, ...), custom_call_target="tpu_custom_call" | custom-call | flops 1 | bytes 1 | tf_op jit(solution)/shard_map/pallas_call | solution.py:58
  508.2 8.3 %shard_map.276 = (f32[2048,1536]{1,0:T(8,128)}, f32[2048,1536]{1,0:T(8,128)}) custom-call(s32[12]{0:T(128)} %pad_add_fusion.8.refs_0_, bf16[3,128,1536]{2,1,0:T(8,128)(2,1)} %collective-permute-done.27.refs_1_.refs_2_, bf16[3,128,1536]{2,1,0:T(8,128)(2,1)} %collective-permute-done.27.refs_1_.refs_2_, ...), custom_call_target="tpu_custom_call", output_to_operand_aliasing={{0}: (17, {}), {1}: (18, {})} | custom-call | flops 1 | bytes 1 | tf_op jit(solution)/shard_map/pallas_call | solution.py:58
  520.3 10.4 %collective-permute-done.47 = bf16[1,128,1536]{2,1,0:T(8,128)(2,1)S(1)} collective-permute-done((bf16[1,128,1536]{2,1,0:T(8,128)(2,1)}, bf16[1,128,1536]{2,1,0:T(8,128)(2,1)S(1)}, u32[]{:S(2)}, u32[]{:S(2)}) %collective-permute-start.47) | collective-permute-done | bytes 393248 | tf_op jit(solution)/shard_map/ppermute | solution.py:86
  544.2 6.9 %collective-permute-done.39 = f32[34,128]{1,0:T(8,128)S(1)} collective-permute-done((f32[34,128]{1,0:T(8,128)S(1)}, f32[34,128]{1,0:T(8,128)S(1)}, u32[]{:S(2)}, u32[]{:S(2)}) %collective-permute-start.39) | collective-permute-done | bytes 17440 | tf_op jit(solution)/shard_map/ppermute | solution.py:86
  553.7 5.9 %shard_map.278.refs_9_ = f32[1536,2048]{1,0:T(8,128)} custom-call(s32[12]{0:T(128)} %pad_add_fusion.8.refs_0_, bf16[3,128,1536]{2,1,0:T(8,128)(2,1)} %collective-permute-done.27.refs_1_.refs_2_, bf16[3,128,1536]{2,1,0:T(8,128)(2,1)} %collective-permute-done.43.refs_3_.refs_4_.refs_2_, ...), custom_call_target="tpu_custom_call", output_to_operand_aliasing={{}: (9, {})} | custom-call | flops 1 | bytes 1 | tf_op jit(solution)/shard_map/pallas_call | solution.py:58
  563.1 9.2 %shard_map.279 = (f32[2048,512]{1,0:T(8,128)}, f32[2048,256]{1,0:T(8,128)}, f32[2048,256]{1,0:T(8,128)}, f32[512,2048]{1,0:T(8,128)}) custom-call(s32[16]{0:T(128)} %pad_add_fusion.7.refs_0_, bf16[1,256,1536]{2,1,0:T(8,128)(2,1)} %copy-done.18, bf16[1,256,1536]{2,1,0:T(8,128)(2,1)} %copy-done.28, bf16[1,256,1536]{2,1,0:T(8,128)(2,1)} %copy-done.19, ...), custom_call_target="tpu_custom_call" | custom-call | flops 1 | bytes 1 | tf_op jit(solution)/shard_map/pallas_call | solution.py:58
  (259 shorter events, 103.8 us)
Async XLA Ops:
  7.2 51.7 %all-gather.5.cloned.1.call-start = ((), (), s32[]{:S(2)}) async-start(), calls=%async_computation.4 | async-start | bytes 2621440 | tf_op jit(solution)/shard_map/all_gather | solution.py:103
  9.3 101.0 %all-gather.7.cloned.1.call-start = ((), (), s32[]{:S(2)}) async-start(), calls=%async_computation.6 | async-start | bytes 2621440 | tf_op jit(solution)/shard_map/all_gather | solution.py:103
  10.1 151.7 %reduce-scatter.5.cloned.1.call-start = ((), (), s32[]{:S(2)}) async-start(), calls=%async_computation.5 | async-start | bytes 2621440 | tf_op jit(solution)/shard_map/reduce_scatter | solution.py:108
  70.5 23.6 %collective-permute-start.3 = (bf16[2,2,256,256]{3,2,1,0:T(8,128)(2,1)}, bf16[2,2,256,256]{3,2,1,0:T(8,128)(2,1)S(1)}, u32[]{:S(2)}, u32[]{:S(2)}) collective-permute-start(bf16[2,2,256,256]{3,2,1,0:T(8,128)(2,1)} %get-tuple-element.68.refs_2_.refs_4_), channel_id=1, source_target_pairs={{0,16},{4,20},{8,24},{12,28},{16,0},{20,4},{24,8},{28,12},{1,17},{... | collective-permute-start | bytes 1572872 | tf_op jit(solution)/shard_map/ppermute | solution.py:86
  71.1 23.2 %collective-permute-start.1 = (bf16[2,2,256,256]{3,2,1,0:T(8,128)(2,1)}, bf16[2,2,256,256]{3,2,1,0:T(8,128)(2,1)S(1)}, u32[]{:S(2)}, u32[]{:S(2)}) collective-permute-start(bf16[2,2,256,256]{3,2,1,0:T(8,128)(2,1)} %get-tuple-element.68.refs_2_.refs_4_), channel_id=1, source_target_pairs={{0,8},{4,12},{8,0},{12,4},{16,24},{20,28},{24,16},{28,20},{1,9},{5... | collective-permute-start | bytes 1572872 | tf_op jit(solution)/shard_map/ppermute | solution.py:86
  72.2 23.4 %collective-permute-start = (bf16[2,2,256,256]{3,2,1,0:T(8,128)(2,1)}, bf16[2,2,256,256]{3,2,1,0:T(8,128)(2,1)S(1)}, u32[]{:S(2)}, u32[]{:S(2)}) collective-permute-start(bf16[2,2,256,256]{3,2,1,0:T(8,128)(2,1)} %get-tuple-element.68.refs_2_.refs_4_), channel_id=1, source_target_pairs={{0,4},{4,0},{8,12},{12,8},{16,20},{20,16},{24,28},{28,24},{1,5},{5... | collective-permute-start | bytes 1572872 | tf_op jit(solution)/shard_map/ppermute | solution.py:86
  110.3 99.6 %all-gather.9.cloned.1.call-start = ((), (), s32[]{:S(2)}) async-start(), calls=%async_computation.7 | async-start | bytes 2621440 | tf_op jit(solution)/shard_map/all_gather | solution.py:103
  164.5 116.1 %reduce-scatter.7.cloned.1.call-start = ((), (), s32[]{:S(2)}) async-start(), calls=%async_computation.8 | async-start | bytes 2621440 | tf_op jit(solution)/shard_map/reduce_scatter | solution.py:108
  237.7 139.3 %all-gather.11.cloned.1.call-start = ((), (), s32[]{:S(2)}) async-start(), calls=%async_computation.10 | async-start | bytes 2621440 | tf_op jit(solution)/shard_map/all_gather | solution.py:103
  252.2 53.9 %collective-permute-start.13 = (bf16[3,256,1536]{2,1,0:T(8,128)(2,1)}, bf16[3,256,1536]{2,1,0:T(8,128)(2,1)}, u32[]{:S(2)}, u32[]{:S(2)}) collective-permute-start(bf16[3,256,1536]{2,1,0:T(8,128)(2,1)} %get-tuple-element.80), channel_id=1, source_target_pairs={{0,16},{4,20},{8,24},{12,28},{16,0},{20,4},{24,8},{28,12},{1,17},{... | collective-permute-start | bytes 7077896 | tf_op jit(solution)/shard_map/ppermute | solution.py:86
  253.7 53.6 %collective-permute-start.12 = (bf16[3,256,1536]{2,1,0:T(8,128)(2,1)}, bf16[3,256,1536]{2,1,0:T(8,128)(2,1)}, u32[]{:S(2)}, u32[]{:S(2)}) collective-permute-start(bf16[3,256,1536]{2,1,0:T(8,128)(2,1)} %get-tuple-element.77.refs_7_), channel_id=1, source_target_pairs={{0,8},{4,12},{8,0},{12,4},{16,24},{20,28},{24,16},{28,20},{1,9},{5... | collective-permute-start | bytes 7077896 | tf_op jit(solution)/shard_map/ppermute | solution.py:86
  310.9 104.9 %reduce-scatter.9.cloned.1.call-start = ((), (), s32[]{:S(2)}) async-start(), calls=%async_computation.9 | async-start | bytes 2621440 | tf_op jit(solution)/shard_map/reduce_scatter | solution.py:108
  315.2 27.4 %collective-permute-start.15 = (bf16[3,128,1536]{2,1,0:T(8,128)(2,1)}, bf16[3,128,1536]{2,1,0:T(8,128)(2,1)S(1)}, u32[]{:S(2)}, u32[]{:S(2)}) collective-permute-start(bf16[3,128,1536]{2,1,0:T(8,128)(2,1)} %get-tuple-element.86), channel_id=1, source_target_pairs={{0,8},{4,12},{8,0},{12,4},{16,24},{20,28},{24,16},{28,20},{1,9},{5... | collective-permute-start | bytes 3538952 | tf_op jit(solution)/shard_map/ppermute | solution.py:86
  316.6 27.1 %collective-permute-start.14 = (bf16[3,128,1536]{2,1,0:T(8,128)(2,1)}, bf16[3,128,1536]{2,1,0:T(8,128)(2,1)S(1)}, u32[]{:S(2)}, u32[]{:S(2)}) collective-permute-start(bf16[3,128,1536]{2,1,0:T(8,128)(2,1)} %get-tuple-element.82.refs_2_), channel_id=1, source_target_pairs={{0,16},{4,20},{8,24},{12,28},{16,0},{20,4},{24,8},{28,12},{1,17},{... | collective-permute-start | bytes 3538952 | tf_op jit(solution)/shard_map/ppermute | solution.py:86
  348.2 26.5 %collective-permute-start.20 = (bf16[3,128,1536]{2,1,0:T(8,128)(2,1)}, bf16[3,128,1536]{2,1,0:T(8,128)(2,1)}, u32[]{:S(2)}, u32[]{:S(2)}) collective-permute-start(bf16[3,128,1536]{2,1,0:T(8,128)(2,1)} %get-tuple-element.88.refs_5_.refs_6_.refs_3_), channel_id=1, source_target_pairs={{0,8},{4,12},{8,0},{12,4},{16,24},{20,28},{24,16},{28,20},{1,9},{5... | collective-permute-start | bytes 3538952 | tf_op jit(solution)/shard_map/ppermute | solution.py:86
  348.8 26.1 %collective-permute-start.18 = (bf16[3,128,1536]{2,1,0:T(8,128)(2,1)}, bf16[3,128,1536]{2,1,0:T(8,128)(2,1)}, u32[]{:S(2)}, u32[]{:S(2)}) collective-permute-start(bf16[3,128,1536]{2,1,0:T(8,128)(2,1)} %get-tuple-element.87.refs_18_.refs_1_.refs_2_), channel_id=1, source_target_pairs={{0,16},{4,20},{8,24},{12,28},{16,0},{20,4},{24,8},{28,12},{1,17},{... | collective-permute-start | bytes 3538952 | tf_op jit(solution)/shard_map/ppermute | solution.py:86
  349.4 154.6 %reduce-scatter.11.cloned.1.call-start = ((), (), s32[]{:S(2)}) async-start(), calls=%async_computation.11 | async-start | bytes 2621440 | tf_op jit(solution)/shard_map/reduce_scatter | solution.py:108
  349.7 26.1 %collective-permute-start.17 = (bf16[3,128,1536]{2,1,0:T(8,128)(2,1)}, bf16[3,128,1536]{2,1,0:T(8,128)(2,1)S(1)}, u32[]{:S(2)}, u32[]{:S(2)}) collective-permute-start(bf16[3,128,1536]{2,1,0:T(8,128)(2,1)} %get-tuple-element.88.refs_5_.refs_6_.refs_3_), channel_id=1, source_target_pairs={{0,4},{4,0},{8,12},{12,8},{16,20},{20,16},{24,28},{28,24},{1,5},{5... | collective-permute-start | bytes 3538952 | tf_op jit(solution)/shard_map/ppermute | solution.py:86
  349.7 27.3 %collective-permute-start.16 = (bf16[3,128,1536]{2,1,0:T(8,128)(2,1)S(1)}, bf16[3,128,1536]{2,1,0:T(8,128)(2,1)}, u32[]{:S(2)}, u32[]{:S(2)}) collective-permute-start(bf16[3,128,1536]{2,1,0:T(8,128)(2,1)S(1)} %copy-done.7), channel_id=1, source_target_pairs={{0,4},{4,0},{8,12},{12,8},{16,20},{20,16},{24,28},{28,24},{1,5},{5... | collective-permute-start | bytes 3538952 | tf_op jit(solution)/shard_map/ppermute | solution.py:86
  375.1 28.5 %collective-permute-start.29 = (bf16[3,128,1536]{2,1,0:T(8,128)(2,1)}, bf16[3,128,1536]{2,1,0:T(8,128)(2,1)}, u32[]{:S(2)}, u32[]{:S(2)}) collective-permute-start(bf16[3,128,1536]{2,1,0:T(8,128)(2,1)} %get-tuple-element.88.refs_5_.refs_6_.refs_3_), channel_id=1, source_target_pairs={{0,16},{4,20},{8,24},{12,28},{16,0},{20,4},{24,8},{28,12},{1,17},{... | collective-permute-start | bytes 3538952 | tf_op jit(solution)/shard_map/ppermute | solution.py:86
  375.8 28.0 %collective-permute-start.27 = (bf16[3,128,1536]{2,1,0:T(8,128)(2,1)S(1)}, bf16[3,128,1536]{2,1,0:T(8,128)(2,1)}, u32[]{:S(2)}, u32[]{:S(2)}) collective-permute-start(bf16[3,128,1536]{2,1,0:T(8,128)(2,1)S(1)} %copy-done.7), channel_id=1, source_target_pairs={{0,8},{4,12},{8,0},{12,4},{16,24},{20,28},{24,16},{28,20},{1,9},{5... | collective-permute-start | bytes 3538952 | tf_op jit(solution)/shard_map/ppermute | solution.py:86
  407.6 20.7 %collective-permute-start.26 = (bf16[2,2,256,256]{3,2,1,0:T(8,128)(2,1)}, bf16[2,2,256,256]{3,2,1,0:T(8,128)(2,1)}, u32[]{:S(2)}, u32[]{:S(2)}) collective-permute-start(bf16[2,2,256,256]{3,2,1,0:T(8,128)(2,1)} %get-tuple-element.125), channel_id=1, source_target_pairs={{0,24},{4,28},{8,16},{12,20},{16,8},{20,12},{24,0},{28,4},{1,25},{... | collective-permute-start | bytes 1572872 | tf_op jit(solution)/shard_map/ppermute | solution.py:86
  415.2 24.0 %collective-permute-start.25 = (bf16[2,2,256,256]{3,2,1,0:T(8,128)(2,1)}, bf16[2,2,256,256]{3,2,1,0:T(8,128)(2,1)}, u32[]{:S(2)}, u32[]{:S(2)}) collective-permute-start(bf16[2,2,256,256]{3,2,1,0:T(8,128)(2,1)} %get-tuple-element.126), channel_id=1, source_target_pairs={{0,16},{4,20},{8,24},{12,28},{16,0},{20,4},{24,8},{28,12},{1,17},{... | collective-permute-start | bytes 1572872 | tf_op jit(solution)/shard_map/ppermute | solution.py:86
  415.2 24.0 %collective-permute-start.23 = (bf16[2,2,256,256]{3,2,1,0:T(8,128)(2,1)}, bf16[2,2,256,256]{3,2,1,0:T(8,128)(2,1)}, u32[]{:S(2)}, u32[]{:S(2)}) collective-permute-start(bf16[2,2,256,256]{3,2,1,0:T(8,128)(2,1)} %get-tuple-element.130), channel_id=1, source_target_pairs={{0,8},{4,12},{8,0},{12,4},{16,24},{20,28},{24,16},{28,20},{1,9},{5... | collective-permute-start | bytes 1572872 | tf_op jit(solution)/shard_map/ppermute | solution.py:86
  453.1 29.1 %collective-permute-start.44 = (bf16[3,128,1536]{2,1,0:T(8,128)(2,1)}, bf16[3,128,1536]{2,1,0:T(8,128)(2,1)}, u32[]{:S(2)}, u32[]{:S(2)}) collective-permute-start(bf16[3,128,1536]{2,1,0:T(8,128)(2,1)} %get-tuple-element.111), channel_id=1, source_target_pairs={{0,16},{4,20},{8,24},{12,28},{16,0},{20,4},{24,8},{28,12},{1,17},{... | collective-permute-start | bytes 3538952 | tf_op jit(solution)/shard_map/ppermute | solution.py:86
  453.7 29.2 %collective-permute-start.43 = (bf16[3,128,1536]{2,1,0:T(8,128)(2,1)}, bf16[3,128,1536]{2,1,0:T(8,128)(2,1)}, u32[]{:S(2)}, u32[]{:S(2)}) collective-permute-start(bf16[3,128,1536]{2,1,0:T(8,128)(2,1)} %get-tuple-element.98.refs_9_), channel_id=1, source_target_pairs={{0,8},{4,12},{8,0},{12,4},{16,24},{20,28},{24,16},{28,20},{1,9},{5... | collective-permute-start | bytes 3538952 | tf_op jit(solution)/shard_map/ppermute | solution.py:86
  469.1 29.3 %collective-permute-start.34 = (bf16[1,256,1536]{2,1,0:T(8,128)(2,1)}, bf16[1,256,1536]{2,1,0:T(8,128)(2,1)S(1)}, u32[]{:S(2)}, u32[]{:S(2)}) collective-permute-start(bf16[1,256,1536]{2,1,0:T(8,128)(2,1)} %get-tuple-element.102), channel_id=1, source_target_pairs={{0,16},{4,20},{8,24},{12,28},{16,0},{20,4},{24,8},{28,12},{1,17},{... | collective-permute-start | bytes 2359304 | tf_op jit(solution)/shard_map/ppermute | solution.py:86
  470.7 27.7 %collective-permute-start.33 = (bf16[1,256,1536]{2,1,0:T(8,128)(2,1)}, bf16[1,256,1536]{2,1,0:T(8,128)(2,1)S(1)}, u32[]{:S(2)}, u32[]{:S(2)}) collective-permute-start(bf16[1,256,1536]{2,1,0:T(8,128)(2,1)} %get-tuple-element.100.refs_17_), channel_id=1, source_target_pairs={{0,8},{4,12},{8,0},{12,4},{16,24},{20,28},{24,16},{28,20},{1,9},{5... | collective-permute-start | bytes 2359304 | tf_op jit(solution)/shard_map/ppermute | solution.py:86
  482.3 24.9 %collective-permute-start.46 = (bf16[3,128,1536]{2,1,0:T(8,128)(2,1)}, bf16[3,128,1536]{2,1,0:T(8,128)(2,1)S(1)}, u32[]{:S(2)}, u32[]{:S(2)}) collective-permute-start(bf16[3,128,1536]{2,1,0:T(8,128)(2,1)} %collective-permute-done.44.refs_7_.refs_8_.refs_4_), channel_id=1, source_target_pairs={{0,4},{4,0},{8,12},{12,8},{16,20},{20,16},{24,28},{28,24},{1,5},{5... | collective-permute-start | bytes 3538952 | tf_op jit(solution)/shard_map/ppermute | solution.py:86
  482.9 24.2 %collective-permute-start.45 = (bf16[3,128,1536]{2,1,0:T(8,128)(2,1)}, bf16[3,128,1536]{2,1,0:T(8,128)(2,1)}, u32[]{:S(2)}, u32[]{:S(2)}) collective-permute-start(bf16[3,128,1536]{2,1,0:T(8,128)(2,1)} %collective-permute-done.43.refs_3_.refs_4_.refs_2_), channel_id=1, source_target_pairs={{0,4},{4,0},{8,12},{12,8},{16,20},{20,16},{24,28},{28,24},{1,5},{5... | collective-permute-start | bytes 3538952 | tf_op jit(solution)/shard_map/ppermute | solution.py:86
  532.0 20.1 %collective-permute-start.48 = (bf16[1,256,1536]{2,1,0:T(8,128)(2,1)S(1)}, bf16[1,256,1536]{2,1,0:T(8,128)(2,1)S(1)}, u32[]{:S(2)}, u32[]{:S(2)}) collective-permute-start(bf16[1,256,1536]{2,1,0:T(8,128)(2,1)S(1)} %maximum_select_fusion.refs_1_), channel_id=1, source_target_pairs={{0,8},{4,12},{8,0},{12,4},{16,24},{20,28},{24,16},{28,20},{1,9},{5... | collective-permute-start | bytes 2359304 | tf_op jit(solution)/shard_map/ppermute | solution.py:86
  533.8 18.8 %collective-permute-start.50 = (bf16[1,256,1536]{2,1,0:T(8,128)(2,1)S(1)}, bf16[1,256,1536]{2,1,0:T(8,128)(2,1)S(1)}, u32[]{:S(2)}, u32[]{:S(2)}) collective-permute-start(bf16[1,256,1536]{2,1,0:T(8,128)(2,1)S(1)} %maximum_select_fusion.1.refs_3_), channel_id=1, source_target_pairs={{0,16},{4,20},{8,24},{12,28},{16,0},{20,4},{24,8},{28,12},{1,17},{... | collective-permute-start | bytes 2359304 | tf_op jit(solution)/shard_map/ppermute | solution.py:86
  (70 other events, 653.6 us)
Sparse Core Ops, SparseCore 0:
  10.2 48.6 all-gather.4
  60.4 44.6 all-gather.6
  110.4 51.3 reduce-scatter.4
  164.6 45.2 all-gather.8
  237.8 42.6 reduce-scatter.6
  311.0 43.2 all-gather.10
  357.2 42.5 reduce-scatter.8
  449.3 41.3 reduce-scatter.10

commit v5 on v4

--- a/solution.py
+++ b/solution.py
@@ -114,61 +114,47 @@
     send_ref[...] = x_ref[:, pl.ds(pl.multiple_of((1 - core) * half, half), half)]
 
 
-def qkv_kernel(row_count, meta, x, wq, wk, wv, gq, gk, cos, sin, q_out, kv_out, q_raw, k_raw, keep, send, acc_q, acc_k, acc_v):
-    j, last = pl.program_id(0), pl.num_programs(0) - 1
-
-    @pl.when(j == 0)
+def qkv_kernel(row_count, meta, x, wq, wk, wv, gq, gk, cos, sin, q_out, kv_out, q_raw, k_raw, keep, send):
+    @pl.when(pl.program_id(0) == 0)
     def _():
         half_out(x, meta[0], keep, send)
-        acc_q[...] = jnp.zeros_like(acc_q)
-        acc_k[...] = jnp.zeros_like(acc_k)
-        acc_v[...] = jnp.zeros_like(acc_v)
-
-    depth = wq.shape[0]
-    xs = x[:, pl.ds(pl.multiple_of(j * depth, depth), depth)]
-    acc_q[...] += dot_nn(xs, wq[...])
-    acc_k[...] += dot_nn(xs, wk[...])
-    acc_v[...] += dot_nn(xs, wv[...])
-
-    @pl.when(j == last)
-    def _():
-        def turn(raw, gain):
-            inverse = lax.rsqrt(jnp.mean(raw * raw, axis=-1, keepdims=True) + EPS)
-            normed = raw * inverse * gain
-            return (normed * cos[...] + pltpu.roll(normed, HEAD // 2, 1) * sin[...]).astype(BF)
-
-        q_raw[...] = acc_q[...]
-        k_raw[...] = acc_k[...]
-        for h in range(acc_q.shape[1] // HEAD):
-            at = slice(h * HEAD, (h + 1) * HEAD)
-            q_out[:, at] = turn(acc_q[:, at], gq[...])
-        span = kv_out.shape[2]
-        for h in range(acc_k.shape[1] // HEAD):
-            at = slice(h * HEAD, (h + 1) * HEAD)
-            turned = turn(acc_k[:, at], gk[...])
-            for r in range(row_count):
-                kv_out[r, 0, :, at] = turned[r * span : (r + 1) * span]
-        for r in range(row_count):
-            kv_out[r, 1] = acc_v[r * span : (r + 1) * span, :].astype(BF)
+
+    def turn(raw, gain):
+        inverse = lax.rsqrt(jnp.mean(raw * raw, axis=-1, keepdims=True) + EPS)
+        normed = raw * inverse * gain
+        return (normed * cos[...] + pltpu.roll(normed, HEAD // 2, 1) * sin[...]).astype(BF)
+
+    query, key, value = dot_nn(x[...], wq[...]), dot_nn(x[...], wk[...]), dot_nn(x[...], wv[...])
+    q_raw[...] = query
+    k_raw[...] = key
+    for h in range(query.shape[1] // HEAD):
+        at = slice(h * HEAD, (h + 1) * HEAD)
+        q_out[:, at] = turn(query[:, at], gq[...])
+    turned = turn(key, gk[...])
+    span = kv_out.shape[2]
+    for r in range(row_count):
+        kv_out[r, 0] = turned[r * span : (r + 1) * span]
+        kv_out[r, 1] = value[r * span : (r + 1) * span].astype(BF)
 
 
 def qkv_call(meta, row_count, x, weights, gains, tables):
     tokens, width = x.shape
     nq, nk = weights[0].shape[1], weights[1].shape[1]
-    depth = width // 4
-    row = lambda n: pl.BlockSpec((depth, n), lambda j, *_: (j, 0))
-    kv = (row_count, 2, tokens // row_count, nk)
+    heads = nk // HEAD
+    column = lambda rows, n: pl.BlockSpec((rows, n), lambda j, *_: (0, j))
+    span = tokens // row_count
     return call(
         functools.partial(qkv_kernel, row_count),
-        (4,),
-        [whole((tokens, width)), row(nq), row(nk), row(nk)]
+        (heads,),
+        [whole((tokens, width)), column(width, nq // heads), column(width, HEAD), column(width, HEAD)]
         + [whole((1, HEAD))] * 2
         + [whole((tokens, HEAD))] * 2,
-        [whole((tokens, nq)), whole(kv), whole((tokens, nq)), whole((tokens, nk))]
+        [column(tokens, nq // heads), pl.BlockSpec((row_count, 2, span, HEAD), lambda j, *_: (0, 0, 0, j))]
+        + [column(tokens, nq // heads), column(tokens, HEAD)]
         + [whole((tokens, width // 2))] * 2,
-        [hbm((tokens, nq), BF), hbm(kv, BF), hbm((tokens, nq), F32), hbm((tokens, nk), F32)]
+        [hbm((tokens, nq), BF), hbm((row_count, 2, span, nk), BF), hbm((tokens, nq), F32), hbm((tokens, nk), F32)]
         + [hbm((tokens, width // 2), BF)] * 2,
-        [pltpu.VMEM((tokens, nq), F32), pltpu.VMEM((tokens, nk), F32), pltpu.VMEM((tokens, nk), F32)],
+        [],
         (meta, x, *weights, *gains, *tables),
         40,
     )
@@ -537,13 +523,17 @@
         out[at] = total[n * part : (n + 1) * part].astype(BF)
 
 
-def ff_grad_kernel(ids, og0, og1, x0, x1, p0, p1, *refs):
-    outs, turned = refs[:-1], refs[-1]
+def ff_grad_kernel(count, ids, *refs):
+    lefts, p0, p1, outs, turned = refs[: 4 * count], refs[4 * count], refs[4 * count + 1], refs[4 * count + 2 : -1], refs[-1]
 
     @pl.when(pl.program_id(0) == 0)
     def _():
-        turn_rows(ids, len(outs), (og0, og1), turned.at[0])
-        turn_rows(ids, len(outs), (x0, x1), turned.at[1])
+        for k in range(4):
+            for n in range(count):
+                block = lefts[k * count + n]
+                tokens, part = block.shape
+                at = k % 2 * tokens
+                turned[k // 2, n * part : (n + 1) * part, at : at + tokens] = block[...].T
 
     for n in range(3):
         right = jnp.concatenate([p0[n], p1[n]], axis=0)
@@ -556,14 +546,16 @@
     wide = next(w for w in (512, 384, 256, 128) if hidden % w == 0)
     part = rows // 4
     count = ids.shape[0]
-    return call(
-        ff_grad_kernel,
+    left = lambda n: pl.BlockSpec((tokens, part), lambda c, ids: (0, ids[n]))
+    return call(
+        functools.partial(ff_grad_kernel, count),
         (hidden // wide,),
-        [whole((tokens, rows))] * 4 + [pl.BlockSpec((3, tokens, wide), lambda c, ids: (0, 0, c))] * 2,
+        [left(n) for _ in range(4) for n in range(count)]
+        + [pl.BlockSpec((3, tokens, wide), lambda c, ids: (0, 0, c))] * 2,
         [pl.BlockSpec((3, part, wide), lambda c, ids: (0, 0, c))] * count,
         [hbm((3, part, hidden), BF)] * count,
         [pltpu.VMEM((2, count * part, 2 * tokens), BF)],
-        (ids, *ogs, *xs, *planes),
+        (ids, *(v for v in (*ogs, *xs) for _ in range(count)), *planes),
         48,
         free=True,
     )
@@ -607,8 +599,9 @@
         [pl.BlockSpec((1, part, wide), lambda c, ids: (0, 0, c))] * count,
         [hbm((1, part, cols), BF)] * count,
         [pltpu.VMEM((count * part, 2 * tokens), BF)],
-        (ids, *xs, *bs, *grads, *outs),
+        (ids, *(in_hbm(v) for v in (*xs, *bs, grads[0])), grads[1], *(in_hbm(v) for v in outs)),
         48,
+        free=True,
     )
 
 
@@ -763,6 +756,30 @@
         24,
         prefetch=0,
     )
+
+
+def pack_kernel(a, b, q, k, out):
+    rows = a.shape[0]
+    out[:rows, :] = a[...]
+    out[rows : 2 * rows, :] = b[...]
+    out[2 * rows : 2 * rows + 1, :] = q[...]
+    out[2 * rows + 1 :, :] = k[...]
+
+
+def pack_call(a, b, q, k):
+    arrays = [v.reshape(-1, HEAD) for v in (a, b, q, k)]
+    shape = (sum(v.shape[0] for v in arrays), HEAD)
+    return call(
+        pack_kernel,
+        (1,),
+        [whole(v.shape) for v in arrays],
+        [whole(shape)],
+        [hbm(shape, F32)],
+        [],
+        tuple(arrays),
+        16,
+        prefetch=0,
+    )[0]
 
 
 def norm_kernel(x, gain, out):
@@ -1035,17 +1052,15 @@
     gate_up_out, down_out = ff.widen(*gate_up, early=True), ff.widen(*down, early=True)
     attn.middle()
     input_grad, attn_gain_grad = norm_grad_call(hidden, flat(n1_got), middle_grad, attn_gain, False)
-    gains = jnp.concatenate(
-        [v.reshape(-1) for v in (attn_gain_grad, ff_gain_grad, q_gain_grad, k_gain_grad)]
-    ).reshape(-1, HEAD)
-    gains = sum_copies(gains, "tp", [1 << level for level in range(tp.bit_length() - 1)])
-    for level in range(seqs.bit_length() - 1):
-        gains = sum_copies(gains, "seq", [1 << level])
     input_grad = shares(input_grad)
     block_out = shares((middle + flat(ff_got).astype(F32)).astype(BF))
     gate_out, up_out = ff.widen(*gate_up, onto=gate_up_out)
     attn.last()
     (down_out,) = ff.widen(*down, onto=down_out)
+    gains = pack_call(attn_gain_grad, ff_gain_grad, q_gain_grad, k_gain_grad)
+    gains = sum_copies(gains, "tp", [1 << level for level in range(tp.bit_length() - 1)])
+    for level in range(seqs.bit_length() - 1):
+        gains = sum_copies(gains, "seq", [1 << level])
     query_out, key_out, value_out, output_out = attn.widen(*attend)
     gains = gains.reshape(-1)
     return (

time: 587 us -> 585 us (level)
    pallas_call x25 -> x26, Pallas kernels: 179 us -> 178 us  [call(): pl.pallas_call(run, grid_spec=pltpu.PrefetchScalarGridSpec(num_scalar_pre...]
  transfers between devices with their start and end apart: 63 -> 63, of which waited for: 32 -> 34; matrix products, arithmetic and copies ran while one was open for 3% -> 3% of each run, Pallas kernels for 23% -> 23%
where the time goes in v5:
time: 585 us; the launch traced here: 576 us
  waiting for transfers between devices  321 us (55%)
  Pallas kernels  178 us (30%)
  starting transfers between devices  44.2 us (8%)
  between operations  15 us (3%)
  other arithmetic  12.3 us (2%)
    pallas_call x26, Pallas kernels, call(): pl.pallas_call(run, grid_spec=pltpu.PrefetchScalarGridSpec(num_scalar_pre...  178 us
    ppermute x55, waiting for transfers between devices, swap(): return lax.ppermute(value, axis, flip(axis, mask))  167 us
    all_gather x4, waiting for transfers between devices, gather_tp(): return lax.all_gather(share, 'tp', axis=1, tiled=True).reshape(-1, width)  85.9 us
    reduce_scatter x4, waiting for transfers between devices, scatter_tp(): return lax.psum_scatter(part, 'tp', scatter_dimension=1, tiled=True)  67.2 us
    ppermute x55, starting transfers between devices, swap(): return lax.ppermute(value, axis, flip(axis, mask))  43.5 us
  transfers between devices with their start and end apart: 63, of which 34 were waited for; matrix products, arithmetic and copies ran while one was open for 3% of the time, Pallas kernels for 23%

profile of v5, /device:TPU:0, one launch (start us, length us, event | category | flops | bytes accessed | tf_op | source)
XLA Modules:
  0.0 576.0 jit_solution(3279072161899713617)
XLA Ops:
  12.9 45.9 %all-gather.5.cloned.1.call-done = bf16[2,256,2048]{2,1,0:T(8,128)(2,1)} async-done(((bf16[2,64,2048]{2,1,0:T(8,128)(2,1)}), bf16[2,256,2048]{2,1,0:T(8,128)(2,1)}) %all-gather.5.cloned.1.call-update) | async-done | bytes 2097168 | tf_op jit(solution)/shard_map/all_gather | solution.py:103
  58.8 8.7 %shard_map.256 = (bf16[512,512]{1,0:T(8,128)(2,1)}, bf16[2,2,256,256]{3,2,1,0:T(8,128)(2,1)}, f32[512,512]{1,0:T(8,128)}, f32[512,256]{1,0:T(8,128)}, bf16[512,1...) custom-call(s32[1]{0:T(128)} %bitcast.4.refs_0_, bf16[512,2048]{1,0:T(8,128)(2,1)} %bitcast.69, bf16[2048,512]{1,0:T(8,128)(2,1)} %refs_1_.3, ...), custom_call_target="tpu_custom_call" | custom-call | flops 1 | bytes 1 | tf_op jit(solution)/shard_map/pallas_call | solution.py:58
  71.7 11.9 %collective-permute-done.5.refs_8_.refs_10_ = bf16[2,2,256,256]{3,2,1,0:T(8,128)(2,1)S(1)} collective-permute-done((bf16[2,2,256,256]{3,2,1,0:T(8,128)(2,1)}, bf16[2,2,256,256]{3,2,1,0:T(8,128)(2,1)S(1)}, u32[]{:S(2)}, u32[]{:S(2)}) %collective-permute-start.5) | collective-permute-done | bytes 524320 | tf_op jit(solution)/shard_map/ppermute | solution.py:86
  83.6 10.0 %collective-permute-done.3.refs_6_.refs_8_ = bf16[2,2,256,256]{3,2,1,0:T(8,128)(2,1)S(1)} collective-permute-done((bf16[2,2,256,256]{3,2,1,0:T(8,128)(2,1)}, bf16[2,2,256,256]{3,2,1,0:T(8,128)(2,1)S(1)}, u32[]{:S(2)}, u32[]{:S(2)}) %collective-permute-start.3) | collective-permute-done | bytes 524320 | tf_op jit(solution)/shard_map/ppermute | solution.py:86
  96.4 13.3 %shard_map.257 = (bf16[512,512]{1,0:T(8,128)(2,1)}, f32[2,2,512,1]{3,2,1,0:T(8,128)}, bf16[512,2048]{1,0:T(8,128)(2,1)}) custom-call(s32[34]{0:T(128)S(1)} %concatenate.77.refs_0_, bf16[512,512]{1,0:T(8,128)(2,1)} %get-tuple-element.67.refs_1_.refs_11_.refs_3_, bf16[2,2,256,256]{3,2,1,0:T(8,128)(2,1)} %get-tuple-element.68.refs_2_.refs_4_, ...), custom_call_target="tpu_custom_call" | custom-call | flops 1 | bytes 1 | tf_op jit(solution)/shard_map/pallas_call | solution.py:58
  109.8 51.7 %reduce-scatter.5.cloned.1.call-done = bf16[2,64,2048]{2,1,0:T(8,128)(2,1)} async-done(((bf16[2,256,2048]{2,1,0:T(8,128)(2,1)}), bf16[2,64,2048]{2,1,0:T(8,128)(2,1)}) %reduce-scatter.5.cloned.1.call-update) | async-done | bytes 524304 | tf_op jit(solution)/shard_map/reduce_scatter | solution.py:108
  169.6 40.0 %all-gather.9.cloned.1.call-done = bf16[2,256,2048]{2,1,0:T(8,128)(2,1)} async-done(((bf16[2,64,2048]{2,1,0:T(8,128)(2,1)}), bf16[2,256,2048]{2,1,0:T(8,128)(2,1)}) %all-gather.9.cloned.1.call-update) | async-done | bytes 2097168 | tf_op jit(solution)/shard_map/all_gather | solution.py:103
  209.6 16.5 %shard_map.259 = (bf16[3,512,1536]{2,1,0:T(8,128)(2,1)}, bf16[512,1024]{1,0:T(8,128)(2,1)}, bf16[512,1024]{1,0:T(8,128)(2,1)}) custom-call(s32[1]{0:T(128)} %bitcast.4.refs_0_, bf16[512,2048]{1,0:T(8,128)(2,1)} %bitcast.67, bf16[512,2048]{1,0:T(8,128)(2,1)} %bitcast.57, bf16[2048,1536]{1,0:T(8,128)(2,1)} %refs_2_.5, bf16[2048,1536]{1,0:T(8,128)(2,1)} %refs_3_.6, ...), custom_call_target="tpu_custom_call" | custom-call | flops 1 | bytes 1 | tf_op jit(solution)/shard_map/pallas_call | solution.py:58
  226.0 11.3 %shard_map.260.refs_11_ = bf16[512,2048]{1,0:T(8,128)(2,1)} custom-call(bf16[3,512,1536]{2,1,0:T(8,128)(2,1)} %get-tuple-element.74.refs_0_.refs_1_.refs_4_.refs_9_, bf16[3,512,1536]{2,1,0:T(8,128)(2,1)} %get-tuple-element.74.refs_0_.refs_1_.refs_4_.refs_9_, bf16[2048,1536]{1,0:T(8,128)(2,1)} %refs_2_.5, bf16[2048,1536]{1,0:T(8,128)(2,1)} %refs_3_.6, ...), custom_call_target="tpu_custom_call" | custom-call | flops 1 | bytes 1 | tf_op jit(solution)/shard_map/pallas_call | solution.py:58
  240.6 10.7 %shard_map.261 = (bf16[3,256,1536]{2,1,0:T(8,128)(2,1)}, bf16[3,256,1536]{2,1,0:T(8,128)(2,1)}) custom-call(s32[2]{0:T(128)S(1)} %get-tuple-element.144.refs_0_, bf16[512,1024]{1,0:T(8,128)(2,1)S(1)} %get-tuple-element.131.refs_1_.refs_2_, bf16[512,1024]{1,0:T(8,128)(2,1)S(1)} %get-tuple-element.131.refs_1_.refs_2_, bf16[512,1024]{1,0:T(8,128)(2,1)S(1)} %copy-done.1, ...), custom_call_target="tpu_custom_call" | custom-call | flops 1 | bytes 1 | tf_op jit(solution)/shard_map/pallas_call | solution.py:58
  254.2 10.4 %shard_map.262 = (bf16[3,256,1536]{2,1,0:T(8,128)(2,1)}, bf16[3,256,1536]{2,1,0:T(8,128)(2,1)}) custom-call(s32[2]{0:T(128)S(1)} %get-tuple-element.145.refs_0_, bf16[512,1024]{1,0:T(8,128)(2,1)S(1)} %get-tuple-element.131.refs_1_.refs_2_, bf16[512,1024]{1,0:T(8,128)(2,1)S(1)} %get-tuple-element.131.refs_1_.refs_2_, bf16[512,1024]{1,0:T(8,128)(2,1)S(1)} %copy-done.1, ...), custom_call_target="tpu_custom_call" | custom-call | flops 1 | bytes 1 | tf_op jit(solution)/shard_map/pallas_call | solution.py:58
  264.6 15.6 %reduce-scatter.7.cloned.1.call-done = bf16[2,64,2048]{2,1,0:T(8,128)(2,1)} async-done(((bf16[2,256,2048]{2,1,0:T(8,128)(2,1)}), bf16[2,64,2048]{2,1,0:T(8,128)(2,1)}) %reduce-scatter.7.cloned.1.call-update) | async-done | bytes 524304 | tf_op jit(solution)/shard_map/reduce_scatter | solution.py:108
  280.1 24.9 %collective-permute-done.13.refs_6_.refs_4_.refs_5_ = bf16[3,256,1536]{2,1,0:T(8,128)(2,1)} collective-permute-done((bf16[3,256,1536]{2,1,0:T(8,128)(2,1)}, bf16[3,256,1536]{2,1,0:T(8,128)(2,1)}, u32[]{:S(2)}, u32[]{:S(2)}) %collective-permute-start.13) | collective-permute-done | bytes 2359328 | tf_op jit(solution)/shard_map/ppermute | solution.py:86
  310.0 4.2 shard_map.264
  316.2 7.4 %shard_map.265.refs_7_ = bf16[512,2048]{1,0:T(8,128)(2,1)} custom-call(bf16[3,512,1536]{2,1,0:T(8,128)(2,1)} %get-tuple-element.74.refs_0_.refs_1_.refs_4_.refs_9_, bf16[1536,2048]{1,0:T(8,128)(2,1)} %refs_1_.2, bf16[3,128,1536]{2,1,0:T(8,128)(2,1)} %get-tuple-element.82.refs_2_), custom_call_target="tpu_custom_call" | custom-call | flops 1 | bytes 1 | tf_op jit(solution)/shard_map/pallas_call | solution.py:58
  323.6 17.9 %collective-permute-done.15.refs_6_ = bf16[3,128,1536]{2,1,0:T(8,128)(2,1)S(1)} collective-permute-done((bf16[3,128,1536]{2,1,0:T(8,128)(2,1)}, bf16[3,128,1536]{2,1,0:T(8,128)(2,1)S(1)}, u32[]{:S(2)}, u32[]{:S(2)}) %collective-permute-start.15) | collective-permute-done | bytes 1179680 | tf_op jit(solution)/shard_map/ppermute | solution.py:86
  342.7 4.4 shard_map.266
  349.1 24.3 %collective-permute-done.20.refs_1_.refs_7_.refs_8_.refs_4_ = bf16[3,128,1536]{2,1,0:T(8,128)(2,1)} collective-permute-done((bf16[3,128,1536]{2,1,0:T(8,128)(2,1)}, bf16[3,128,1536]{2,1,0:T(8,128)(2,1)}, u32[]{:S(2)}, u32[]{:S(2)}) %collective-permute-start.20) | collective-permute-done | bytes 1179680 | tf_op jit(solution)/shard_map/ppermute | solution.py:86
  378.3 12.7 %shard_map.267 = (bf16[512,512]{1,0:T(8,128)(2,1)}, bf16[4,2,2,256,256]{4,3,2,1,0:T(8,128)(2,1)}, bf16[2,2,2,256,256]{4,3,2,1,0:T(8,128)(2,1)}, bf16[2,2,2,256,2...) custom-call(s32[34]{0:T(128)S(1)} %concatenate.77.refs_0_, ...), custom_call_target="tpu_custom_call" | custom-call | flops 1 | bytes 1 | tf_op jit(solution)/shard_map/pallas_call | solution.py:58
  393.9 8.4 %collective-permute-done.29.refs_5_.refs_6_.refs_3_ = bf16[3,128,1536]{2,1,0:T(8,128)(2,1)} collective-permute-done((bf16[3,128,1536]{2,1,0:T(8,128)(2,1)}, bf16[3,128,1536]{2,1,0:T(8,128)(2,1)}, u32[]{:S(2)}, u32[]{:S(2)}) %collective-permute-start.29) | collective-permute-done | bytes 1179680 | tf_op jit(solution)/shard_map/ppermute | solution.py:86
  406.4 7.8 %collective-permute-start.26 = (bf16[2,2,256,256]{3,2,1,0:T(8,128)(2,1)}, bf16[2,2,256,256]{3,2,1,0:T(8,128)(2,1)}, u32[]{:S(2)}, u32[]{:S(2)}) collective-permute-start(bf16[2,2,256,256]{3,2,1,0:T(8,128)(2,1)} %get-tuple-element.125), channel_id=1, source_target_pairs={{0,24},{4,28},{8,16},{12,20},{16,8},{20,12},{24,0},{28,4},{1,25},{... | collective-permute-start | bytes 1572872 | tf_op jit(solution)/shard_map/ppermute | solution.py:86
  414.8 12.4 %collective-permute-done.26.refs_3_ = bf16[2,2,256,256]{3,2,1,0:T(8,128)(2,1)} collective-permute-done((bf16[2,2,256,256]{3,2,1,0:T(8,128)(2,1)}, bf16[2,2,256,256]{3,2,1,0:T(8,128)(2,1)}, u32[]{:S(2)}, u32[]{:S(2)}) %collective-permute-start.26) | collective-permute-done | bytes 524320 | tf_op jit(solution)/shard_map/ppermute | solution.py:86
  427.2 10.7 %collective-permute-done.25.refs_2_ = bf16[2,2,256,256]{3,2,1,0:T(8,128)(2,1)} collective-permute-done((bf16[2,2,256,256]{3,2,1,0:T(8,128)(2,1)}, bf16[2,2,256,256]{3,2,1,0:T(8,128)(2,1)}, u32[]{:S(2)}, u32[]{:S(2)}) %collective-permute-start.25) | collective-permute-done | bytes 524320 | tf_op jit(solution)/shard_map/ppermute | solution.py:86
  441.8 6.2 %shard_map.269.refs_2_ = bf16[512,2048]{1,0:T(8,128)(2,1)} custom-call(bf16[512,1024]{1,0:T(8,128)(2,1)} %get-tuple-element.95.refs_0_.refs_4_.refs_5_, bf16[2048,512]{1,0:T(8,128)(2,1)} %refs_1_.3, bf16[2048,256]{1,0:T(8,128)(2,1)} %refs_2_.7, bf16[2048,256]{1,0:T(8,128)(2,1)} %refs_3_.7, bf16[512,1024]{1,0:T(8,128)(2,1)} %get-tuple-element.95.refs_0_.refs_4_.refs_5_), custom_call_target="tpu_custom_call" | custom-call | flops 1 | bytes 1 | tf_op jit(solution)/shard_map/pallas_call | solution.py:58
  456.9 9.8 %shard_map.271 = (bf16[1,256,1536]{2,1,0:T(8,128)(2,1)}, bf16[1,256,1536]{2,1,0:T(8,128)(2,1)}, bf16[1,256,1536]{2,1,0:T(8,128)(2,1)}, bf16[1,256,1536]{2,1,0:T(8,128)(2,1)}) custom-call(s32[4]{0:T(128)S(1)} %pad_add_fusion.3.refs_0_, bf16[512,1024]{1,0:T(8,128)(2,1)} %get-tuple-element.96.refs_1_, bf16[512,1024]{1,0:T(8,128)(2,1)} %copy-done.17, ...), custom_call_target="tpu_custom_call" | custom-call | flops 1 | bytes 1 | tf_op jit(solution)/shard_map/pallas_call | solution.py:58
  468.4 12.5 %collective-permute-done.36.refs_7_.refs_8_.refs_4_ = bf16[3,128,1536]{2,1,0:T(8,128)(2,1)S(1)} collective-permute-done((bf16[3,128,1536]{2,1,0:T(8,128)(2,1)}, bf16[3,128,1536]{2,1,0:T(8,128)(2,1)S(1)}, u32[]{:S(2)}, u32[]{:S(2)}) %collective-permute-start.36) | collective-permute-done | bytes 1179680 | tf_op jit(solution)/shard_map/ppermute | solution.py:86
  482.8 8.3 %shard_map.272 = (f32[2048,1536]{1,0:T(8,128)}, f32[2048,1536]{1,0:T(8,128)}) custom-call(s32[12]{0:T(128)} %pad_add_fusion.6.refs_0_, bf16[3,128,1536]{2,1,0:T(8,128)(2,1)} %get-tuple-element.87.refs_18_.refs_1_.refs_2_, bf16[3,128,1536]{2,1,0:T(8,128)(2,1)} %get-tuple-element.87.refs_18_.refs_1_.refs_2_, ...), custom_call_target="tpu_custom_call" | custom-call | flops 1 | bytes 1 | tf_op jit(solution)/shard_map/pallas_call | solution.py:58
  491.2 6.0 %shard_map.273.refs_5_.refs_9_ = f32[1536,2048]{1,0:T(8,128)} custom-call(s32[12]{0:T(128)} %pad_add_fusion.6.refs_0_, bf16[3,128,1536]{2,1,0:T(8,128)(2,1)} %get-tuple-element.87.refs_18_.refs_1_.refs_2_, bf16[3,128,1536]{2,1,0:T(8,128)(2,1)} %collective-permute-done.18.refs_0_.refs_3_.refs_4_.refs_2_, ...), custom_call_target="tpu_custom_call" | custom-call | flops 1 | bytes 1 | tf_op jit(solution)/shard_map/pallas_call | solution.py:58
  506.0 8.3 %shard_map.276 = (f32[2048,1536]{1,0:T(8,128)}, f32[2048,1536]{1,0:T(8,128)}) custom-call(s32[12]{0:T(128)} %pad_add_fusion.7.refs_0_, bf16[3,128,1536]{2,1,0:T(8,128)(2,1)} %collective-permute-done.27.refs_1_.refs_2_, bf16[3,128,1536]{2,1,0:T(8,128)(2,1)} %collective-permute-done.27.refs_1_.refs_2_, ...), custom_call_target="tpu_custom_call", output_to_operand_aliasing={{0}: (17, {}), {1}: (18, {})} | custom-call | flops 1 | bytes 1 | tf_op jit(solution)/shard_map/pallas_call | solution.py:58
  518.1 10.3 %collective-permute-done.47 = bf16[1,128,1536]{2,1,0:T(8,128)(2,1)S(1)} collective-permute-done((bf16[1,128,1536]{2,1,0:T(8,128)(2,1)}, bf16[1,128,1536]{2,1,0:T(8,128)(2,1)S(1)}, u32[]{:S(2)}, u32[]{:S(2)}) %collective-permute-start.47) | collective-permute-done | bytes 393248 | tf_op jit(solution)/shard_map/ppermute | solution.py:86
  532.1 5.9 %shard_map.278.refs_4_ = f32[1536,2048]{1,0:T(8,128)} custom-call(s32[12]{0:T(128)} %pad_add_fusion.7.refs_0_, bf16[3,128,1536]{2,1,0:T(8,128)(2,1)} %collective-permute-done.27.refs_1_.refs_2_, bf16[3,128,1536]{2,1,0:T(8,128)(2,1)} %collective-permute-done.35.refs_3_.refs_4_.refs_2_, ...), custom_call_target="tpu_custom_call", output_to_operand_aliasing={{}: (9, {})} | custom-call | flops 1 | bytes 1 | tf_op jit(solution)/shard_map/pallas_call | solution.py:58
  559.5 9.2 %shard_map.280 = (f32[2048,512]{1,0:T(8,128)}, f32[2048,256]{1,0:T(8,128)}, f32[2048,256]{1,0:T(8,128)}, f32[512,2048]{1,0:T(8,128)}) custom-call(s32[16]{0:T(128)} %pad_add_fusion.8.refs_0_, bf16[1,256,1536]{2,1,0:T(8,128)(2,1)} %copy-done.19, bf16[1,256,1536]{2,1,0:T(8,128)(2,1)} %copy-done.28, bf16[1,256,1536]{2,1,0:T(8,128)(2,1)} %copy-done.20, ...), custom_call_target="tpu_custom_call" | custom-call | flops 1 | bytes 1 | tf_op jit(solution)/shard_map/pallas_call | solution.py:58
  (253 shorter events, 103.4 us)
Async XLA Ops:
  7.2 51.7 %all-gather.5.cloned.1.call-start = ((), (), s32[]{:S(2)}) async-start(), calls=%async_computation.4 | async-start | bytes 2621440 | tf_op jit(solution)/shard_map/all_gather | solution.py:103
  9.3 100.5 %all-gather.7.cloned.1.call-start = ((), (), s32[]{:S(2)}) async-start(), calls=%async_computation.6 | async-start | bytes 2621440 | tf_op jit(solution)/shard_map/all_gather | solution.py:103
  10.1 151.4 %reduce-scatter.5.cloned.1.call-start = ((), (), s32[]{:S(2)}) async-start(), calls=%async_computation.5 | async-start | bytes 2621440 | tf_op jit(solution)/shard_map/reduce_scatter | solution.py:108
  69.9 23.6 %collective-permute-start.3 = (bf16[2,2,256,256]{3,2,1,0:T(8,128)(2,1)}, bf16[2,2,256,256]{3,2,1,0:T(8,128)(2,1)S(1)}, u32[]{:S(2)}, u32[]{:S(2)}) collective-permute-start(bf16[2,2,256,256]{3,2,1,0:T(8,128)(2,1)} %get-tuple-element.68.refs_2_.refs_4_), channel_id=1, source_target_pairs={{0,16},{4,20},{8,24},{12,28},{16,0},{20,4},{24,8},{28,12},{1,17},{... | collective-permute-start | bytes 1572872 | tf_op jit(solution)/shard_map/ppermute | solution.py:86
  70.5 23.2 %collective-permute-start.1 = (bf16[2,2,256,256]{3,2,1,0:T(8,128)(2,1)}, bf16[2,2,256,256]{3,2,1,0:T(8,128)(2,1)S(1)}, u32[]{:S(2)}, u32[]{:S(2)}) collective-permute-start(bf16[2,2,256,256]{3,2,1,0:T(8,128)(2,1)} %get-tuple-element.68.refs_2_.refs_4_), channel_id=1, source_target_pairs={{0,8},{4,12},{8,0},{12,4},{16,24},{20,28},{24,16},{28,20},{1,9},{5... | collective-permute-start | bytes 1572872 | tf_op jit(solution)/shard_map/ppermute | solution.py:86
  71.7 23.4 %collective-permute-start = (bf16[2,2,256,256]{3,2,1,0:T(8,128)(2,1)}, bf16[2,2,256,256]{3,2,1,0:T(8,128)(2,1)S(1)}, u32[]{:S(2)}, u32[]{:S(2)}) collective-permute-start(bf16[2,2,256,256]{3,2,1,0:T(8,128)(2,1)} %get-tuple-element.68.refs_2_.refs_4_), channel_id=1, source_target_pairs={{0,4},{4,0},{8,12},{12,8},{16,20},{20,16},{24,28},{28,24},{1,5},{5... | collective-permute-start | bytes 1572872 | tf_op jit(solution)/shard_map/ppermute | solution.py:86
  109.7 99.8 %all-gather.9.cloned.1.call-start = ((), (), s32[]{:S(2)}) async-start(), calls=%async_computation.7 | async-start | bytes 2621440 | tf_op jit(solution)/shard_map/all_gather | solution.py:103
  164.1 116.0 %reduce-scatter.7.cloned.1.call-start = ((), (), s32[]{:S(2)}) async-start(), calls=%async_computation.8 | async-start | bytes 2621440 | tf_op jit(solution)/shard_map/reduce_scatter | solution.py:108
  237.3 138.4 %all-gather.11.cloned.1.call-start = ((), (), s32[]{:S(2)}) async-start(), calls=%async_computation.10 | async-start | bytes 2621440 | tf_op jit(solution)/shard_map/all_gather | solution.py:103
  251.2 53.8 %collective-permute-start.13 = (bf16[3,256,1536]{2,1,0:T(8,128)(2,1)}, bf16[3,256,1536]{2,1,0:T(8,128)(2,1)}, u32[]{:S(2)}, u32[]{:S(2)}) collective-permute-start(bf16[3,256,1536]{2,1,0:T(8,128)(2,1)} %get-tuple-element.80), channel_id=1, source_target_pairs={{0,16},{4,20},{8,24},{12,28},{16,0},{20,4},{24,8},{28,12},{1,17},{... | collective-permute-start | bytes 7077896 | tf_op jit(solution)/shard_map/ppermute | solution.py:86
  252.7 53.5 %collective-permute-start.12 = (bf16[3,256,1536]{2,1,0:T(8,128)(2,1)}, bf16[3,256,1536]{2,1,0:T(8,128)(2,1)}, u32[]{:S(2)}, u32[]{:S(2)}) collective-permute-start(bf16[3,256,1536]{2,1,0:T(8,128)(2,1)} %get-tuple-element.77.refs_11_), channel_id=1, source_target_pairs={{0,8},{4,12},{8,0},{12,4},{16,24},{20,28},{24,16},{28,20},{1,9},{5... | collective-permute-start | bytes 7077896 | tf_op jit(solution)/shard_map/ppermute | solution.py:86
  309.9 105.0 %reduce-scatter.9.cloned.1.call-start = ((), (), s32[]{:S(2)}) async-start(), calls=%async_computation.9 | async-start | bytes 2621440 | tf_op jit(solution)/shard_map/reduce_scatter | solution.py:108
  314.2 27.3 %collective-permute-start.15 = (bf16[3,128,1536]{2,1,0:T(8,128)(2,1)}, bf16[3,128,1536]{2,1,0:T(8,128)(2,1)S(1)}, u32[]{:S(2)}, u32[]{:S(2)}) collective-permute-start(bf16[3,128,1536]{2,1,0:T(8,128)(2,1)} %get-tuple-element.86), channel_id=1, source_target_pairs={{0,8},{4,12},{8,0},{12,4},{16,24},{20,28},{24,16},{28,20},{1,9},{5... | collective-permute-start | bytes 3538952 | tf_op jit(solution)/shard_map/ppermute | solution.py:86
  315.6 27.0 %collective-permute-start.14 = (bf16[3,128,1536]{2,1,0:T(8,128)(2,1)}, bf16[3,128,1536]{2,1,0:T(8,128)(2,1)S(1)}, u32[]{:S(2)}, u32[]{:S(2)}) collective-permute-start(bf16[3,128,1536]{2,1,0:T(8,128)(2,1)} %get-tuple-element.82.refs_2_), channel_id=1, source_target_pairs={{0,16},{4,20},{8,24},{12,28},{16,0},{20,4},{24,8},{28,12},{1,17},{... | collective-permute-start | bytes 3538952 | tf_op jit(solution)/shard_map/ppermute | solution.py:86
  347.1 26.4 %collective-permute-start.20 = (bf16[3,128,1536]{2,1,0:T(8,128)(2,1)}, bf16[3,128,1536]{2,1,0:T(8,128)(2,1)}, u32[]{:S(2)}, u32[]{:S(2)}) collective-permute-start(bf16[3,128,1536]{2,1,0:T(8,128)(2,1)} %get-tuple-element.88.refs_5_.refs_6_.refs_3_), channel_id=1, source_target_pairs={{0,8},{4,12},{8,0},{12,4},{16,24},{20,28},{24,16},{28,20},{1,9},{5... | collective-permute-start | bytes 3538952 | tf_op jit(solution)/shard_map/ppermute | solution.py:86
  347.7 26.0 %collective-permute-start.18 = (bf16[3,128,1536]{2,1,0:T(8,128)(2,1)}, bf16[3,128,1536]{2,1,0:T(8,128)(2,1)}, u32[]{:S(2)}, u32[]{:S(2)}) collective-permute-start(bf16[3,128,1536]{2,1,0:T(8,128)(2,1)} %get-tuple-element.87.refs_18_.refs_1_.refs_2_), channel_id=1, source_target_pairs={{0,16},{4,20},{8,24},{12,28},{16,0},{20,4},{24,8},{28,12},{1,17},{... | collective-permute-start | bytes 3538952 | tf_op jit(solution)/shard_map/ppermute | solution.py:86
  348.3 154.5 %reduce-scatter.11.cloned.1.call-start = ((), (), s32[]{:S(2)}) async-start(), calls=%async_computation.11 | async-start | bytes 2621440 | tf_op jit(solution)/shard_map/reduce_scatter | solution.py:108
  348.5 26.0 %collective-permute-start.17 = (bf16[3,128,1536]{2,1,0:T(8,128)(2,1)}, bf16[3,128,1536]{2,1,0:T(8,128)(2,1)S(1)}, u32[]{:S(2)}, u32[]{:S(2)}) collective-permute-start(bf16[3,128,1536]{2,1,0:T(8,128)(2,1)} %get-tuple-element.88.refs_5_.refs_6_.refs_3_), channel_id=1, source_target_pairs={{0,4},{4,0},{8,12},{12,8},{16,20},{20,16},{24,28},{28,24},{1,5},{5... | collective-permute-start | bytes 3538952 | tf_op jit(solution)/shard_map/ppermute | solution.py:86
  348.6 27.2 %collective-permute-start.16 = (bf16[3,128,1536]{2,1,0:T(8,128)(2,1)S(1)}, bf16[3,128,1536]{2,1,0:T(8,128)(2,1)}, u32[]{:S(2)}, u32[]{:S(2)}) collective-permute-start(bf16[3,128,1536]{2,1,0:T(8,128)(2,1)S(1)} %copy-done.8), channel_id=1, source_target_pairs={{0,4},{4,0},{8,12},{12,8},{16,20},{20,16},{24,28},{28,24},{1,5},{5... | collective-permute-start | bytes 3538952 | tf_op jit(solution)/shard_map/ppermute | solution.py:86
  373.9 28.5 %collective-permute-start.29 = (bf16[3,128,1536]{2,1,0:T(8,128)(2,1)}, bf16[3,128,1536]{2,1,0:T(8,128)(2,1)}, u32[]{:S(2)}, u32[]{:S(2)}) collective-permute-start(bf16[3,128,1536]{2,1,0:T(8,128)(2,1)} %get-tuple-element.88.refs_5_.refs_6_.refs_3_), channel_id=1, source_target_pairs={{0,16},{4,20},{8,24},{12,28},{16,0},{20,4},{24,8},{28,12},{1,17},{... | collective-permute-start | bytes 3538952 | tf_op jit(solution)/shard_map/ppermute | solution.py:86
  374.5 28.0 %collective-permute-start.27 = (bf16[3,128,1536]{2,1,0:T(8,128)(2,1)S(1)}, bf16[3,128,1536]{2,1,0:T(8,128)(2,1)}, u32[]{:S(2)}, u32[]{:S(2)}) collective-permute-start(bf16[3,128,1536]{2,1,0:T(8,128)(2,1)S(1)} %copy-done.8), channel_id=1, source_target_pairs={{0,8},{4,12},{8,0},{12,4},{16,24},{20,28},{24,16},{28,20},{1,9},{5... | collective-permute-start | bytes 3538952 | tf_op jit(solution)/shard_map/ppermute | solution.py:86
  406.4 20.9 %collective-permute-start.26 = (bf16[2,2,256,256]{3,2,1,0:T(8,128)(2,1)}, bf16[2,2,256,256]{3,2,1,0:T(8,128)(2,1)}, u32[]{:S(2)}, u32[]{:S(2)}) collective-permute-start(bf16[2,2,256,256]{3,2,1,0:T(8,128)(2,1)} %get-tuple-element.125), channel_id=1, source_target_pairs={{0,24},{4,28},{8,16},{12,20},{16,8},{20,12},{24,0},{28,4},{1,25},{... | collective-permute-start | bytes 1572872 | tf_op jit(solution)/shard_map/ppermute | solution.py:86
  414.2 23.8 %collective-permute-start.25 = (bf16[2,2,256,256]{3,2,1,0:T(8,128)(2,1)}, bf16[2,2,256,256]{3,2,1,0:T(8,128)(2,1)}, u32[]{:S(2)}, u32[]{:S(2)}) collective-permute-start(bf16[2,2,256,256]{3,2,1,0:T(8,128)(2,1)} %get-tuple-element.126), channel_id=1, source_target_pairs={{0,16},{4,20},{8,24},{12,28},{16,0},{20,4},{24,8},{28,12},{1,17},{... | collective-permute-start | bytes 1572872 | tf_op jit(solution)/shard_map/ppermute | solution.py:86
  414.2 23.8 %collective-permute-start.23 = (bf16[2,2,256,256]{3,2,1,0:T(8,128)(2,1)}, bf16[2,2,256,256]{3,2,1,0:T(8,128)(2,1)}, u32[]{:S(2)}, u32[]{:S(2)}) collective-permute-start(bf16[2,2,256,256]{3,2,1,0:T(8,128)(2,1)} %get-tuple-element.130), channel_id=1, source_target_pairs={{0,8},{4,12},{8,0},{12,4},{16,24},{20,28},{24,16},{28,20},{1,9},{5... | collective-permute-start | bytes 1572872 | tf_op jit(solution)/shard_map/ppermute | solution.py:86
  451.9 29.0 %collective-permute-start.36 = (bf16[3,128,1536]{2,1,0:T(8,128)(2,1)}, bf16[3,128,1536]{2,1,0:T(8,128)(2,1)S(1)}, u32[]{:S(2)}, u32[]{:S(2)}) collective-permute-start(bf16[3,128,1536]{2,1,0:T(8,128)(2,1)} %get-tuple-element.110), channel_id=1, source_target_pairs={{0,16},{4,20},{8,24},{12,28},{16,0},{20,4},{24,8},{28,12},{1,17},{... | collective-permute-start | bytes 3538952 | tf_op jit(solution)/shard_map/ppermute | solution.py:86
  452.5 29.2 %collective-permute-start.35 = (bf16[3,128,1536]{2,1,0:T(8,128)(2,1)}, bf16[3,128,1536]{2,1,0:T(8,128)(2,1)}, u32[]{:S(2)}, u32[]{:S(2)}) collective-permute-start(bf16[3,128,1536]{2,1,0:T(8,128)(2,1)} %get-tuple-element.98.refs_9_), channel_id=1, source_target_pairs={{0,8},{4,12},{8,0},{12,4},{16,24},{20,28},{24,16},{28,20},{1,9},{5... | collective-permute-start | bytes 3538952 | tf_op jit(solution)/shard_map/ppermute | solution.py:86
  466.7 30.5 %collective-permute-start.34 = (bf16[1,256,1536]{2,1,0:T(8,128)(2,1)}, bf16[1,256,1536]{2,1,0:T(8,128)(2,1)S(1)}, u32[]{:S(2)}, u32[]{:S(2)}) collective-permute-start(bf16[1,256,1536]{2,1,0:T(8,128)(2,1)} %get-tuple-element.102), channel_id=1, source_target_pairs={{0,16},{4,20},{8,24},{12,28},{16,0},{20,4},{24,8},{28,12},{1,17},{... | collective-permute-start | bytes 2359304 | tf_op jit(solution)/shard_map/ppermute | solution.py:86
  468.2 29.1 %collective-permute-start.33 = (bf16[1,256,1536]{2,1,0:T(8,128)(2,1)}, bf16[1,256,1536]{2,1,0:T(8,128)(2,1)S(1)}, u32[]{:S(2)}, u32[]{:S(2)}) collective-permute-start(bf16[1,256,1536]{2,1,0:T(8,128)(2,1)} %get-tuple-element.100.refs_17_), channel_id=1, source_target_pairs={{0,8},{4,12},{8,0},{12,4},{16,24},{20,28},{24,16},{28,20},{1,9},{5... | collective-permute-start | bytes 2359304 | tf_op jit(solution)/shard_map/ppermute | solution.py:86
  480.9 25.0 %collective-permute-start.38 = (bf16[3,128,1536]{2,1,0:T(8,128)(2,1)S(1)}, bf16[3,128,1536]{2,1,0:T(8,128)(2,1)}, u32[]{:S(2)}, u32[]{:S(2)}) collective-permute-start(bf16[3,128,1536]{2,1,0:T(8,128)(2,1)S(1)} %collective-permute-done.36.refs_7_.refs_8_.refs_4_), channel_id=1, source_target_pairs={{0,4},{4,0},{8,12},{12,8},{16,20},{20,16},{24,28},{28,24},{1,5},{5... | collective-permute-start | bytes 3538952 | tf_op jit(solution)/shard_map/ppermute | solution.py:86
  481.7 24.3 %collective-permute-start.37 = (bf16[3,128,1536]{2,1,0:T(8,128)(2,1)}, bf16[3,128,1536]{2,1,0:T(8,128)(2,1)}, u32[]{:S(2)}, u32[]{:S(2)}) collective-permute-start(bf16[3,128,1536]{2,1,0:T(8,128)(2,1)} %collective-permute-done.35.refs_3_.refs_4_.refs_2_), channel_id=1, source_target_pairs={{0,4},{4,0},{8,12},{12,8},{16,20},{20,16},{24,28},{28,24},{1,5},{5... | collective-permute-start | bytes 3538952 | tf_op jit(solution)/shard_map/ppermute | solution.py:86
  529.7 23.8 %collective-permute-start.48 = (bf16[1,256,1536]{2,1,0:T(8,128)(2,1)S(1)}, bf16[1,256,1536]{2,1,0:T(8,128)(2,1)S(1)}, u32[]{:S(2)}, u32[]{:S(2)}) collective-permute-start(bf16[1,256,1536]{2,1,0:T(8,128)(2,1)S(1)} %maximum_select_fusion.refs_1_), channel_id=1, source_target_pairs={{0,8},{4,12},{8,0},{12,4},{16,24},{20,28},{24,16},{28,20},{1,9},{5... | collective-permute-start | bytes 2359304 | tf_op jit(solution)/shard_map/ppermute | solution.py:86
  531.5 22.1 %collective-permute-start.50 = (bf16[1,256,1536]{2,1,0:T(8,128)(2,1)S(1)}, bf16[1,256,1536]{2,1,0:T(8,128)(2,1)S(1)}, u32[]{:S(2)}, u32[]{:S(2)}) collective-permute-start(bf16[1,256,1536]{2,1,0:T(8,128)(2,1)S(1)} %maximum_select_fusion.1.refs_3_), channel_id=1, source_target_pairs={{0,16},{4,20},{8,24},{12,28},{16,0},{20,4},{24,8},{28,12},{1,17},{... | collective-permute-start | bytes 2359304 | tf_op jit(solution)/shard_map/ppermute | solution.py:86
  (67 other events, 556.8 us)
Sparse Core Ops, SparseCore 0:
  10.2 48.6 all-gather.4
  60.4 44.6 all-gather.6
  109.8 51.5 reduce-scatter.4
  164.3 45.2 all-gather.8
  237.5 42.6 reduce-scatter.6
  310.0 43.3 all-gather.10
  356.3 42.5 reduce-scatter.8
  448.1 41.6 reduce-scatter.10
